TPU v7x, 32 devices: a whole 2x2x4 slice. The times are simulated.
32 devices in a mesh: ctx: 8 (over z, x), head: 4 (over y, core).
Axes of the slice: x: 2, y: 2, z: 4, core: 2. Of those that a mesh axis runs over, the one named last changes fastest.
Arguments:
- queries: bfloat16 [512, 5120], P(None, 'head'), may hold values from -18 to 18
- keys: bfloat16 [4096, 1024], P('ctx', 'head'), may hold values from -20 to 20
- values: bfloat16 [4096, 1024], P('ctx', 'head'), may hold values from -6 to 6
- stretch_lengths: int32 [32], replicated, may hold values from 1 to 512, 4096 in all
- query_pos: int32 [512], replicated, may hold values from 0 to 511, each once
Outputs:
- attended: bfloat16 [512, 5120], P('ctx', 'head')
- stretch_mass: float32 [32, 512], replicated
Inputs may be any that keep to these rules, and one draw needn't show every extreme that they name: `stretch_lengths`: stretch lengths sum to 4096; the longest is exactly 512. `query_pos`: each of 0 to 511 appears once.
All inputs are finite; a program needn't handle non-finite values.
Results may differ from a plain program's by a relative error of at most 0.0076.
Values sent between devices are 32-bit elements; how exact they have to be, the bound alone decides.
No kernel may reach another device: no remote copies, remote signals or barrier semaphores. Data moves between devices by JAX's collectives and lax.ppermute only.
A program may use at most 64 MiB of HBM per device.

v0:
```python
import jax
import jax.numpy as jnp
from jax import lax
from jax.sharding import PartitionSpec as P

HD = 128


ROPE_BASE = 1000000.0


def rope_queries(queries, query_pos):
    query_count = queries.shape[0]
    head_count = queries.shape[1] // HD
    half_dim = HD // 2
    frequency = ROPE_BASE ** (-(jnp.arange(half_dim, dtype=jnp.float32) * 2.0 / HD))
    angles = query_pos.astype(jnp.float32)[:, None] * frequency[None, :]
    cosine = jnp.cos(angles)[:, None, :]
    sin_part = jnp.sin(angles)[:, None, :]
    as_float = queries.astype(jnp.float32).reshape(query_count, head_count, HD)
    front_half = as_float[..., :half_dim]
    back_half = as_float[..., half_dim:]
    rotated = jnp.concatenate(
        [front_half * cosine - back_half * sin_part, back_half * cosine + front_half * sin_part],
        axis=-1,
    )
    return rotated.astype(jnp.bfloat16)


def local(queries, keys, values, stretch_lengths, query_pos):
    roped = rope_queries(queries, query_pos)
    query_count = roped.shape[0]
    heads_here = roped.shape[1]
    kv_here = keys.shape[1] // HD
    group_size = heads_here // kv_here
    tok_here = keys.shape[0]
    stretch_count = stretch_lengths.shape[0]
    block_rows = min(64, query_count)
    block_count = query_count // block_rows
    q_blocks = roped.reshape(block_count, block_rows, kv_here, group_size, HD)
    key_rows = keys.reshape(tok_here, kv_here, HD)
    value_rows = values.reshape(tok_here, kv_here, HD)
    starts = jnp.cumsum(stretch_lengths) - stretch_lengths
    stretch_ends = starts + stretch_lengths
    key_position = lax.axis_index("ctx") * tok_here + jnp.arange(tok_here, dtype=jnp.int32)
    onehot = (
        (key_position[:, None] >= starts[None, :]) & (key_position[:, None] < stretch_ends[None, :])
    ).astype(jnp.bfloat16)
    score_scale = HD ** (-0.5)

    def score_block(q_block):
        return (
            jnp.einsum("qgjd,kgd->gjqk", q_block, key_rows, preferred_element_type=jnp.float32)
            * score_scale
        )

    def weigh(logits, row_top):
        weights = jnp.exp(logits - row_top[..., None])
        row_sum = jnp.sum(weights, axis=-1)
        rounded = weights.astype(jnp.bfloat16)
        weighted = jnp.einsum(
            "gjqk,kgd->gjqd", rounded, value_rows, preferred_element_type=jnp.float32
        )
        return (row_sum, weighted)

    local_top = lax.map(lambda q_block: score_block(q_block).max(-1), q_blocks)
    row_top = lax.pmax(local_top, "ctx")
    row_sum, weighted = lax.map(
        lambda pieces: weigh(score_block(pieces[0]), pieces[1]), (q_blocks, row_top)
    )
    whole_sum = lax.psum(row_sum, "ctx")
    inverse = 1.0 / whole_sum

    def mass_block(pieces):
        q_block, top_block, inverse_block = pieces
        logits = score_block(q_block)
        rounded = jnp.exp(logits - top_block[..., None]).astype(jnp.bfloat16)
        share = jnp.sum(rounded.astype(jnp.float32) * inverse_block[..., None], axis=(0, 1))
        high_part = share.astype(jnp.bfloat16)
        low_part = (share - high_part.astype(jnp.float32)).astype(jnp.bfloat16)
        return jnp.einsum(
            "qk,kc->cq", high_part, onehot, preferred_element_type=jnp.float32
        ) + jnp.einsum("qk,kc->cq", low_part, onehot, preferred_element_type=jnp.float32)

    block_mass = lax.map(mass_block, (q_blocks, row_top, inverse))
    mass_factor = stretch_count / (heads_here * lax.axis_size("head"))
    mass_term = block_mass.transpose(1, 0, 2).reshape(stretch_count, query_count) * mass_factor
    stretch_mass = lax.psum(mass_term, ("ctx", "head"))
    scaled = weighted.transpose(0, 3, 1, 2, 4).reshape(query_count, heads_here * HD)
    inverse_rows = inverse.transpose(0, 3, 1, 2).reshape(query_count, heads_here)
    rows_here = query_count // lax.axis_size("ctx")
    inverse_here = lax.dynamic_slice_in_dim(
        inverse_rows, lax.axis_index("ctx") * rows_here, rows_here, 0
    )
    whole_out = lax.psum(scaled, "ctx")
    summed = lax.dynamic_slice_in_dim(whole_out, lax.axis_index("ctx") * rows_here, rows_here, 0)
    normalized = summed.reshape(rows_here, heads_here, HD) * inverse_here[..., None]
    attended = normalized.reshape(rows_here, heads_here * HD).astype(jnp.bfloat16)
    return (attended, stretch_mass)


def solution(mesh):
    placed = (P(None, "head"), P("ctx", "head"), P("ctx", "head"), P(), P())
    return jax.shard_map(
        local, mesh=mesh, in_specs=placed, out_specs=(P("ctx", "head"), P()), check_vma=False
    )
```

profile of v0, /device:TPU:0, one launch (start us, length us, event | category | flops | bytes accessed | tf_op | source)
XLA Modules:
  0.0 347.0 jit_solution(11300220203523453421)
XLA Ops:
  8.0 1.1 copy.11
  9.3 1.1 copy.14
  12.6 1.8 concatenate.9
  14.4 1.7 concatenate.10
  16.1 2.2 pad_maximum_fusion
  18.3 3.3 copy.15
  21.7 10.9 %while.33 = (s32[]{:T(128)}, f32[8,2,5,64]{3,2,1,0:T(8,128)S(1)}, bf16[8,64,2,5,128]{4,1,3,2,0:T(8,128)(2,1)}, bf16[512,2,128]{2,0,1:T(8,128)(2,1)S(1)}, s32[]{:T(128)}) while((s32[]{:T(128)}, f32[8,2,5,64]{3,2,1,0:T(8,128)S(1)}, bf16[8,64,2,5,128]{4,1,3,2,0:T(8,128)(2,1)}, bf16[512,2,128]{2,0,1:T(8,128)(2,1)S(1)}, s32[]{:T(128)}) %tuple.64), condition=%wide.region_2.3_spmd, body=%wide.region_0.2_spmd.sunk | while | flops 84540800 | bytes 445005 | solution.py:66
  21.7 1.3 fusion.58
  23.0 1.3 fusion.58
  24.4 1.3 fusion.58
  25.7 1.3 fusion.58
  27.1 1.3 fusion.58
  28.5 1.3 fusion.58
  29.8 1.3 fusion.58
  31.2 1.3 fusion.58
  32.5 39.3 %pmax.7 = f32[8,2,5,64]{3,2,1,0:T(8,128)S(1)} all-reduce(f32[8,2,5,64]{3,2,1,0:T(8,128)S(1)} %get-tuple-element.99), channel_id=1, replica_groups=mesh['ctx'=8,'head'=4] {'ctx'}, use_global_device_ids=true, to_apply=%region_3.4 | all-reduce | flops 5120 | bytes 40960 | tf_op jit(solution)/shard_map/pmax | solution.py:67
  71.8 19.9 %while.34 = (s32[]{:T(128)}, f32[8,2,5,64]{3,2,1,0:T(8,128)S(1)}, f32[8,2,5,64,128]{4,3,2,1,0:T(8,128)}, bf16[8,64,2,5,128]{4,1,3,2,0:T(8,128)(2,1)}, bf16[512,2...) while((s32[]{:T(128)}, f32[8,2,5,64]{3,2,1,0:T(8,128)S(1)}, ...), condition=%wide.region_6.7_spmd, body=%wide.region_4.6_spmd.sunk | while | flops 169082240 | bytes 2353261 | solution.py:68
  71.8 1.4 fusion.61
  73.3 1.1 fusion.62
  74.3 1.4 fusion.61
  75.7 1.1 fusion.62
  76.8 1.4 fusion.61
  78.2 1.1 fusion.62
  79.3 1.4 fusion.61
  80.7 1.1 fusion.62
  81.8 1.4 fusion.61
  83.2 1.1 fusion.62
  84.3 1.4 fusion.61
  85.7 1.1 fusion.62
  86.8 1.4 fusion.61
  89.3 1.4 fusion.61
  90.7 1.1 fusion.62
  91.7 5.2 %copy.18 = f32[8,64,2,5,128]{4,3,2,1,0:T(8,128)} copy(f32[8,64,2,5,128]{4,1,3,2,0:T(8,128)} %bitcast.130) | data formatting | bytes 5242880 | tf_op jit(solution)/shard_map/transpose | solution.py:89
  97.0 4.7 %reshape.123 = f32[512,1280]{1,0:T(8,128)} reshape(f32[8,64,2,5,128]{4,3,2,1,0:T(8,128)} %copy.18) | data formatting | bytes 5242880 | tf_op jit(solution)/shard_map/reshape | solution.py:89
  102.6 36.0 %psum.22 = f32[8,2,5,64]{3,2,1,0:T(8,128)S(1)} all-reduce(f32[8,2,5,64]{3,2,1,0:T(8,128)S(1)} %get-tuple-element.101), channel_id=1, replica_groups=mesh['ctx'=8,'head'=4] {'ctx'}, use_global_device_ids=true, to_apply=%region_8.9 | all-reduce | flops 5120 | bytes 40960 | tf_op jit(solution)/shard_map/psum | solution.py:71
  138.6 15.8 %while.35 = (s32[]{:T(128)}, f32[8,32,64]{2,1,0:T(8,128)S(1)}, bf16[8,64,2,5,128]{4,1,3,2,0:T(8,128)(2,1)}, bf16[512,2,128]{2,0,1:T(8,128)(2,1)S(1)}, f32[8,2,5,...) while((s32[]{:T(128)}, f32[8,32,64]{2,1,0:T(8,128)S(1)}, ...), condition=%wide.region_12.13_spmd.clone, body=%wide.region_10.12_spmd.clone.sunk | while | flops 90310656 | bytes 881017 | solution.py:85
  138.7 1.4 fusion.66
  140.6 1.4 fusion.66
  142.6 1.4 fusion.66
  144.6 1.4 fusion.66
  146.6 1.4 fusion.66
  148.5 1.4 fusion.66
  150.5 1.4 fusion.66
  152.5 1.4 fusion.66
  155.6 60.4 %all-reduce.3.cloned.1.call-done = f32[512,1280]{1,0:T(8,128)} async-done(((f32[512,1280]{1,0:T(8,128)}), f32[512,1280]{1,0:T(8,128)}) %all-reduce.3.cloned.1.call-update) | async-done | bytes 2621456 | tf_op jit(solution)/shard_map/psum | solution.py:95
  216.2 1.8 fusion.39
  217.9 120.8 %all-reduce.5.cloned.1.call-done = f32[32,512]{1,0:T(8,128)} async-done(((f32[32,512]{1,0:T(8,128)}), f32[32,512]{1,0:T(8,128)}) %all-reduce.5.cloned.1.call-update) | async-done | bytes 65552 | tf_op jit(solution)/shard_map/psum | solution.py:88
  338.7 1.5 copy.58
  (83 shorter events, 11.2 us)
Async XLA Ops:
  7.2 3.4 copy-start
  7.2 208.8 %all-reduce.3.cloned.1.call-start = ((), (), s32[]{:S(2)}) async-start(), calls=%async_computation | async-start | bytes 5242880 | tf_op jit(solution)/shard_map/psum | solution.py:95
  101.7 0.7 copy-start.1
  101.7 237.0 %all-reduce.5.cloned.1.call-start = ((), (), s32[]{:S(2)}) async-start(), calls=%async_computation.1 | async-start | bytes 131072 | tf_op jit(solution)/shard_map/psum | solution.py:88
Sparse Core Ops, SparseCore 0:
  101.8 114.1 all-reduce.2
  222.1 116.5 all-reduce.4
where the time goes:
time: 349 us; the launch traced here: 347 us
  waiting for transfers between devices  181 us (52%)
  blocking collectives  75.3 us (22%)
  matrix products  46 us (13%)
  local copies, waits for them, and re-layouts  23.5 us (7%)
  between operations  14.2 us (4%)
  other arithmetic  6.34 us (2%)
    psum x1, waiting for transfers between devices, local(): stretch_mass = lax.psum(mass_term, ('ctx', 'head'))  121 us
    psum x1, waiting for transfers between devices, local(): whole_out = lax.psum(scaled, 'ctx')  60.4 us
    pmax x1, blocking collectives, local(): row_top = lax.pmax(local_top, 'ctx')  39.3 us
    psum x1, blocking collectives, local(): whole_sum = lax.psum(row_sum, 'ctx')  36 us
    dot_general x24, matrix products, score_block(): jnp.einsum('qgjd,kgd->gjqk', q_block, key_rows, preferred_element_type=jn...  32.8 us
    dot_general x8, matrix products, weigh(): jnp.einsum('gjqk,kgd->gjqd', rounded, value_rows, preferred_element_type=...  8.57 us
  transfers between devices with their start and end apart: 2, of which 2 were waited for; matrix products, arithmetic and copies ran while one was open for 5% of the time, Pallas kernels for 0%

commit v1 on v0

v1 whole, which is shorter than its diff:
```python
import functools
import math

import jax
import jax.numpy as jnp
from jax import lax
from jax.experimental import pallas as pl
from jax.experimental.pallas import tpu as pltpu
from jax.sharding import PartitionSpec as P

HD = 128
ROPE_BASE = 1000000.0
LOG2_SCALE = HD ** (-0.5) * math.log2(math.e)
VMEM_LIMIT = 40 * 1024 * 1024
STAT_ROWS = 16

CHUNKS = ((3, 0), (2, 1), (3, 0), (2, 0))
TIES = {}


def position(rel, order):
    place = 0
    for bit in order:
        place = place * 2 + ((rel // bit) & 1)
    return place


def blocks_in_order(order):
    return sorted(range(2 ** len(order)), key=lambda rel: position(rel, order))


def flash_kernel(
    order, first_head, group_size,
    where_ref, q_ref, k_ref, v_ref, cos_ref, sin_ref, lens_ref,
    keep_ref, send_ref, stats_ref, mass_ref, values_t, whole,
):
    step = pl.program_id(0)
    head = first_head + step
    tok_here = k_ref.shape[0]
    stretch_count = lens_ref.shape[1]
    me = where_ref[0]

    @pl.when(step == 0)
    def _():
        stats_ref[...] = jnp.zeros_like(stats_ref)
        lens = lens_ref[...].astype(jnp.float32)
        row = lax.broadcasted_iota(jnp.int32, (stretch_count, stretch_count), 0)
        column = lax.broadcasted_iota(jnp.int32, (stretch_count, stretch_count), 1)
        ends = jnp.sum(jnp.where(column <= row, lens, 0.0), axis=1, keepdims=True)
        starts = jnp.sum(jnp.where(column < row, lens, 0.0), axis=1, keepdims=True)
        at = lax.broadcasted_iota(jnp.int32, (stretch_count, tok_here), 1) + me * tok_here
        at = at.astype(jnp.float32)
        inside = (at >= starts) & (at < ends)
        values_t[HD:, :] = jnp.where(inside, 1.0, 0.0).astype(jnp.bfloat16)

    @pl.when((step == 0) | (lax.rem(head, group_size) == 0))
    def _():
        values_t[:HD, :] = v_ref[...].T

    q = q_ref[...].astype(jnp.float32)
    turned = pltpu.roll(q, HD // 2, axis=1)
    roped = (q * cos_ref[...] + turned * sin_ref[...]).astype(jnp.bfloat16)
    raw = lax.dot_general(
        k_ref[...], roped, (((1,), (1,)), ((), ())), preferred_element_type=jnp.float32
    )
    top = jnp.max(raw, axis=0, keepdims=True)
    weights = jnp.exp2((raw - top) * LOG2_SCALE)
    row_sum = jnp.sum(weights, axis=0, keepdims=True)
    stats_ref[pl.ds(step, 1), :] = top * LOG2_SCALE
    stats_ref[pl.ds(STAT_ROWS + step, 1), :] = row_sum
    out_t = jnp.dot(values_t[...], weights.astype(jnp.bfloat16), preferred_element_type=jnp.float32)
    mass_ref[...] = out_t[HD:]
    whole[...] = out_t[:HD].T
    blocks = blocks_in_order(order)
    rows = whole.shape[0] // len(blocks)
    half = len(blocks) // 2
    for place, rel in enumerate(blocks):
        source = pl.multiple_of((me ^ rel) * rows, rows)
        target = keep_ref if place < half else send_ref
        target[(place % half) * rows : (place % half + 1) * rows, :] = whole[pl.ds(source, rows), :]


def flash(order, first_head, head_count, group_size, where, queries, keys, values, cosine, sine, lens):
    query_count = queries.shape[0]
    tok_here = keys.shape[0]
    stretch_count = lens.shape[1]
    half = query_count // 2
    work = head_count * query_count * tok_here
    vmem = pl.BlockSpec(memory_space=pltpu.VMEM)
    kv_spec = pl.BlockSpec((tok_here, HD), lambda j: (0, (first_head + j) // group_size))
    return pl.pallas_call(
        functools.partial(flash_kernel, order, first_head, group_size),
        grid=(head_count,),
        in_specs=[
            pl.BlockSpec(memory_space=pltpu.SMEM),
            pl.BlockSpec((query_count, HD), lambda j: (0, first_head + j)),
            kv_spec,
            kv_spec,
            vmem,
            vmem,
            vmem,
        ],
        out_specs=[
            pl.BlockSpec((half, HD), lambda j: (0, j)),
            pl.BlockSpec((half, HD), lambda j: (0, j)),
            pl.BlockSpec((2 * STAT_ROWS, query_count), lambda j: (0, 0)),
            pl.BlockSpec((stretch_count, query_count), lambda j: (j, 0)),
        ],
        out_shape=[
            jax.ShapeDtypeStruct((half, head_count * HD), jnp.float32),
            jax.ShapeDtypeStruct((half, head_count * HD), jnp.float32),
            jax.ShapeDtypeStruct((2 * STAT_ROWS, query_count), jnp.float32),
            jax.ShapeDtypeStruct((head_count * stretch_count, query_count), jnp.float32),
        ],
        scratch_shapes=[
            pltpu.VMEM((HD + stretch_count, tok_here), jnp.bfloat16),
            pltpu.VMEM((query_count, HD), jnp.float32),
        ],
        compiler_params=pltpu.CompilerParams(vmem_limit_bytes=VMEM_LIMIT),
        cost_estimate=pl.CostEstimate(
            flops=work * 4 * HD, bytes_accessed=work, transcendentals=work
        ),
    )(where, queries, keys, values, cosine, sine, lens)


def weigh_kernel(orders, head_counts, factor, where_ref, own_ref, whole_ref, *refs):
    order_count = len(orders)
    tops_refs = refs[:order_count]
    mass_refs = refs[order_count : order_count + len(head_counts)]
    out_ref = refs[order_count + len(head_counts)]
    weight_refs = refs[order_count + len(head_counts) + 1 : -1]
    columns = refs[-1]
    me = where_ref[0]
    top, inverse = whole_ref[:STAT_ROWS], 1.0 / whole_ref[STAT_ROWS:]
    mine = jnp.exp2(own_ref[:STAT_ROWS] - top) * inverse
    stretch_count = out_ref.shape[0]
    total, head = None, 0
    for count, mass_ref in zip(head_counts, mass_refs):
        for j in range(count):
            term = mass_ref[j * stretch_count : (j + 1) * stretch_count] * mine[head : head + 1]
            total = term if total is None else total + term
            head += 1
    out_ref[...] = total * factor
    theirs = [jnp.exp2(tops_ref[...] - top) * inverse for tops_ref in tops_refs]
    filled = (1 + order_count) * STAT_ROWS
    rest = jnp.zeros((HD - filled, top.shape[1]), jnp.float32)
    columns[...] = jnp.concatenate([mine] + theirs + [rest], axis=0).T
    for order, weight_ref in zip(orders, weight_refs):
        blocks = blocks_in_order(order)
        rows = columns.shape[0] // len(blocks)
        for place, rel in enumerate(blocks[: len(blocks) // 2]):
            source = pl.multiple_of((me ^ rel) * rows, rows)
            weight_ref[place * rows : (place + 1) * rows, :] = columns[pl.ds(source, rows), :]


def weigh(orders, head_counts, factor, where, own, whole, tops, masses):
    query_count = own.shape[1]
    stretch_count = masses[0].shape[0] // head_counts[0]
    vmem = pl.BlockSpec(memory_space=pltpu.VMEM)
    return pl.pallas_call(
        functools.partial(weigh_kernel, orders, head_counts, factor),
        in_specs=[pl.BlockSpec(memory_space=pltpu.SMEM)] + [vmem] * (2 + len(tops) + len(masses)),
        out_specs=[vmem] * (1 + len(orders)),
        out_shape=[jax.ShapeDtypeStruct((stretch_count, query_count), jnp.float32)]
        + [jax.ShapeDtypeStruct((query_count // 2, HD), jnp.float32)] * len(orders),
        scratch_shapes=[pltpu.VMEM((query_count, HD), jnp.float32)],
        compiler_params=pltpu.CompilerParams(vmem_limit_bytes=VMEM_LIMIT),
        cost_estimate=pl.CostEstimate(flops=1 << 20, bytes_accessed=1 << 20, transcendentals=1 << 14),
    )(where, own, whole, *tops, *masses)


def merge_kernel(first_head, other, keep_ref, got_ref, weight_ref, near_ref, far_ref):
    half = near_ref.shape[0]
    for j in range(keep_ref.shape[1] // HD):
        columns = slice(j * HD, (j + 1) * HD)
        head = first_head + j
        theirs = (1 + other) * STAT_ROWS + head
        for rows, target in ((slice(0, half), near_ref), (slice(half, 2 * half), far_ref)):
            target[:, columns] = (
                keep_ref[rows, columns] * weight_ref[rows, head : head + 1]
                + got_ref[rows, columns] * weight_ref[rows, theirs : theirs + 1]
            )


def merge(first_head, other, keep, got, weights):
    rows, columns = keep.shape
    vmem = pl.BlockSpec(memory_space=pltpu.VMEM)
    return pl.pallas_call(
        functools.partial(merge_kernel, first_head, other),
        in_specs=[vmem] * 3,
        out_specs=[vmem] * 2,
        out_shape=[jax.ShapeDtypeStruct((rows // 2, columns), jnp.float32)] * 2,
        compiler_params=pltpu.CompilerParams(vmem_limit_bytes=VMEM_LIMIT),
        cost_estimate=pl.CostEstimate(
            flops=3 * rows * columns, bytes_accessed=12 * rows * columns, transcendentals=0
        ),
    )(keep, got, weights)


def join_stats(one, two):
    top = jnp.maximum(one[:STAT_ROWS], two[:STAT_ROWS])
    total = one[STAT_ROWS:] * jnp.exp2(one[:STAT_ROWS] - top) + two[STAT_ROWS:] * jnp.exp2(
        two[:STAT_ROWS] - top
    )
    return jnp.concatenate([top, total], axis=0)


def local(queries, keys, values, stretch_lengths, query_pos):
    query_count = queries.shape[0]
    heads_here = queries.shape[1] // HD
    group_size = heads_here // (keys.shape[1] // HD)
    stretch_count = stretch_lengths.shape[0]
    ctx_size, head_size = lax.axis_size("ctx"), lax.axis_size("head")
    where = lax.axis_index("ctx").astype(jnp.int32).reshape(1)
    bits = tuple(2**i for i in range(ctx_size.bit_length() - 1))
    done = {}

    def swap(name, array, axis, bit):
        size = lax.axis_size(axis)
        waits = [done[other] for other in TIES.get(name, ()) if other in done]
        if waits:
            array = lax.optimization_barrier((array, *waits))[0]
        done[name] = lax.ppermute(array, axis, [(i, i ^ bit) for i in range(size)])
        return done[name]

    half_dim = HD // 2
    frequency = ROPE_BASE ** (-(jnp.arange(half_dim, dtype=jnp.float32) * 2.0 / HD))
    angles = query_pos.astype(jnp.float32)[:, None] * frequency[None, :]
    cosine, sine = jnp.cos(angles), jnp.sin(angles)
    cosine = jnp.concatenate([cosine, cosine], axis=1)
    sine = jnp.concatenate([-sine, sine], axis=1)
    lens = stretch_lengths.reshape(1, stretch_count)

    orders = {}
    chunks = []
    first_head = 0
    for head_count, turn in CHUNKS:
        order = bits[turn:] + bits[:turn]
        keep, send, stats, masses = flash(
            order, first_head, head_count, group_size, where, queries, keys, values, cosine, sine, lens
        )
        orders.setdefault(order, len(orders))
        name = "c%d" % len(chunks)
        got = swap("%s.%d" % (name, order[0]), send, "ctx", order[0])
        chunks.append((name, order, first_head, head_count, keep, got, stats, masses))
        first_head += head_count

    pad = jnp.zeros((STAT_ROWS - heads_here, query_count), jnp.float32)
    tops = [c[6][: c[3]] for c in chunks] + [pad]
    sums = [c[6][STAT_ROWS : STAT_ROWS + c[3]] for c in chunks] + [pad + 1.0]
    own = jnp.concatenate(tops + sums, axis=0)
    joined, partner_tops = own, {}
    firsts = [order[0] for order in orders]
    for bit in bits:
        message = joined
        if bit in firsts and bit != bits[0]:
            message = jnp.concatenate([joined, own[:STAT_ROWS]], axis=0)
        got = swap("a.%d" % bit, message, "ctx", bit)
        if bit in firsts:
            partner_tops[bit] = got[:STAT_ROWS] if bit == bits[0] else got[2 * STAT_ROWS :]
        joined = join_stats(joined, got[: 2 * STAT_ROWS])

    factor = stretch_count / (heads_here * head_size)
    mass, *weights = weigh(
        tuple(orders), tuple(c[3] for c in chunks), factor, where, own, joined,
        [partner_tops[bit] for bit in firsts], [c[7] for c in chunks],
    )

    for bit in (2**i for i in range(head_size.bit_length() - 1)):
        mass = mass + swap("mh.%d" % bit, mass, "head", bit)
    for bit in bits:
        mass = mass + swap("m.%d" % bit, mass, "ctx", bit)

    state = []
    for name, order, first_head, head_count, keep, got, _, _ in chunks:
        kind = orders[order]
        state.append(merge(first_head, kind, keep, got, weights[kind]))
    for i in range(1, len(bits)):
        for n, (name, order, *_) in enumerate(chunks):
            keep, send = state[n]
            keep = keep + swap("%s.%d" % (name, order[i]), send, "ctx", order[i])
            if i < len(bits) - 1:
                rows = keep.shape[0] // 2
                state[n] = (keep[:rows], keep[rows:])
            else:
                state[n] = keep
    attended = jnp.concatenate([part.astype(jnp.bfloat16) for part in state], axis=1)
    return attended, mass


def solution(mesh):
    placed = (P(None, "head"), P("ctx", "head"), P("ctx", "head"), P(), P())
    return jax.shard_map(
        local, mesh=mesh, in_specs=placed, out_specs=(P("ctx", "head"), P()), check_vma=False
    )
```

time: 349 us -> 85.3 us (0.24)
  waiting for transfers between devices: 181 us -> 37.5 us
  blocking collectives: 75.3 us -> 0 us
  matrix products: 46 us -> 0 us
  starting transfers between devices: 0.08 us -> 27.8 us
  local copies, waits for them, and re-layouts: 23.5 us -> 3.06 us
  between operations: 14.2 us -> 0.99 us
  Pallas kernels: 0 us -> 12.2 us
    psum x2 -> x0, waiting for transfers between devices: 181 us -> none  [the longest x1 121 us: local(): stretch_mass = lax.psum(mass_term, ('ctx', 'head'))]
    dot_general x48 -> x0, matrix products: 46 us -> none  [the longest x24 32.8 us: score_block(): jnp.einsum('qgjd,kgd->gjqk', q_block, key_rows, preferred_element_type=jn...]
    pmax x1 -> x0, blocking collectives: 39.3 us -> none  [local(): row_top = lax.pmax(local_top, 'ctx')]
    ppermute x0 -> x20, waiting for transfers between devices: none -> 37.5 us  [swap(): done[name] = lax.ppermute(array, axis, [(i, i ^ bit) for i in range(size)])]
    psum x1 -> x0, blocking collectives: 36 us -> none  [local(): whole_sum = lax.psum(row_sum, 'ctx')]
    ppermute x0 -> x20, starting transfers between devices: none -> 27.8 us  [swap(): done[name] = lax.ppermute(array, axis, [(i, i ^ bit) for i in range(size)])]
    pallas_call x0 -> x9, Pallas kernels: none -> 12.2 us  [the longest x4 11.1 us: flash(): pl.pallas_call(functools.partial(flash_kernel, order, first_head, group_s...]
    transpose x2 -> x0, local copies, waits for them, and re-layouts: 5.24 us -> none  [the longest x1 5.22 us: local(): weighted.transpose(0, 3, 1, 2, 4).reshape(query_count, heads_here * HD)]
  transfers between devices with their start and end apart: 2 -> 20, of which waited for: 2 -> 9; matrix products, arithmetic and copies ran while one was open for 5% -> 1% of each run, Pallas kernels for 0% -> 1%
where the time goes in v1:
time: 85.3 us; the launch traced here: 85.2 us
  waiting for transfers between devices  37.5 us (44%)
  starting transfers between devices  27.8 us (33%)
  Pallas kernels  12.2 us (14%)
  other arithmetic  3.59 us (4%)
  local copies, waits for them, and re-layouts  3.06 us (4%)
  between operations  0.99 us (1%)
    ppermute x20, waiting for transfers between devices, swap(): done[name] = lax.ppermute(array, axis, [(i, i ^ bit) for i in range(size)])  37.5 us
    ppermute x20, starting transfers between devices, swap(): done[name] = lax.ppermute(array, axis, [(i, i ^ bit) for i in range(size)])  27.8 us
    pallas_call x4, Pallas kernels, flash(): pl.pallas_call(functools.partial(flash_kernel, order, first_head, group_s...  11.1 us
    unnamed x24, local copies, waits for them, and re-layouts  2.78 us
  transfers between devices with their start and end apart: 20, of which 9 were waited for; matrix products, arithmetic and copies ran while one was open for 1% of the time, Pallas kernels for 1%

profile of v1, /device:TPU:0, one launch (start us, length us, event | category | flops | bytes accessed | tf_op | source)
XLA Modules:
  0.0 85.2 jit_solution(7414177681848807147)
XLA Ops:
  0.7 0.8 convert_element_type.15
  1.5 1.0 %fusion.2 = (f32[512,64]{1,0:T(8,128)S(1)}, f32[512,64]{1,0:T(8,128)S(1)}, f32[512,64]{1,0:T(8,128)S(1)}) fusion(f32[64]{0:T(128)S(1)} %negate_power_fusion, f32[512]{0:T(512)S(1)} %convert_element_type.15), kind=kLoop, calls=%fused_computation.9 | loop fusion | flops 65536 | bytes 395520 | tf_op jit(solution)/shard_map/neg | solution.py:231
  2.5 0.2 pad_maximum_fusion
  2.7 3.3 %shard_map.70 = (f32[256,384]{1,0:T(8,128)S(1)}, f32[256,384]{1,0:T(8,128)S(1)}, f32[32,512]{1,0:T(8,128)S(1)}, f32[96,512]{1,0:T(8,128)S(1)}) custom-call(s32[1]{0:T(128)} %bitcast.where_ref, bf16[512,1280]{1,0:T(8,128)(2,1)S(1)} %copy-done, bf16[512,256]{1,0:T(8,128)(2,1)S(1)} %copy-done.1, bf16[512,256]{1,0:T(8,128)(2,1)S(1)} %copy-done.2, ...), custom_call_target="tpu_custom_call" | custom-call | flops 402653184 | bytes 786432 | tf_op jit(solution)/shard_map/pallas_call | solution.py:91
  6.1 3.3 %shard_map.68 = (f32[256,384]{1,0:T(8,128)S(1)}, f32[256,384]{1,0:T(8,128)S(1)}, f32[32,512]{1,0:T(8,128)S(1)}, f32[96,512]{1,0:T(8,128)S(1)}) custom-call(s32[1]{0:T(128)} %bitcast.where_ref, bf16[512,1280]{1,0:T(8,128)(2,1)S(1)} %copy-done, bf16[512,256]{1,0:T(8,128)(2,1)S(1)} %copy-done.1, bf16[512,256]{1,0:T(8,128)(2,1)S(1)} %copy-done.2, ...), custom_call_target="tpu_custom_call" | custom-call | flops 402653184 | bytes 786432 | tf_op jit(solution)/shard_map/pallas_call | solution.py:91
  9.4 0.8 copy-done.9
  10.1 2.2 %shard_map.69 = (f32[256,256]{1,0:T(8,128)S(1)}, f32[256,256]{1,0:T(8,128)S(1)}, f32[32,512]{1,0:T(8,128)S(1)}, f32[64,512]{1,0:T(8,128)S(1)}) custom-call(s32[1]{0:T(128)} %bitcast.where_ref, bf16[512,1280]{1,0:T(8,128)(2,1)S(1)} %copy-done, bf16[512,256]{1,0:T(8,128)(2,1)S(1)} %copy-done.1, bf16[512,256]{1,0:T(8,128)(2,1)S(1)} %copy-done.2, ...), custom_call_target="tpu_custom_call" | custom-call | flops 268435456 | bytes 524288 | tf_op jit(solution)/shard_map/pallas_call | solution.py:91
  12.4 0.7 copy-done.11
  13.1 2.2 %shard_map.71 = (f32[256,256]{1,0:T(8,128)S(1)}, f32[256,256]{1,0:T(8,128)S(1)}, f32[32,512]{1,0:T(8,128)S(1)}, f32[64,512]{1,0:T(8,128)S(1)}) custom-call(s32[1]{0:T(128)} %bitcast.where_ref, bf16[512,1280]{1,0:T(8,128)(2,1)S(1)} %copy-done, bf16[512,256]{1,0:T(8,128)(2,1)S(1)} %copy-done.1, bf16[512,256]{1,0:T(8,128)(2,1)S(1)} %copy-done.2, ...), custom_call_target="tpu_custom_call" | custom-call | flops 268435456 | bytes 524288 | tf_op jit(solution)/shard_map/pallas_call | solution.py:91
  15.3 0.7 copy-done.10
  16.1 0.6 copy-done.5
  16.7 0.1 concatenate.30.own_ref
  16.8 3.0 %collective-permute-start.1 = (f32[32,512]{1,0:T(8,128)S(1)}, f32[32,512]{1,0:T(8,128)S(1)}, u32[]{:S(2)}, u32[]{:S(2)}) collective-permute-start(f32[32,512]{1,0:T(8,128)S(1)} %concatenate.30.own_ref), channel_id=1, source_target_pairs={{0,4},{4,0},{8,12},{12,8},{16,20},{20,16},{24,28},{28,24},{1,5},{5... | collective-permute-start | bytes 196616 | tf_op jit(solution)/shard_map/ppermute | solution.py:223
  19.9 2.2 %collective-permute-done.1 = f32[32,512]{1,0:T(8,128)S(1)} collective-permute-done((f32[32,512]{1,0:T(8,128)S(1)}, f32[32,512]{1,0:T(8,128)S(1)}, u32[]{:S(2)}, u32[]{:S(2)}) %collective-permute-start.1) | collective-permute-done | bytes 65568 | tf_op jit(solution)/shard_map/ppermute | solution.py:223
  22.1 2.2 %collective-permute-start.2 = (f32[48,512]{1,0:T(8,128)S(1)}, f32[48,512]{1,0:T(8,128)S(1)}, u32[]{:S(2)}, u32[]{:S(2)}) collective-permute-start(f32[48,512]{1,0:T(8,128)S(1)} %concatenate.33), channel_id=1, source_target_pairs={{0,8},{4,12},{8,0},{12,4},{16,24},{20,28},{24,16},{28,20},{1,9},{5... | collective-permute-start | bytes 294920 | tf_op jit(solution)/shard_map/ppermute | solution.py:223
  24.3 2.6 %collective-permute-done.2 = f32[48,512]{1,0:T(8,128)S(1)} collective-permute-done((f32[48,512]{1,0:T(8,128)S(1)}, f32[48,512]{1,0:T(8,128)S(1)}, u32[]{:S(2)}, u32[]{:S(2)}) %collective-permute-start.2) | collective-permute-done | bytes 98336 | tf_op jit(solution)/shard_map/ppermute | solution.py:223
  26.9 3.1 %collective-permute-start.3 = (f32[32,512]{1,0:T(8,128)S(1)}, f32[32,512]{1,0:T(8,128)S(1)}, u32[]{:S(2)}, u32[]{:S(2)}) collective-permute-start(f32[32,512]{1,0:T(8,128)S(1)} %pad_maximum_fusion.3), channel_id=1, source_target_pairs={{0,16},{4,20},{8,24},{12,28},{16,0},{20,4},{24,8},{28,12},{1,17},{... | collective-permute-start | bytes 196616 | tf_op jit(solution)/shard_map/ppermute | solution.py:223
  30.0 1.5 %collective-permute-start = (f32[256,384]{1,0:T(8,128)}, f32[256,384]{1,0:T(8,128)S(1)}, u32[]{:S(2)}, u32[]{:S(2)}) collective-permute-start(f32[256,384]{1,0:T(8,128)} %copy-done.9), channel_id=1, source_target_pairs={{0,4},{4,0},{8,12},{12,8},{16,20},{20,16},{24,28},{28,24},{1,5},{5... | collective-permute-start | bytes 1179656 | tf_op jit(solution)/shard_map/ppermute | solution.py:223
  31.5 1.6 %collective-permute-start.6 = (f32[256,256]{1,0:T(8,128)}, f32[256,256]{1,0:T(8,128)S(1)}, u32[]{:S(2)}, u32[]{:S(2)}) collective-permute-start(f32[256,256]{1,0:T(8,128)} %copy-done.11), channel_id=1, source_target_pairs={{0,8},{4,12},{8,0},{12,4},{16,24},{20,28},{24,16},{28,20},{1,9},{5... | collective-permute-start | bytes 786440 | tf_op jit(solution)/shard_map/ppermute | solution.py:223
  33.1 0.5 collective-permute-start.9
  33.6 1.5 %collective-permute-start.12 = (f32[256,256]{1,0:T(8,128)}, f32[256,256]{1,0:T(8,128)S(1)}, u32[]{:S(2)}, u32[]{:S(2)}) collective-permute-start(f32[256,256]{1,0:T(8,128)} %copy-done.10), channel_id=1, source_target_pairs={{0,4},{4,0},{8,12},{12,8},{16,20},{20,16},{24,28},{28,24},{1,5},{5... | collective-permute-start | bytes 786440 | tf_op jit(solution)/shard_map/ppermute | solution.py:223
  35.2 0.2 shard_map.72
  35.4 0.1 collective-permute-start.15
  35.5 2.6 %collective-permute-done.6.got_ref = f32[256,256]{1,0:T(8,128)S(1)} collective-permute-done((f32[256,256]{1,0:T(8,128)}, f32[256,256]{1,0:T(8,128)S(1)}, u32[]{:S(2)}, u32[]{:S(2)}) %collective-permute-start.6) | collective-permute-done | bytes 262176 | tf_op jit(solution)/shard_map/ppermute | solution.py:223
  38.1 0.2 shard_map.74
  38.3 0.4 collective-permute-start.7
  38.7 13.8 %collective-permute-done.12.got_ref = f32[256,256]{1,0:T(8,128)S(1)} collective-permute-done((f32[256,256]{1,0:T(8,128)}, f32[256,256]{1,0:T(8,128)S(1)}, u32[]{:S(2)}, u32[]{:S(2)}) %collective-permute-start.12) | collective-permute-done | bytes 262176 | tf_op jit(solution)/shard_map/ppermute | solution.py:223
  52.5 0.2 shard_map.76
  52.8 1.6 %collective-permute-start.13 = (f32[128,256]{1,0:T(8,128)S(1)}, f32[128,256]{1,0:T(8,128)S(1)}, u32[]{:S(2)}, u32[]{:S(2)}) collective-permute-start(f32[128,256]{1,0:T(8,128)S(1)} %get-tuple-element.54), channel_id=1, source_target_pairs={{0,8},{4,12},{8,0},{12,4},{16,24},{20,28},{24,16},{28,20},{1,9},{5... | collective-permute-start | bytes 393224 | tf_op jit(solution)/shard_map/ppermute | solution.py:223
  54.4 1.6 %collective-permute-start.16 = (f32[32,512]{1,0:T(8,128)S(1)}, f32[32,512]{1,0:T(8,128)S(1)}, u32[]{:S(2)}, u32[]{:S(2)}) collective-permute-start(f32[32,512]{1,0:T(8,128)S(1)} %add.63), channel_id=1, source_target_pairs={{0,2},{1,3},{2,0},{3,1},{4,6},{5,7},{6,4},{7,5},{8,10},{9,11},{10,... | collective-permute-start | bytes 196616 | tf_op jit(solution)/shard_map/ppermute | solution.py:223
  56.0 2.7 %collective-permute-done.16 = f32[32,512]{1,0:T(8,128)S(1)} collective-permute-done((f32[32,512]{1,0:T(8,128)S(1)}, f32[32,512]{1,0:T(8,128)S(1)}, u32[]{:S(2)}, u32[]{:S(2)}) %collective-permute-start.16) | collective-permute-done | bytes 65568 | tf_op jit(solution)/shard_map/ppermute | solution.py:223
  58.8 1.6 %collective-permute-start.17 = (f32[32,512]{1,0:T(8,128)S(1)}, f32[32,512]{1,0:T(8,128)S(1)}, u32[]{:S(2)}, u32[]{:S(2)}) collective-permute-start(f32[32,512]{1,0:T(8,128)S(1)} %add.64), channel_id=1, source_target_pairs={{0,4},{4,0},{8,12},{12,8},{16,20},{20,16},{24,28},{28,24},{1,5},{5... | collective-permute-start | bytes 196616 | tf_op jit(solution)/shard_map/ppermute | solution.py:223
  60.4 0.6 collective-permute-start.8
  61.0 0.4 collective-permute-start.14
  61.4 0.3 shard_map.73
  61.7 0.5 collective-permute-start.4
  62.2 0.3 shard_map.75
  62.5 1.6 %collective-permute-start.10 = (f32[128,384]{1,0:T(8,128)S(1)}, f32[128,384]{1,0:T(8,128)S(1)}, u32[]{:S(2)}, u32[]{:S(2)}) collective-permute-start(f32[128,384]{1,0:T(8,128)S(1)} %get-tuple-element.50), channel_id=1, source_target_pairs={{0,8},{4,12},{8,0},{12,4},{16,24},{20,28},{24,16},{28,20},{1,9},{5... | collective-permute-start | bytes 589832 | tf_op jit(solution)/shard_map/ppermute | solution.py:223
  64.2 0.5 collective-permute-start.18
  64.8 8.0 %collective-permute-done.18 = f32[32,512]{1,0:T(8,128)S(1)} collective-permute-done((f32[32,512]{1,0:T(8,128)S(1)}, f32[32,512]{1,0:T(8,128)S(1)}, u32[]{:S(2)}, u32[]{:S(2)}) %collective-permute-start.18) | collective-permute-done | bytes 65568 | tf_op jit(solution)/shard_map/ppermute | solution.py:223
  72.7 2.3 %collective-permute-start.19 = (f32[32,512]{1,0:T(8,128)S(1)}, f32[32,512]{1,0:T(8,128)S(1)}, u32[]{:S(2)}, u32[]{:S(2)}) collective-permute-start(f32[32,512]{1,0:T(8,128)S(1)} %add.66), channel_id=1, source_target_pairs={{0,16},{4,20},{8,24},{12,28},{16,0},{20,4},{24,8},{28,12},{1,17},{... | collective-permute-start | bytes 196616 | tf_op jit(solution)/shard_map/ppermute | solution.py:223
  75.1 0.7 collective-permute-start.5
  75.9 2.1 %collective-permute-done.19 = f32[32,512]{1,0:T(8,128)S(1)} collective-permute-done((f32[32,512]{1,0:T(8,128)S(1)}, f32[32,512]{1,0:T(8,128)S(1)}, u32[]{:S(2)}, u32[]{:S(2)}) %collective-permute-start.19) | collective-permute-done | bytes 65568 | tf_op jit(solution)/shard_map/ppermute | solution.py:223
  78.0 0.6 add.67
  78.6 2.4 %collective-permute-start.11 = (f32[64,384]{1,0:T(8,128)S(1)}, f32[64,384]{1,0:T(8,128)S(1)}, u32[]{:S(2)}, u32[]{:S(2)}) collective-permute-start(f32[64,384]{1,0:T(8,128)S(1)} %slice.117), channel_id=1, source_target_pairs={{0,16},{4,20},{8,24},{12,28},{16,0},{20,4},{24,8},{28,12},{1,17},{... | collective-permute-start | bytes 294920 | tf_op jit(solution)/shard_map/ppermute | solution.py:223
  81.1 0.1 collective-permute-done.5
  81.2 3.2 %collective-permute-done.11 = f32[64,384]{1,0:T(8,128)S(1)} collective-permute-done((f32[64,384]{1,0:T(8,128)S(1)}, f32[64,384]{1,0:T(8,128)S(1)}, u32[]{:S(2)}, u32[]{:S(2)}) %collective-permute-start.11) | collective-permute-done | bytes 98336 | tf_op jit(solution)/shard_map/ppermute | solution.py:223
  84.5 0.7 pad_maximum_fusion.2
  (62 shorter events, 0.6 us)
Async XLA Ops:
  0.6 2.1 %copy-start.7 = (s32[32]{0:T(128)S(1)}, s32[32]{0:T(128)}, u32[]{:S(2)}) copy-start(s32[32]{0:T(128)} %param.8) | copy-start | bytes 388
  0.6 2.1 %copy-start = (bf16[512,1280]{1,0:T(8,128)(2,1)S(1)}, bf16[512,1280]{1,0:T(8,128)(2,1)}, u32[]{:S(2)}) copy-start(bf16[512,1280]{1,0:T(8,128)(2,1)} %q_ref.7) | copy-start | bytes 3932164
  0.7 2.1 %copy-start.1 = (bf16[512,256]{1,0:T(8,128)(2,1)S(1)}, bf16[512,256]{1,0:T(8,128)(2,1)}, u32[]{:S(2)}) copy-start(bf16[512,256]{1,0:T(8,128)(2,1)} %k_ref.7) | copy-start | bytes 786436
  0.7 2.1 %copy-start.2 = (bf16[512,256]{1,0:T(8,128)(2,1)S(1)}, bf16[512,256]{1,0:T(8,128)(2,1)}, u32[]{:S(2)}) copy-start(bf16[512,256]{1,0:T(8,128)(2,1)} %v_ref.7) | copy-start | bytes 786436
  6.0 3.3 %copy-start.8 = (f32[256,384]{1,0:T(8,128)}, f32[256,384]{1,0:T(8,128)S(1)}, u32[]{:S(2)}) copy-start(f32[256,384]{1,0:T(8,128)S(1)} %get-tuple-element.48) | copy-start | bytes 1179652
  9.3 0.8 copy-start.9
  12.4 0.7 copy-start.11
  13.1 3.0 %copy-start.3 = (f32[64,512]{1,0:T(8,128)}, f32[64,512]{1,0:T(8,128)S(1)}, u32[]{:S(2)}) copy-start(f32[64,512]{1,0:T(8,128)S(1)} %get-tuple-element.36.refs_3_) | copy-start | bytes 393220
  15.3 0.7 copy-start.10
  16.0 0.7 copy-start.5
  16.7 18.5 %copy-start.4 = (f32[64,512]{1,0:T(8,128)S(1)}, f32[64,512]{1,0:T(8,128)}, u32[]{:S(2)}) copy-start(f32[64,512]{1,0:T(8,128)} %copy-done.3) | copy-start | bytes 393220
  16.7 18.5 %copy-start.6 = (f32[64,512]{1,0:T(8,128)S(1)}, f32[64,512]{1,0:T(8,128)}, u32[]{:S(2)}) copy-start(f32[64,512]{1,0:T(8,128)} %copy-done.5) | copy-start | bytes 393220
  16.8 5.3 %collective-permute-start.1 = (f32[32,512]{1,0:T(8,128)S(1)}, f32[32,512]{1,0:T(8,128)S(1)}, u32[]{:S(2)}, u32[]{:S(2)}) collective-permute-start(f32[32,512]{1,0:T(8,128)S(1)} %concatenate.30.own_ref), channel_id=1, source_target_pairs={{0,4},{4,0},{8,12},{12,8},{16,20},{20,16},{24,28},{28,24},{1,5},{5... | collective-permute-start | bytes 196616 | tf_op jit(solution)/shard_map/ppermute | solution.py:223
  22.1 4.8 %collective-permute-start.2 = (f32[48,512]{1,0:T(8,128)S(1)}, f32[48,512]{1,0:T(8,128)S(1)}, u32[]{:S(2)}, u32[]{:S(2)}) collective-permute-start(f32[48,512]{1,0:T(8,128)S(1)} %concatenate.33), channel_id=1, source_target_pairs={{0,8},{4,12},{8,0},{12,4},{16,24},{20,28},{24,16},{28,20},{1,9},{5... | collective-permute-start | bytes 294920 | tf_op jit(solution)/shard_map/ppermute | solution.py:223
  26.9 8.2 %collective-permute-start.3 = (f32[32,512]{1,0:T(8,128)S(1)}, f32[32,512]{1,0:T(8,128)S(1)}, u32[]{:S(2)}, u32[]{:S(2)}) collective-permute-start(f32[32,512]{1,0:T(8,128)S(1)} %pad_maximum_fusion.3), channel_id=1, source_target_pairs={{0,16},{4,20},{8,24},{12,28},{16,0},{20,4},{24,8},{28,12},{1,17},{... | collective-permute-start | bytes 196616 | tf_op jit(solution)/shard_map/ppermute | solution.py:223
  30.0 31.4 %collective-permute-start = (f32[256,384]{1,0:T(8,128)}, f32[256,384]{1,0:T(8,128)S(1)}, u32[]{:S(2)}, u32[]{:S(2)}) collective-permute-start(f32[256,384]{1,0:T(8,128)} %copy-done.9), channel_id=1, source_target_pairs={{0,4},{4,0},{8,12},{12,8},{16,20},{20,16},{24,28},{28,24},{1,5},{5... | collective-permute-start | bytes 1179656 | tf_op jit(solution)/shard_map/ppermute | solution.py:223
  31.5 6.6 %collective-permute-start.6 = (f32[256,256]{1,0:T(8,128)}, f32[256,256]{1,0:T(8,128)S(1)}, u32[]{:S(2)}, u32[]{:S(2)}) collective-permute-start(f32[256,256]{1,0:T(8,128)} %copy-done.11), channel_id=1, source_target_pairs={{0,8},{4,12},{8,0},{12,4},{16,24},{20,28},{24,16},{28,20},{1,9},{5... | collective-permute-start | bytes 786440 | tf_op jit(solution)/shard_map/ppermute | solution.py:223
  33.1 29.1 %collective-permute-start.9 = (f32[256,384]{1,0:T(8,128)}, f32[256,384]{1,0:T(8,128)S(1)}, u32[]{:S(2)}, u32[]{:S(2)}) collective-permute-start(f32[256,384]{1,0:T(8,128)} %copy-done.8), channel_id=1, source_target_pairs={{0,4},{4,0},{8,12},{12,8},{16,20},{20,16},{24,28},{28,24},{1,5},{5... | collective-permute-start | bytes 1179656 | tf_op jit(solution)/shard_map/ppermute | solution.py:223
  33.6 18.9 %collective-permute-start.12 = (f32[256,256]{1,0:T(8,128)}, f32[256,256]{1,0:T(8,128)S(1)}, u32[]{:S(2)}, u32[]{:S(2)}) collective-permute-start(f32[256,256]{1,0:T(8,128)} %copy-done.10), channel_id=1, source_target_pairs={{0,4},{4,0},{8,12},{12,8},{16,20},{20,16},{24,28},{28,24},{1,5},{5... | collective-permute-start | bytes 786440 | tf_op jit(solution)/shard_map/ppermute | solution.py:223
  35.4 19.0 %collective-permute-start.15 = (f32[32,512]{1,0:T(8,128)S(1)}, f32[32,512]{1,0:T(8,128)S(1)}, u32[]{:S(2)}, u32[]{:S(2)}) collective-permute-start(f32[32,512]{1,0:T(8,128)S(1)} %get-tuple-element.55), channel_id=1, source_target_pairs={{0,1},{1,0},{2,3},{3,2},{4,5},{5,4},{6,7},{7,6},{8,9},{9,8},{10,11... | collective-permute-start | bytes 196616 | tf_op jit(solution)/shard_map/ppermute | solution.py:223
  38.3 22.0 %collective-permute-start.7 = (f32[128,256]{1,0:T(8,128)S(1)}, f32[128,256]{1,0:T(8,128)S(1)}, u32[]{:S(2)}, u32[]{:S(2)}) collective-permute-start(f32[128,256]{1,0:T(8,128)S(1)} %get-tuple-element.46), channel_id=1, source_target_pairs={{0,16},{4,20},{8,24},{12,28},{16,0},{20,4},{24,8},{28,12},{1,17},{... | collective-permute-start | bytes 393224 | tf_op jit(solution)/shard_map/ppermute | solution.py:223
  52.8 8.2 %collective-permute-start.13 = (f32[128,256]{1,0:T(8,128)S(1)}, f32[128,256]{1,0:T(8,128)S(1)}, u32[]{:S(2)}, u32[]{:S(2)}) collective-permute-start(f32[128,256]{1,0:T(8,128)S(1)} %get-tuple-element.54), channel_id=1, source_target_pairs={{0,8},{4,12},{8,0},{12,4},{16,24},{20,28},{24,16},{28,20},{1,9},{5... | collective-permute-start | bytes 393224 | tf_op jit(solution)/shard_map/ppermute | solution.py:223
  54.4 4.3 %collective-permute-start.16 = (f32[32,512]{1,0:T(8,128)S(1)}, f32[32,512]{1,0:T(8,128)S(1)}, u32[]{:S(2)}, u32[]{:S(2)}) collective-permute-start(f32[32,512]{1,0:T(8,128)S(1)} %add.63), channel_id=1, source_target_pairs={{0,2},{1,3},{2,0},{3,1},{4,6},{5,7},{6,4},{7,5},{8,10},{9,11},{10,... | collective-permute-start | bytes 196616 | tf_op jit(solution)/shard_map/ppermute | solution.py:223
  58.8 5.4 %collective-permute-start.17 = (f32[32,512]{1,0:T(8,128)S(1)}, f32[32,512]{1,0:T(8,128)S(1)}, u32[]{:S(2)}, u32[]{:S(2)}) collective-permute-start(f32[32,512]{1,0:T(8,128)S(1)} %add.64), channel_id=1, source_target_pairs={{0,4},{4,0},{8,12},{12,8},{16,20},{20,16},{24,28},{28,24},{1,5},{5... | collective-permute-start | bytes 196616 | tf_op jit(solution)/shard_map/ppermute | solution.py:223
  60.4 4.3 %collective-permute-start.8 = (f32[64,256]{1,0:T(8,128)S(1)}, f32[64,256]{1,0:T(8,128)S(1)}, u32[]{:S(2)}, u32[]{:S(2)}) collective-permute-start(f32[64,256]{1,0:T(8,128)S(1)} %slice.115), channel_id=1, source_target_pairs={{0,4},{4,0},{8,12},{12,8},{16,20},{20,16},{24,28},{28,24},{1,5},{5... | collective-permute-start | bytes 196616 | tf_op jit(solution)/shard_map/ppermute | solution.py:223
  61.0 14.8 %collective-permute-start.14 = (f32[64,256]{1,0:T(8,128)S(1)}, f32[64,256]{1,0:T(8,128)S(1)}, u32[]{:S(2)}, u32[]{:S(2)}) collective-permute-start(f32[64,256]{1,0:T(8,128)S(1)} %slice.119), channel_id=1, source_target_pairs={{0,16},{4,20},{8,24},{12,28},{16,0},{20,4},{24,8},{28,12},{1,17},{... | collective-permute-start | bytes 196616 | tf_op jit(solution)/shard_map/ppermute | solution.py:223
  61.7 13.3 %collective-permute-start.4 = (f32[128,384]{1,0:T(8,128)S(1)}, f32[128,384]{1,0:T(8,128)S(1)}, u32[]{:S(2)}, u32[]{:S(2)}) collective-permute-start(f32[128,384]{1,0:T(8,128)S(1)} %get-tuple-element.41), channel_id=1, source_target_pairs={{0,8},{4,12},{8,0},{12,4},{16,24},{20,28},{24,16},{28,20},{1,9},{5... | collective-permute-start | bytes 589832 | tf_op jit(solution)/shard_map/ppermute | solution.py:223
  62.5 16.1 %collective-permute-start.10 = (f32[128,384]{1,0:T(8,128)S(1)}, f32[128,384]{1,0:T(8,128)S(1)}, u32[]{:S(2)}, u32[]{:S(2)}) collective-permute-start(f32[128,384]{1,0:T(8,128)S(1)} %get-tuple-element.50), channel_id=1, source_target_pairs={{0,8},{4,12},{8,0},{12,4},{16,24},{20,28},{24,16},{28,20},{1,9},{5... | collective-permute-start | bytes 589832 | tf_op jit(solution)/shard_map/ppermute | solution.py:223
  64.2 8.5 %collective-permute-start.18 = (f32[32,512]{1,0:T(8,128)S(1)}, f32[32,512]{1,0:T(8,128)S(1)}, u32[]{:S(2)}, u32[]{:S(2)}) collective-permute-start(f32[32,512]{1,0:T(8,128)S(1)} %add.65), channel_id=1, source_target_pairs={{0,8},{4,12},{8,0},{12,4},{16,24},{20,28},{24,16},{28,20},{1,9},{5... | collective-permute-start | bytes 196616 | tf_op jit(solution)/shard_map/ppermute | solution.py:223
  72.7 5.2 %collective-permute-start.19 = (f32[32,512]{1,0:T(8,128)S(1)}, f32[32,512]{1,0:T(8,128)S(1)}, u32[]{:S(2)}, u32[]{:S(2)}) collective-permute-start(f32[32,512]{1,0:T(8,128)S(1)} %add.66), channel_id=1, source_target_pairs={{0,16},{4,20},{8,24},{12,28},{16,0},{20,4},{24,8},{28,12},{1,17},{... | collective-permute-start | bytes 196616 | tf_op jit(solution)/shard_map/ppermute | solution.py:223
  75.1 6.1 %collective-permute-start.5 = (f32[64,384]{1,0:T(8,128)S(1)}, f32[64,384]{1,0:T(8,128)S(1)}, u32[]{:S(2)}, u32[]{:S(2)}) collective-permute-start(f32[64,384]{1,0:T(8,128)S(1)} %slice.113), channel_id=1, source_target_pairs={{0,16},{4,20},{8,24},{12,28},{16,0},{20,4},{24,8},{28,12},{1,17},{... | collective-permute-start | bytes 294920 | tf_op jit(solution)/shard_map/ppermute | solution.py:223
  78.6 5.8 %collective-permute-start.11 = (f32[64,384]{1,0:T(8,128)S(1)}, f32[64,384]{1,0:T(8,128)S(1)}, u32[]{:S(2)}, u32[]{:S(2)}) collective-permute-start(f32[64,384]{1,0:T(8,128)S(1)} %slice.117), channel_id=1, source_target_pairs={{0,16},{4,20},{8,24},{12,28},{16,0},{20,4},{24,8},{28,12},{1,17},{... | collective-permute-start | bytes 294920 | tf_op jit(solution)/shard_map/ppermute | solution.py:223

commit v2 on v1

v2 whole, which is shorter than its diff:
```python
import functools
import math

import jax
import jax.numpy as jnp
import numpy as np
from jax import lax
from jax.experimental import pallas as pl
from jax.experimental.pallas import tpu as pltpu
from jax.sharding import PartitionSpec as P

HD = 128
ROPE_BASE = 1000000.0
LOG2_SCALE = HD ** (-0.5) * math.log2(math.e)
VMEM_LIMIT = 16 * 1024 * 1024
FLASH_VMEM = 60 * 1024 * 1024
STAT_ROWS = 16
TILE = 128
HALF_PI = (1.5706787109375, 1.1761486530303955e-4, 9.920935796805404e-10)

CHUNKS = ((4, 0), (1, 1), (4, 0), (1, 1))
TIES = {
    "c0.2": ("c1.2",),
    "m.2": ("c0.2",),
    "c1.1": ("a.4",),
    "m.1": ("h.2",),
    "c3.4": ("c0.1",),
}
FENCES = ()
MASS_ORDER = ("h.1", "h.2", "m.1", "m.2", "m.4")


def position(rel, order):
    place = 0
    for bit in order:
        place = place * 2 + ((rel // bit) & 1)
    return place


def blocks_in_order(order):
    return sorted(range(2 ** len(order)), key=lambda rel: position(rel, order))


def rope_tables(pos_ref, frequency_ref, cos_ref, sin_ref):
    query_count = cos_ref.shape[0]
    half = query_count // 2
    rows = []
    for group in range(query_count // HD):
        row = pos_ref[group : group + 1, :].astype(jnp.float32)
        rows.append(jnp.broadcast_to(row, (HD, HD)).T)
    places = jnp.concatenate(rows, axis=0)
    left = lax.broadcasted_iota(jnp.int32, (1, HD), 1) < HD // 2
    angle = jnp.where(left, places[:half], places[half:]) * frequency_ref[...]
    turns = jnp.floor(angle * (2.0 / math.pi) + 0.5)
    rest = ((angle - turns * HALF_PI[0]) - turns * HALF_PI[1]) - turns * HALF_PI[2]
    square = rest * rest
    sine = rest + rest * square * (
        -1.6666654611e-1 + square * (8.3321608736e-3 + square * -1.9515295891e-4)
    )
    cosine = (1.0 - 0.5 * square) + square * square * (
        4.166664568298827e-2 + square * (-1.388731625493765e-3 + square * 2.443315711809948e-5)
    )
    quarter = turns.astype(jnp.int32) & 3
    odd = (quarter & 1) == 1
    cos_value = jnp.where(odd, sine, cosine) * jnp.where((quarter == 1) | (quarter == 2), -1.0, 1.0)
    sin_value = jnp.where(odd, cosine, sine) * jnp.where(quarter >= 2, -1.0, 1.0)
    cos_other = pltpu.roll(cos_value, HD // 2, axis=1)
    sin_other = pltpu.roll(sin_value, HD // 2, axis=1)
    cos_ref[:half, :] = jnp.where(left, cos_value, cos_other)
    cos_ref[half:, :] = jnp.where(left, cos_other, cos_value)
    sin_ref[:half, :] = jnp.where(left, -sin_value, sin_other)
    sin_ref[half:, :] = jnp.where(left, -sin_other, sin_value)


def flash_kernel(parts, group_size, slots, lens_ref, pos_ref, frequency_ref, q_hbm, k_hbm, v_hbm, *refs):
    refs = list(refs)
    keeps = [refs.pop(0) for _ in parts]
    sends = [refs.pop(0) for _ in parts]
    mass_hbm, stats_ref = refs.pop(0), refs.pop(0)
    q_ref, k_ref, v_ref, cos_ref, sin_ref, values, whole, halves, mass_ref, columns = refs[:10]
    kv_sems, half_sems, mass_sems = refs[10:]
    query_count, tok_here = q_ref.shape[0], k_ref.shape[0]
    stretch_count = lens_ref.shape[0]
    me = lax.axis_index("ctx")
    head_count = sum(count for _, count in parts)
    kv_count = head_count // group_size
    width = slots * stretch_count

    k_copy = pltpu.make_async_copy(k_hbm, k_ref, kv_sems.at[0])
    v_copy = pltpu.make_async_copy(v_hbm, v_ref, kv_sems.at[1])
    k_copy.start()
    q_copy = pltpu.make_async_copy(q_hbm, q_ref, kv_sems.at[2])
    q_copy.start()
    v_copy.start()

    rope_tables(pos_ref, frequency_ref, cos_ref, sin_ref)
    lane = lax.broadcasted_iota(jnp.int32, columns.shape, 1)
    columns[...] = jnp.where(lane < STAT_ROWS, 0.0, 1.0)
    lane = lax.broadcasted_iota(jnp.int32, (1, width), 1)
    starts, ends = jnp.zeros((1, width), jnp.int32), jnp.zeros((1, width), jnp.int32)
    edge = -me * tok_here
    for c in range(stretch_count):
        here = (lane & (stretch_count - 1)) == c
        starts = jnp.where(here, edge, starts)
        edge = edge + lens_ref[c]
        ends = jnp.where(here, edge, ends)
    at = lax.broadcasted_iota(jnp.int32, (tok_here, width), 0)
    inside = jnp.where((at >= starts) & (at < ends), 1.0, 0.0)
    slot_of_lane = lane // stretch_count
    for slot in range(slots):
        marks = jnp.where(slot_of_lane == slot, inside, 0.0).astype(jnp.bfloat16)
        for g in range(kv_count):
            values[g, slot, :, HD:] = marks
    v_copy.wait()
    for g in range(kv_count):
        for slot in range(slots):
            values[g, slot, :, :HD] = v_ref[:, g * HD : (g + 1) * HD]
    k_copy.wait()
    q_copy.wait()

    tile = min(TILE, query_count)
    half_copies, mass_copies = [], []
    for j in range(head_count):
        g = j // group_size
        lanes = slice(j // slots * width, (j // slots + 1) * width)
        for t in range(query_count // tile):
            rows = slice(t * tile, (t + 1) * tile)
            q = q_ref[rows, j * HD : (j + 1) * HD].astype(jnp.float32)
            turned = pltpu.roll(q, HD // 2, axis=1)
            roped = (q * cos_ref[rows, :] + turned * sin_ref[rows, :]).astype(jnp.bfloat16)
            raw = lax.dot_general(
                roped, k_ref[:, g * HD : (g + 1) * HD], (((1,), (1,)), ((), ())),
                preferred_element_type=jnp.float32,
            )
            top = jnp.max(raw, axis=1, keepdims=True)
            weights = jnp.exp2((raw - top) * LOG2_SCALE)
            columns[rows, j : j + 1] = top
            columns[rows, STAT_ROWS + j : STAT_ROWS + j + 1] = jnp.sum(weights, axis=1, keepdims=True)
            out = jnp.dot(
                weights.astype(jnp.bfloat16), values[g, j % slots], preferred_element_type=jnp.float32
            )
            whole[j % 2, rows, :] = out[:, :HD]
            if j % slots == 0:
                mass_ref[rows, lanes] = out[:, HD:]
            else:
                mass_ref[rows, lanes] += out[:, HD:]
        part, local_head = 0, j
        while local_head >= parts[part][1]:
            local_head -= parts[part][1]
            part += 1
        blocks = blocks_in_order(parts[part][0])
        size = query_count // len(blocks)
        half = len(blocks) // 2
        for place, rel in enumerate(blocks):
            source = pl.multiple_of((me ^ rel) * size, size)
            side, place = place // half, place % half
            halves[j, side, place * size : (place + 1) * size, :] = whole[j % 2, pl.ds(source, size), :]
        if local_head == parts[part][1] - 1:
            first_head = j - local_head
            for i in range(first_head, j + 1):
                lanes = pl.ds((i - first_head) * HD, HD)
                for side, target in ((0, keeps[part]), (1, sends[part])):
                    half_copies.append(
                        pltpu.make_async_copy(
                            halves.at[i, side], target.at[:, lanes], half_sems.at[i, side]
                        )
                    )
                    half_copies[-1].start()
    for group in range(-(-head_count // slots)):
        lanes = pl.ds(group * width, width)
        mass_copies.append(
            pltpu.make_async_copy(mass_ref.at[:, lanes], mass_hbm.at[:, lanes], mass_sems.at[group])
        )
        mass_copies[-1].start()
    stats_ref[...] = columns[...].T[: 2 * STAT_ROWS]
    for copy in half_copies + mass_copies:
        copy.wait()


def flash(parts, group_size, queries, keys, values, lens, places, frequency):
    query_count = queries.shape[0]
    tok_here = keys.shape[0]
    stretch_count = lens.shape[0]
    head_count = sum(count for _, count in parts)
    half = query_count // 2
    slots = max(1, HD // stretch_count)
    width = slots * stretch_count
    groups = -(-head_count // slots)
    work = head_count * query_count * tok_here
    vmem = pl.BlockSpec(memory_space=pltpu.VMEM)
    hbm = pl.BlockSpec(memory_space=pltpu.HBM)
    halves = [jax.ShapeDtypeStruct((half, count * HD), jnp.float32) for _, count in parts]
    mass = jax.ShapeDtypeStruct((query_count, groups * width), jnp.float32)
    stats = jax.ShapeDtypeStruct((2 * STAT_ROWS, query_count), jnp.float32)
    return pl.pallas_call(
        functools.partial(flash_kernel, parts, group_size, slots),
        in_specs=[pl.BlockSpec(memory_space=pltpu.SMEM), vmem, vmem, hbm, hbm, hbm],
        out_specs=[hbm] * (2 * len(parts) + 1) + [vmem],
        out_shape=halves + halves + [mass, stats],
        scratch_shapes=[
            pltpu.VMEM(queries.shape, jnp.bfloat16),
            pltpu.VMEM(keys.shape, jnp.bfloat16),
            pltpu.VMEM(values.shape, jnp.bfloat16),
            pltpu.VMEM((query_count, HD), jnp.float32),
            pltpu.VMEM((query_count, HD), jnp.float32),
            pltpu.VMEM((head_count // group_size, slots, tok_here, HD + width), jnp.bfloat16),
            pltpu.VMEM((2, query_count, HD), jnp.float32),
            pltpu.VMEM((head_count, 2, half, HD), jnp.float32),
            pltpu.VMEM(mass.shape, jnp.float32),
            pltpu.VMEM((query_count, HD), jnp.float32),
            pltpu.SemaphoreType.DMA((3,)),
            pltpu.SemaphoreType.DMA((head_count, 2)),
            pltpu.SemaphoreType.DMA((groups,)),
        ],
        compiler_params=pltpu.CompilerParams(vmem_limit_bytes=FLASH_VMEM),
        cost_estimate=pl.CostEstimate(
            flops=work * 4 * HD, bytes_accessed=work, transcendentals=work
        ),
    )(lens, places, frequency, queries, keys, values)


def weigh_kernel(orders, head_counts, factor, own_ref, whole_ref, *refs):
    order_count = len(orders)
    tops_refs = refs[:order_count]
    mass_refs = refs[order_count : order_count + len(head_counts)]
    out_ref = refs[order_count + len(head_counts)]
    weight_refs = refs[order_count + len(head_counts) + 1 : -1]
    columns = refs[-1]
    me = lax.axis_index("ctx")
    top, inverse = whole_ref[:STAT_ROWS], 1.0 / whole_ref[STAT_ROWS:]
    mine = jnp.exp2(own_ref[:STAT_ROWS] - top) * inverse
    stretch_count = out_ref.shape[0]
    slots = max(1, HD // stretch_count)
    width = slots * stretch_count
    total, head = None, 0
    for count, mass_ref in zip(head_counts, mass_refs):
        for j in range(count):
            if j % slots == 0:
                turned = mass_ref[:, j // slots * width : (j // slots + 1) * width].T
            at = j % slots * stretch_count
            term = turned[at : at + stretch_count] * mine[head : head + 1]
            total = term if total is None else total + term
            head += 1
    out_ref[...] = total * factor
    theirs = [jnp.exp2(tops_ref[...] - top) * inverse for tops_ref in tops_refs]
    filled = (1 + order_count) * STAT_ROWS
    rest = jnp.zeros((HD - filled, top.shape[1]), jnp.float32)
    columns[...] = jnp.concatenate([mine] + theirs + [rest], axis=0).T
    for order, weight_ref in zip(orders, weight_refs):
        blocks = blocks_in_order(order)
        rows = columns.shape[0] // len(blocks)
        for place, rel in enumerate(blocks[: len(blocks) // 2]):
            source = pl.multiple_of((me ^ rel) * rows, rows)
            weight_ref[place * rows : (place + 1) * rows, :] = columns[pl.ds(source, rows), :]


def weigh(orders, head_counts, stretch_count, factor, own, whole, tops, masses):
    query_count = own.shape[1]
    vmem = pl.BlockSpec(memory_space=pltpu.VMEM)
    return pl.pallas_call(
        functools.partial(weigh_kernel, orders, head_counts, factor),
        in_specs=[vmem] * (2 + len(tops) + len(masses)),
        out_specs=[vmem] * (1 + len(orders)),
        out_shape=[jax.ShapeDtypeStruct((stretch_count, query_count), jnp.float32)]
        + [jax.ShapeDtypeStruct((query_count // 2, HD), jnp.float32)] * len(orders),
        scratch_shapes=[pltpu.VMEM((query_count, HD), jnp.float32)],
        compiler_params=pltpu.CompilerParams(vmem_limit_bytes=VMEM_LIMIT),
        cost_estimate=pl.CostEstimate(flops=1 << 20, bytes_accessed=1 << 20, transcendentals=1 << 14),
    )(own, whole, *tops, *masses)


def merge_kernel(first_head, other, keep_ref, got_ref, weight_ref, near_ref, far_ref):
    half = near_ref.shape[0]
    for j in range(keep_ref.shape[1] // HD):
        columns = slice(j * HD, (j + 1) * HD)
        head = first_head + j
        theirs = (1 + other) * STAT_ROWS + head
        for rows, target in ((slice(0, half), near_ref), (slice(half, 2 * half), far_ref)):
            target[:, columns] = (
                keep_ref[rows, columns] * weight_ref[rows, head : head + 1]
                + got_ref[rows, columns] * weight_ref[rows, theirs : theirs + 1]
            )


def merge(first_head, other, keep, got, weights):
    rows, columns = keep.shape
    vmem = pl.BlockSpec(memory_space=pltpu.VMEM)
    return pl.pallas_call(
        functools.partial(merge_kernel, first_head, other),
        in_specs=[vmem] * 3,
        out_specs=[vmem] * 2,
        out_shape=[jax.ShapeDtypeStruct((rows // 2, columns), jnp.float32)] * 2,
        compiler_params=pltpu.CompilerParams(vmem_limit_bytes=VMEM_LIMIT),
        cost_estimate=pl.CostEstimate(
            flops=3 * rows * columns, bytes_accessed=12 * rows * columns, transcendentals=0
        ),
    )(keep, got, weights)


def in_log2(stats):
    return jnp.concatenate([stats[:STAT_ROWS] * LOG2_SCALE, stats[STAT_ROWS:]], axis=0)


def join_stats(one, two):
    top = jnp.maximum(one[:STAT_ROWS], two[:STAT_ROWS])
    total = one[STAT_ROWS:] * jnp.exp2(one[:STAT_ROWS] - top) + two[STAT_ROWS:] * jnp.exp2(
        two[:STAT_ROWS] - top
    )
    return jnp.concatenate([top, total], axis=0)


def local(queries, keys, values, stretch_lengths, query_pos):
    query_count = queries.shape[0]
    heads_here = queries.shape[1] // HD
    group_size = heads_here // (keys.shape[1] // HD)
    stretch_count = stretch_lengths.shape[0]
    ctx_size, head_size = lax.axis_size("ctx"), lax.axis_size("head")
    bits = tuple(2**i for i in range(ctx_size.bit_length() - 1))
    head_bits = tuple(2**i for i in range(head_size.bit_length() - 1))
    results = {}

    def once(make):
        @functools.wraps(make)
        def cached(*key):
            if (make.__name__, *key) not in results:
                results[(make.__name__, *key)] = make(*key)
            return results[(make.__name__, *key)]

        return cached

    def exchange(array, axis, bit):
        return lax.ppermute(array, axis, [(i, i ^ bit) for i in range(lax.axis_size(axis))])

    def after(names, arrays):
        waits = [arrived(other) for name in names for other in TIES.get(name, ()) if known(other)]
        return lax.optimization_barrier((*arrays, *waits))[: len(arrays)] if waits else arrays

    def run(names, step, state):
        state = tuple(after(names, state))
        if names not in FENCES:
            return step(names[0], *state)

        def steps(*state):
            for name in names:
                state = step(name, *state)
            return state

        return lax.cond(stretch_lengths[0] > 0, steps, lambda *state: state, *state)

    def runs(names):
        fences = [tuple(name for name in fence if name in names) for fence in FENCES]
        fences = [fence for fence in fences if fence]
        fenced = {name for fence in fences for name in fence}
        starts = {fence[0]: fence for fence in fences}
        return [starts.get(name, (name,)) for name in names if name in starts or name not in fenced]

    lane = np.arange(HD) % (HD // 2)
    frequency = jnp.asarray((ROPE_BASE ** (-2.0 * lane / HD)).astype(np.float32).reshape(1, HD))
    places = query_pos.reshape(query_count // HD, HD)
    parts = []
    for count, turn in CHUNKS:
        rotated = bits[turn:] + bits[:turn]
        first = bits[-turn]
        moved = (first,) + tuple(bit for bit in bits if bit != first)
        parts.append((rotated if turn >= 0 else moved, count))
    parts = tuple(parts)
    mass_steps = ["h.%d" % bit for bit in head_bits] + ["m.%d" % bit for bit in bits]
    mass_steps.sort(key=lambda name: MASS_ORDER.index(name) if name in MASS_ORDER else len(MASS_ORDER))
    orders = {}
    for order, _ in parts:
        orders.setdefault(order, len(orders))
    *halves, masses, raw_stats = flash(
        parts, group_size, queries, keys, values, stretch_lengths, places, frequency
    )
    keeps, sends = halves[: len(parts)], halves[len(parts) :]
    own = lax.optimization_barrier(in_log2(raw_stats))
    firsts = [order[0] for order in orders]

    def known(name):
        kind, bit = name.split(".")
        if kind == "h":
            return int(bit) in head_bits
        return int(bit) in bits

    stat_steps = ["a.%d" % bit for bit in bits]
    stat_runs, mass_runs = runs(stat_steps), runs(mass_steps)
    run_of = {name: i for names in (stat_runs, mass_runs) for i, run_ in enumerate(names) for name in run_}

    @once
    def arrived(name):
        kind, bit = name.split(".")
        if kind == "a":
            return stats(run_of[name] + 1)[0]
        if kind in ("h", "m"):
            return mass(run_of[name] + 1)[0]
        n, bit = int(kind[1:]), int(bit)
        i = parts[n][0].index(bit)
        send = sends[n] if i == 0 else halved(n, i)[1]
        return exchange(after([name], (send,))[0], "ctx", bit)

    def stat_step(name, joined, *tops):
        bit = int(name.split(".")[1])
        opening = bit == bits[0]
        message = raw_stats if opening else joined
        if bit in firsts and not opening:
            message = jnp.concatenate([message, own[:STAT_ROWS]], axis=0)
        got = exchange(message, "ctx", bit)
        joined = join_stats(joined, in_log2(got) if opening else got[: 2 * STAT_ROWS])
        if bit in firsts:
            top = got[:STAT_ROWS] * LOG2_SCALE if opening else got[2 * STAT_ROWS :]
            tops = tuple(top if i == firsts.index(bit) else old for i, old in enumerate(tops))
        return (joined, *tops)

    def mass_step(name, total):
        kind, bit = name.split(".")
        return (total + exchange(total, "head" if kind == "h" else "ctx", int(bit)),)

    @once
    def stats(step):
        if step == 0:
            return (own,) + (own[:STAT_ROWS],) * len(firsts)
        return run(stat_runs[step - 1], stat_step, stats(step - 1))

    @once
    def weighed():
        joined, *tops = stats(len(stat_runs))
        factor = stretch_count / (heads_here * head_size)
        return weigh(tuple(orders), (heads_here,), stretch_count, factor, own, joined, tops, [masses])

    @once
    def mass(step):
        if step == 0:
            return (weighed()[0],)
        return run(mass_runs[step - 1], mass_step, mass(step - 1))

    @once
    def halved(n, i):
        order, count = parts[n]
        got = arrived("c%d.%d" % (n, order[i - 1]))
        if i == 1:
            first_head = sum(c for _, c in parts[:n])
            kind = orders[order]
            return merge(first_head, kind, keeps[n], got, weighed()[1 + kind])
        total = halved(n, i - 1)[0] + got
        if i == len(order):
            return total
        rows = total.shape[0] // 2
        return total[:rows], total[rows:]

    done = [halved(n, len(bits)).astype(jnp.bfloat16) for n in range(len(parts))]
    return jnp.concatenate(done, axis=1), mass(len(mass_runs))[0]


def solution(mesh):
    placed = (P(None, "head"), P("ctx", "head"), P("ctx", "head"), P(), P())
    return jax.shard_map(
        local, mesh=mesh, in_specs=placed, out_specs=(P("ctx", "head"), P()), check_vma=False
    )
```

time: 85.3 us -> 60.4 us (0.71)
  waiting for transfers between devices: 37.5 us -> 15.9 us
  starting transfers between devices: 27.8 us -> 31.2 us
  local copies, waits for them, and re-layouts: 3.06 us -> 0.05 us
  Pallas kernels: 12.2 us -> 9.68 us
  other arithmetic: 3.59 us -> 2.41 us
    ppermute x20, waiting for transfers between devices: 37.5 us -> 15.9 us  [exchange(): lax.ppermute(array, axis, [(i, i ^ bit) for i in range(lax.axis_size(axis...]
    ppermute x20, starting transfers between devices: 27.8 us -> 31.2 us  [exchange(): lax.ppermute(array, axis, [(i, i ^ bit) for i in range(lax.axis_size(axis...]
    unnamed x24 -> x10, local copies, waits for them, and re-layouts: 2.78 us -> 0.02 us
    pallas_call x4 -> x1, Pallas kernels: 11.1 us -> 8.33 us  [flash(): pl.pallas_call(functools.partial(flash_kernel, parts, group_size, slots),...]
    neg x1 -> x0, other arithmetic: 0.99 us -> none  [local(): sine = jnp.concatenate([-sine, sine], axis=1)]
  transfers between devices with their start and end apart: 20 -> 20, of which waited for: 9 -> 8; matrix products, arithmetic and copies ran while one was open for 1% -> 3% of each run, Pallas kernels for 1% -> 2%
where the time goes in v2:
time: 60.4 us; the launch traced here: 60.1 us
  starting transfers between devices  31.2 us (52%)
  waiting for transfers between devices  15.9 us (26%)
  Pallas kernels  9.68 us (16%)
  other arithmetic  2.41 us (4%)
  between operations  0.85 us (1%)
    ppermute x20, starting transfers between devices, exchange(): lax.ppermute(array, axis, [(i, i ^ bit) for i in range(lax.axis_size(axis...  31.2 us
    ppermute x20, waiting for transfers between devices, exchange(): lax.ppermute(array, axis, [(i, i ^ bit) for i in range(lax.axis_size(axis...  15.9 us
    pallas_call x1, Pallas kernels, flash(): pl.pallas_call(functools.partial(flash_kernel, parts, group_size, slots),...  8.33 us
  transfers between devices with their start and end apart: 20, of which 8 were waited for; matrix products, arithmetic and copies ran while one was open for 3% of the time, Pallas kernels for 2%

profile of v2, /device:TPU:0, one launch (start us, length us, event | category | flops | bytes accessed | tf_op | source)
XLA Modules:
  0.0 60.1 jit_solution(3498345658509881883)
XLA Ops:
  0.6 8.3 %shard_map.77 = (f32[256,512]{1,0:T(8,128)}, f32[256,128]{1,0:T(8,128)}, f32[256,512]{1,0:T(8,128)}, f32[256,128]{1,0:T(8,128)}, f32[256,512]{1,0:T(8,128)}, /*i...) custom-call(s32[32]{0:T(128)} %lens_ref.1, ...), custom_call_target="tpu_custom_call" | custom-call | flops 1342177280 | bytes 2621440 | tf_op jit(solution)/shard_map/pallas_call | solution.py:195
  9.0 0.0 copy-start.4
  9.0 3.0 %collective-permute-start.1 = (f32[32,512]{1,0:T(8,128)}, f32[32,512]{1,0:T(8,128)S(1)}, u32[]{:S(2)}, u32[]{:S(2)}) collective-permute-start(f32[32,512]{1,0:T(8,128)} %get-tuple-element.29), channel_id=1, source_target_pairs={{0,4},{4,0},{8,12},{12,8},{16,20},{20,16},{24,28},{28,24},{1,5},{5... | collective-permute-start | bytes 196616 | tf_op jit(solution)/shard_map/ppermute | solution.py:332
  12.0 0.8 %slice_multiply_fusion.5 = (f32[16,512]{1,0:T(8,128)S(1)}, f32[16,512]{1,0:T(8,128)S(1)}) fusion(f32[32,512]{1,0:T(8,128)} %get-tuple-element.29), kind=kLoop, calls=%fused_computation.21 | loop fusion | flops 8192 | bytes 131072 | tf_op jit(solution)/shard_map/mul | solution.py:301
  12.8 1.6 %collective-permute-done.1 = f32[32,512]{1,0:T(8,128)S(1)} collective-permute-done((f32[32,512]{1,0:T(8,128)}, f32[32,512]{1,0:T(8,128)S(1)}, u32[]{:S(2)}, u32[]{:S(2)}) %collective-permute-start.1) | collective-permute-done | bytes 65568 | tf_op jit(solution)/shard_map/ppermute | solution.py:332
  14.5 2.2 %collective-permute-start.2 = (f32[48,512]{1,0:T(8,128)S(1)}, f32[48,512]{1,0:T(8,128)S(1)}, u32[]{:S(2)}, u32[]{:S(2)}) collective-permute-start(f32[48,512]{1,0:T(8,128)S(1)} %pad_maximum_fusion.1), channel_id=1, source_target_pairs={{0,8},{4,12},{8,0},{12,4},{16,24},{20,28},{24,16},{28,20},{1,9},{5... | collective-permute-start | bytes 294920 | tf_op jit(solution)/shard_map/ppermute | solution.py:332
  16.7 1.5 %collective-permute-start = (f32[256,512]{1,0:T(8,128)}, f32[256,512]{1,0:T(8,128)S(1)}, u32[]{:S(2)}, u32[]{:S(2)}) collective-permute-start(f32[256,512]{1,0:T(8,128)} %get-tuple-element.28), channel_id=1, source_target_pairs={{0,4},{4,0},{8,12},{12,8},{16,20},{20,16},{24,28},{28,24},{1,5},{5... | collective-permute-start | bytes 1572872 | tf_op jit(solution)/shard_map/ppermute | solution.py:332
  18.2 1.1 %collective-permute-done.2 = f32[48,512]{1,0:T(8,128)S(1)} collective-permute-done((f32[48,512]{1,0:T(8,128)S(1)}, f32[48,512]{1,0:T(8,128)S(1)}, u32[]{:S(2)}, u32[]{:S(2)}) %collective-permute-start.2) | collective-permute-done | bytes 98336 | tf_op jit(solution)/shard_map/ppermute | solution.py:332
  19.3 3.1 %collective-permute-start.3 = (f32[32,512]{1,0:T(8,128)S(1)}, f32[32,512]{1,0:T(8,128)S(1)}, u32[]{:S(2)}, u32[]{:S(2)}) collective-permute-start(f32[32,512]{1,0:T(8,128)S(1)} %pad_maximum_fusion.3), channel_id=1, source_target_pairs={{0,16},{4,20},{8,24},{12,28},{16,0},{20,4},{24,8},{28,12},{1,17},{... | collective-permute-start | bytes 196616 | tf_op jit(solution)/shard_map/ppermute | solution.py:332
  22.4 1.5 %collective-permute-start.9 = (f32[256,512]{1,0:T(8,128)}, f32[256,512]{1,0:T(8,128)S(1)}, u32[]{:S(2)}, u32[]{:S(2)}) collective-permute-start(f32[256,512]{1,0:T(8,128)} %get-tuple-element.42), channel_id=1, source_target_pairs={{0,4},{4,0},{8,12},{12,8},{16,20},{20,16},{24,28},{28,24},{1,5},{5... | collective-permute-start | bytes 1572872 | tf_op jit(solution)/shard_map/ppermute | solution.py:332
  23.9 1.6 %collective-permute-start.4 = (f32[256,128]{1,0:T(8,128)}, f32[256,128]{1,0:T(8,128)S(1)}, u32[]{:S(2)}, u32[]{:S(2)}) collective-permute-start(f32[256,128]{1,0:T(8,128)} %get-tuple-element.34), channel_id=1, source_target_pairs={{0,8},{4,12},{8,0},{12,4},{16,24},{20,28},{24,16},{28,20},{1,9},{5... | collective-permute-start | bytes 393224 | tf_op jit(solution)/shard_map/ppermute | solution.py:332
  25.5 0.4 collective-permute-start.12
  25.9 0.0 collective-permute-done.3
  26.0 0.4 shard_map.78
  26.3 0.1 collective-permute-start.15
  26.4 2.7 %collective-permute-done.4.got_ref = f32[256,128]{1,0:T(8,128)S(1)} collective-permute-done((f32[256,128]{1,0:T(8,128)}, f32[256,128]{1,0:T(8,128)S(1)}, u32[]{:S(2)}, u32[]{:S(2)}) %collective-permute-start.4) | collective-permute-done | bytes 131104 | tf_op jit(solution)/shard_map/ppermute | solution.py:332
  29.1 0.1 shard_map.80
  29.2 0.4 collective-permute-start.7
  29.6 0.0 collective-permute-done.15
  29.6 1.6 %collective-permute-start.16 = (f32[32,512]{1,0:T(8,128)S(1)}, f32[32,512]{1,0:T(8,128)S(1)}, u32[]{:S(2)}, u32[]{:S(2)}) collective-permute-start(f32[32,512]{1,0:T(8,128)S(1)} %add.59), channel_id=1, source_target_pairs={{0,2},{1,3},{2,0},{3,1},{4,6},{5,7},{6,4},{7,5},{8,10},{9,11},{10,... | collective-permute-start | bytes 196616 | tf_op jit(solution)/shard_map/ppermute | solution.py:332
  31.2 0.0 collective-permute-done.12.got_ref
  31.2 0.1 shard_map.82
  31.4 0.4 collective-permute-done.got_ref
  31.7 2.6 %collective-permute-start.13 = (f32[128,128]{1,0:T(8,128)S(1)}, f32[128,128]{1,0:T(8,128)S(1)}, u32[]{:S(2)}, u32[]{:S(2)}) collective-permute-start(f32[128,128]{1,0:T(8,128)S(1)} %get-tuple-element.49), channel_id=1, source_target_pairs={{0,16},{4,20},{8,24},{12,28},{16,0},{20,4},{24,8},{28,12},{1,17},{... | collective-permute-start | bytes 196616 | tf_op jit(solution)/shard_map/ppermute | solution.py:332
  34.3 0.4 shard_map.79
  34.7 1.4 %collective-permute-start.5 = (f32[128,512]{1,0:T(8,128)S(1)}, f32[128,512]{1,0:T(8,128)S(1)}, u32[]{:S(2)}, u32[]{:S(2)}) collective-permute-start(f32[128,512]{1,0:T(8,128)S(1)} %get-tuple-element.35), channel_id=1, source_target_pairs={{0,8},{4,12},{8,0},{12,4},{16,24},{20,28},{24,16},{28,20},{1,9},{5... | collective-permute-start | bytes 786440 | tf_op jit(solution)/shard_map/ppermute | solution.py:332
  36.1 0.7 %collective-permute-start.8 = (f32[64,128]{1,0:T(8,128)S(1)}, f32[64,128]{1,0:T(8,128)S(1)}, u32[]{:S(2)}, u32[]{:S(2)}) collective-permute-start(f32[64,128]{1,0:T(8,128)S(1)} %slice.96), channel_id=1, source_target_pairs={{0,4},{4,0},{8,12},{12,8},{16,20},{20,16},{24,28},{28,24},{1,5},{5... | collective-permute-start | bytes 98312 | tf_op jit(solution)/shard_map/ppermute | solution.py:332
  36.8 0.0 collective-permute-done.16
  36.8 1.4 %collective-permute-start.17 = (f32[32,512]{1,0:T(8,128)S(1)}, f32[32,512]{1,0:T(8,128)S(1)}, u32[]{:S(2)}, u32[]{:S(2)}) collective-permute-start(f32[32,512]{1,0:T(8,128)S(1)} %add.60), channel_id=1, source_target_pairs={{0,4},{4,0},{8,12},{12,8},{16,20},{20,16},{24,28},{28,24},{1,5},{5... | collective-permute-start | bytes 196616 | tf_op jit(solution)/shard_map/ppermute | solution.py:332
  38.3 3.2 %collective-permute-done.9.got_ref = f32[256,512]{1,0:T(8,128)S(1)} collective-permute-done((f32[256,512]{1,0:T(8,128)}, f32[256,512]{1,0:T(8,128)S(1)}, u32[]{:S(2)}, u32[]{:S(2)}) %collective-permute-start.9) | collective-permute-done | bytes 524320 | tf_op jit(solution)/shard_map/ppermute | solution.py:332
  41.4 0.4 shard_map.81
  41.8 0.4 collective-permute-start.10
  42.2 0.0 collective-permute-done.13
  42.2 1.6 %collective-permute-start.14 = (f32[64,128]{1,0:T(8,128)S(1)}, f32[64,128]{1,0:T(8,128)S(1)}, u32[]{:S(2)}, u32[]{:S(2)}) collective-permute-start(f32[64,128]{1,0:T(8,128)S(1)} %slice.100), channel_id=1, source_target_pairs={{0,4},{4,0},{8,12},{12,8},{16,20},{20,16},{24,28},{28,24},{1,5},{5... | collective-permute-start | bytes 98312 | tf_op jit(solution)/shard_map/ppermute | solution.py:332
  43.9 0.0 collective-permute-done.8
  43.9 0.0 collective-permute-done.17
  43.9 0.0 collective-permute-done.5
  43.9 1.9 %collective-permute-start.18 = (f32[32,512]{1,0:T(8,128)S(1)}, f32[32,512]{1,0:T(8,128)S(1)}, u32[]{:S(2)}, u32[]{:S(2)}) collective-permute-start(f32[32,512]{1,0:T(8,128)S(1)} %add.61), channel_id=1, source_target_pairs={{0,8},{4,12},{8,0},{12,4},{16,24},{20,28},{24,16},{28,20},{1,9},{5... | collective-permute-start | bytes 196616 | tf_op jit(solution)/shard_map/ppermute | solution.py:332
  45.8 2.7 %collective-permute-start.6 = (f32[64,512]{1,0:T(8,128)S(1)}, f32[64,512]{1,0:T(8,128)S(1)}, u32[]{:S(2)}, u32[]{:S(2)}) collective-permute-start(f32[64,512]{1,0:T(8,128)S(1)} %slice.94), channel_id=1, source_target_pairs={{0,16},{4,20},{8,24},{12,28},{16,0},{20,4},{24,8},{28,12},{1,17},{... | collective-permute-start | bytes 393224 | tf_op jit(solution)/shard_map/ppermute | solution.py:332
  48.5 0.0 collective-permute-done.14
  48.5 2.3 %collective-permute-done.10 = f32[128,512]{1,0:T(8,128)S(1)} collective-permute-done((f32[128,512]{1,0:T(8,128)S(1)}, f32[128,512]{1,0:T(8,128)S(1)}, u32[]{:S(2)}, u32[]{:S(2)}) %collective-permute-start.10) | collective-permute-done | bytes 262176 | tf_op jit(solution)/shard_map/ppermute | solution.py:332
  50.9 2.5 %collective-permute-start.11 = (f32[64,512]{1,0:T(8,128)S(1)}, f32[64,512]{1,0:T(8,128)S(1)}, u32[]{:S(2)}, u32[]{:S(2)}) collective-permute-start(f32[64,512]{1,0:T(8,128)S(1)} %slice.98), channel_id=1, source_target_pairs={{0,16},{4,20},{8,24},{12,28},{16,0},{20,4},{24,8},{28,12},{1,17},{... | collective-permute-start | bytes 393224 | tf_op jit(solution)/shard_map/ppermute | solution.py:332
  53.4 0.6 %collective-permute-start.19 = (f32[32,512]{1,0:T(8,128)S(1)}, f32[32,512]{1,0:T(8,128)S(1)}, u32[]{:S(2)}, u32[]{:S(2)}) collective-permute-start(f32[32,512]{1,0:T(8,128)S(1)} %add.62), channel_id=1, source_target_pairs={{0,16},{4,20},{8,24},{12,28},{16,0},{20,4},{24,8},{28,12},{1,17},{... | collective-permute-start | bytes 196616 | tf_op jit(solution)/shard_map/ppermute | solution.py:332
  54.1 0.0 collective-permute-done.6
  54.1 4.0 %collective-permute-done.11 = f32[64,512]{1,0:T(8,128)S(1)} collective-permute-done((f32[64,512]{1,0:T(8,128)S(1)}, f32[64,512]{1,0:T(8,128)S(1)}, u32[]{:S(2)}, u32[]{:S(2)}) %collective-permute-start.11) | collective-permute-done | bytes 131104 | tf_op jit(solution)/shard_map/ppermute | solution.py:332
  58.1 0.7 %pad_maximum_fusion = bf16[64,1280]{1,0:T(8,128)(2,1)} fusion(bf16[64,128]{1,0:T(8,128)(2,1)S(1)} %fusion.2, bf16[64,512]{1,0:T(8,128)(2,1)S(1)} %fusion, bf16[64,128]{1,0:T(8,128)(2,1)S(1)} %fusion.3, bf16[64,512]{1,0:T(8,128)(2,1)S(1)} %fusion.1), kind=kLoop, calls=%fused_computation | loop fusion | flops 655360 | bytes 327680 | tf_op jit(solution)/shard_map/concatenate | solution.py:451
  58.8 0.7 %collective-permute-done.19 = f32[32,512]{1,0:T(8,128)S(1)} collective-permute-done((f32[32,512]{1,0:T(8,128)S(1)}, f32[32,512]{1,0:T(8,128)S(1)}, u32[]{:S(2)}, u32[]{:S(2)}) %collective-permute-start.19) | collective-permute-done | bytes 65568 | tf_op jit(solution)/shard_map/ppermute | solution.py:332
  59.5 0.6 %add.63 = f32[32,512]{1,0:T(8,128)} add(f32[32,512]{1,0:T(8,128)S(1)} %add.62, f32[32,512]{1,0:T(8,128)S(1)} %collective-permute-done.19) | non-fusion elementwise | flops 16384 | bytes 196608 | tf_op jit(solution)/shard_map/add | solution.py:416
  (34 shorter events, 0.3 us)
Async XLA Ops:
  9.0 17.0 %copy-start = (f32[512,384]{1,0:T(8,128)S(1)}, f32[512,384]{1,0:T(8,128)}, u32[]{:S(2)}) copy-start(f32[512,384]{1,0:T(8,128)} %get-tuple-element.30.refs_2_) | copy-start | bytes 2359300
  9.0 20.1 %copy-start.4 = (f32[256,128]{1,0:T(8,128)S(1)}, f32[256,128]{1,0:T(8,128)}, u32[]{:S(2)}) copy-start(f32[256,128]{1,0:T(8,128)} %get-tuple-element.36.keep_ref) | copy-start | bytes 393220
  9.0 5.5 %collective-permute-start.1 = (f32[32,512]{1,0:T(8,128)}, f32[32,512]{1,0:T(8,128)S(1)}, u32[]{:S(2)}, u32[]{:S(2)}) collective-permute-start(f32[32,512]{1,0:T(8,128)} %get-tuple-element.29), channel_id=1, source_target_pairs={{0,4},{4,0},{8,12},{12,8},{16,20},{20,16},{24,28},{28,24},{1,5},{5... | collective-permute-start | bytes 196616 | tf_op jit(solution)/shard_map/ppermute | solution.py:332
  14.5 16.8 %copy-start.3 = (f32[256,128]{1,0:T(8,128)S(1)}, f32[256,128]{1,0:T(8,128)}, u32[]{:S(2)}) copy-start(f32[256,128]{1,0:T(8,128)} %get-tuple-element.45.keep_ref) | copy-start | bytes 393220
  14.5 4.8 %collective-permute-start.2 = (f32[48,512]{1,0:T(8,128)S(1)}, f32[48,512]{1,0:T(8,128)S(1)}, u32[]{:S(2)}, u32[]{:S(2)}) collective-permute-start(f32[48,512]{1,0:T(8,128)S(1)} %pad_maximum_fusion.1), channel_id=1, source_target_pairs={{0,8},{4,12},{8,0},{12,4},{16,24},{20,28},{24,16},{28,20},{1,9},{5... | collective-permute-start | bytes 294920 | tf_op jit(solution)/shard_map/ppermute | solution.py:332
  16.7 17.7 %copy-start.2 = (f32[256,512]{1,0:T(8,128)S(1)}, f32[256,512]{1,0:T(8,128)}, u32[]{:S(2)}) copy-start(f32[256,512]{1,0:T(8,128)} %get-tuple-element.27.keep_ref) | copy-start | bytes 1572868
  16.7 15.1 %collective-permute-start = (f32[256,512]{1,0:T(8,128)}, f32[256,512]{1,0:T(8,128)S(1)}, u32[]{:S(2)}, u32[]{:S(2)}) collective-permute-start(f32[256,512]{1,0:T(8,128)} %get-tuple-element.28), channel_id=1, source_target_pairs={{0,4},{4,0},{8,12},{12,8},{16,20},{20,16},{24,28},{28,24},{1,5},{5... | collective-permute-start | bytes 1572872 | tf_op jit(solution)/shard_map/ppermute | solution.py:332
  19.3 6.6 %collective-permute-start.3 = (f32[32,512]{1,0:T(8,128)S(1)}, f32[32,512]{1,0:T(8,128)S(1)}, u32[]{:S(2)}, u32[]{:S(2)}) collective-permute-start(f32[32,512]{1,0:T(8,128)S(1)} %pad_maximum_fusion.3), channel_id=1, source_target_pairs={{0,16},{4,20},{8,24},{12,28},{16,0},{20,4},{24,8},{28,12},{1,17},{... | collective-permute-start | bytes 196616 | tf_op jit(solution)/shard_map/ppermute | solution.py:332
  22.4 19.0 %collective-permute-start.9 = (f32[256,512]{1,0:T(8,128)}, f32[256,512]{1,0:T(8,128)S(1)}, u32[]{:S(2)}, u32[]{:S(2)}) collective-permute-start(f32[256,512]{1,0:T(8,128)} %get-tuple-element.42), channel_id=1, source_target_pairs={{0,4},{4,0},{8,12},{12,8},{16,20},{20,16},{24,28},{28,24},{1,5},{5... | collective-permute-start | bytes 1572872 | tf_op jit(solution)/shard_map/ppermute | solution.py:332
  23.9 5.2 %collective-permute-start.4 = (f32[256,128]{1,0:T(8,128)}, f32[256,128]{1,0:T(8,128)S(1)}, u32[]{:S(2)}, u32[]{:S(2)}) collective-permute-start(f32[256,128]{1,0:T(8,128)} %get-tuple-element.34), channel_id=1, source_target_pairs={{0,8},{4,12},{8,0},{12,4},{16,24},{20,28},{24,16},{28,20},{1,9},{5... | collective-permute-start | bytes 393224 | tf_op jit(solution)/shard_map/ppermute | solution.py:332
  25.5 5.8 %collective-permute-start.12 = (f32[256,128]{1,0:T(8,128)}, f32[256,128]{1,0:T(8,128)S(1)}, u32[]{:S(2)}, u32[]{:S(2)}) collective-permute-start(f32[256,128]{1,0:T(8,128)} %get-tuple-element.46), channel_id=1, source_target_pairs={{0,8},{4,12},{8,0},{12,4},{16,24},{20,28},{24,16},{28,20},{1,9},{5... | collective-permute-start | bytes 393224 | tf_op jit(solution)/shard_map/ppermute | solution.py:332
  26.3 3.3 %collective-permute-start.15 = (f32[32,512]{1,0:T(8,128)S(1)}, f32[32,512]{1,0:T(8,128)S(1)}, u32[]{:S(2)}, u32[]{:S(2)}) collective-permute-start(f32[32,512]{1,0:T(8,128)S(1)} %get-tuple-element.50), channel_id=1, source_target_pairs={{0,1},{1,0},{2,3},{3,2},{4,5},{5,4},{6,7},{7,6},{8,9},{9,8},{10,11... | collective-permute-start | bytes 196616 | tf_op jit(solution)/shard_map/ppermute | solution.py:332
  29.1 12.3 %copy-start.1 = (f32[256,512]{1,0:T(8,128)S(1)}, f32[256,512]{1,0:T(8,128)}, u32[]{:S(2)}) copy-start(f32[256,512]{1,0:T(8,128)} %get-tuple-element.41.keep_ref) | copy-start | bytes 1572868
  29.2 6.8 %collective-permute-start.7 = (f32[128,128]{1,0:T(8,128)S(1)}, f32[128,128]{1,0:T(8,128)S(1)}, u32[]{:S(2)}, u32[]{:S(2)}) collective-permute-start(f32[128,128]{1,0:T(8,128)S(1)} %get-tuple-element.39), channel_id=1, source_target_pairs={{0,16},{4,20},{8,24},{12,28},{16,0},{20,4},{24,8},{28,12},{1,17},{... | collective-permute-start | bytes 196616 | tf_op jit(solution)/shard_map/ppermute | solution.py:332
  29.6 7.2 %collective-permute-start.16 = (f32[32,512]{1,0:T(8,128)S(1)}, f32[32,512]{1,0:T(8,128)S(1)}, u32[]{:S(2)}, u32[]{:S(2)}) collective-permute-start(f32[32,512]{1,0:T(8,128)S(1)} %add.59), channel_id=1, source_target_pairs={{0,2},{1,3},{2,0},{3,1},{4,6},{5,7},{6,4},{7,5},{8,10},{9,11},{10,... | collective-permute-start | bytes 196616 | tf_op jit(solution)/shard_map/ppermute | solution.py:332
  31.7 10.5 %collective-permute-start.13 = (f32[128,128]{1,0:T(8,128)S(1)}, f32[128,128]{1,0:T(8,128)S(1)}, u32[]{:S(2)}, u32[]{:S(2)}) collective-permute-start(f32[128,128]{1,0:T(8,128)S(1)} %get-tuple-element.49), channel_id=1, source_target_pairs={{0,16},{4,20},{8,24},{12,28},{16,0},{20,4},{24,8},{28,12},{1,17},{... | collective-permute-start | bytes 196616 | tf_op jit(solution)/shard_map/ppermute | solution.py:332
  34.7 9.2 %collective-permute-start.5 = (f32[128,512]{1,0:T(8,128)S(1)}, f32[128,512]{1,0:T(8,128)S(1)}, u32[]{:S(2)}, u32[]{:S(2)}) collective-permute-start(f32[128,512]{1,0:T(8,128)S(1)} %get-tuple-element.35), channel_id=1, source_target_pairs={{0,8},{4,12},{8,0},{12,4},{16,24},{20,28},{24,16},{28,20},{1,9},{5... | collective-permute-start | bytes 786440 | tf_op jit(solution)/shard_map/ppermute | solution.py:332
  36.1 7.8 %collective-permute-start.8 = (f32[64,128]{1,0:T(8,128)S(1)}, f32[64,128]{1,0:T(8,128)S(1)}, u32[]{:S(2)}, u32[]{:S(2)}) collective-permute-start(f32[64,128]{1,0:T(8,128)S(1)} %slice.96), channel_id=1, source_target_pairs={{0,4},{4,0},{8,12},{12,8},{16,20},{20,16},{24,28},{28,24},{1,5},{5... | collective-permute-start | bytes 98312 | tf_op jit(solution)/shard_map/ppermute | solution.py:332
  36.8 7.1 %collective-permute-start.17 = (f32[32,512]{1,0:T(8,128)S(1)}, f32[32,512]{1,0:T(8,128)S(1)}, u32[]{:S(2)}, u32[]{:S(2)}) collective-permute-start(f32[32,512]{1,0:T(8,128)S(1)} %add.60), channel_id=1, source_target_pairs={{0,4},{4,0},{8,12},{12,8},{16,20},{20,16},{24,28},{28,24},{1,5},{5... | collective-permute-start | bytes 196616 | tf_op jit(solution)/shard_map/ppermute | solution.py:332
  41.8 9.1 %collective-permute-start.10 = (f32[128,512]{1,0:T(8,128)S(1)}, f32[128,512]{1,0:T(8,128)S(1)}, u32[]{:S(2)}, u32[]{:S(2)}) collective-permute-start(f32[128,512]{1,0:T(8,128)S(1)} %get-tuple-element.44), channel_id=1, source_target_pairs={{0,8},{4,12},{8,0},{12,4},{16,24},{20,28},{24,16},{28,20},{1,9},{5... | collective-permute-start | bytes 786440 | tf_op jit(solution)/shard_map/ppermute | solution.py:332
  42.2 6.3 %collective-permute-start.14 = (f32[64,128]{1,0:T(8,128)S(1)}, f32[64,128]{1,0:T(8,128)S(1)}, u32[]{:S(2)}, u32[]{:S(2)}) collective-permute-start(f32[64,128]{1,0:T(8,128)S(1)} %slice.100), channel_id=1, source_target_pairs={{0,4},{4,0},{8,12},{12,8},{16,20},{20,16},{24,28},{28,24},{1,5},{5... | collective-permute-start | bytes 98312 | tf_op jit(solution)/shard_map/ppermute | solution.py:332
  43.9 9.5 %collective-permute-start.18 = (f32[32,512]{1,0:T(8,128)S(1)}, f32[32,512]{1,0:T(8,128)S(1)}, u32[]{:S(2)}, u32[]{:S(2)}) collective-permute-start(f32[32,512]{1,0:T(8,128)S(1)} %add.61), channel_id=1, source_target_pairs={{0,8},{4,12},{8,0},{12,4},{16,24},{20,28},{24,16},{28,20},{1,9},{5... | collective-permute-start | bytes 196616 | tf_op jit(solution)/shard_map/ppermute | solution.py:332
  45.8 8.2 %collective-permute-start.6 = (f32[64,512]{1,0:T(8,128)S(1)}, f32[64,512]{1,0:T(8,128)S(1)}, u32[]{:S(2)}, u32[]{:S(2)}) collective-permute-start(f32[64,512]{1,0:T(8,128)S(1)} %slice.94), channel_id=1, source_target_pairs={{0,16},{4,20},{8,24},{12,28},{16,0},{20,4},{24,8},{28,12},{1,17},{... | collective-permute-start | bytes 393224 | tf_op jit(solution)/shard_map/ppermute | solution.py:332
  50.9 7.2 %collective-permute-start.11 = (f32[64,512]{1,0:T(8,128)S(1)}, f32[64,512]{1,0:T(8,128)S(1)}, u32[]{:S(2)}, u32[]{:S(2)}) collective-permute-start(f32[64,512]{1,0:T(8,128)S(1)} %slice.98), channel_id=1, source_target_pairs={{0,16},{4,20},{8,24},{12,28},{16,0},{20,4},{24,8},{28,12},{1,17},{... | collective-permute-start | bytes 393224 | tf_op jit(solution)/shard_map/ppermute | solution.py:332
  53.4 6.0 %collective-permute-start.19 = (f32[32,512]{1,0:T(8,128)S(1)}, f32[32,512]{1,0:T(8,128)S(1)}, u32[]{:S(2)}, u32[]{:S(2)}) collective-permute-start(f32[32,512]{1,0:T(8,128)S(1)} %add.62), channel_id=1, source_target_pairs={{0,16},{4,20},{8,24},{12,28},{16,0},{20,4},{24,8},{28,12},{1,17},{... | collective-permute-start | bytes 196616 | tf_op jit(solution)/shard_map/ppermute | solution.py:332

commit v3 on v2

--- a/solution.py
+++ b/solution.py
@@ -18,16 +18,10 @@
 TILE = 128
 HALF_PI = (1.5706787109375, 1.1761486530303955e-4, 9.920935796805404e-10)
 
-CHUNKS = ((4, 0), (1, 1), (4, 0), (1, 1))
-TIES = {
-    "c0.2": ("c1.2",),
-    "m.2": ("c0.2",),
-    "c1.1": ("a.4",),
-    "m.1": ("h.2",),
-    "c3.4": ("c0.1",),
-}
-FENCES = ()
-MASS_ORDER = ("h.1", "h.2", "m.1", "m.2", "m.4")
+CHUNKS = ((4, 0), (4, 0), (2, 1))
+TIES = {"c1.1": ("a.2",), "c2.2": ("a.2",), "h.1": ("c0.1",)}
+FENCES = (("a.2",),)
+MASS_ORDER = ("h.1", "h.2", "m.1", "m.4", "m.2")
 
 
 def position(rel, order):
@@ -89,9 +83,16 @@
     k_copy = pltpu.make_async_copy(k_hbm, k_ref, kv_sems.at[0])
     v_copy = pltpu.make_async_copy(v_hbm, v_ref, kv_sems.at[1])
     k_copy.start()
-    q_copy = pltpu.make_async_copy(q_hbm, q_ref, kv_sems.at[2])
-    q_copy.start()
+    q_copies = []
+    for g in range(kv_count):
+        lanes = pl.ds(g * group_size * HD, group_size * HD)
+        q_copies.append(
+            pltpu.make_async_copy(q_hbm.at[:, lanes], q_ref.at[:, lanes], kv_sems.at[2 + g])
+        )
+    q_copies[0].start()
     v_copy.start()
+    for copy in q_copies[1:]:
+        copy.start()
 
     rope_tables(pos_ref, frequency_ref, cos_ref, sin_ref)
     lane = lax.broadcasted_iota(jnp.int32, columns.shape, 1)
@@ -116,12 +117,13 @@
         for slot in range(slots):
             values[g, slot, :, :HD] = v_ref[:, g * HD : (g + 1) * HD]
     k_copy.wait()
-    q_copy.wait()
 
     tile = min(TILE, query_count)
     half_copies, mass_copies = [], []
     for j in range(head_count):
         g = j // group_size
+        if j % group_size == 0:
+            q_copies[g].wait()
         lanes = slice(j // slots * width, (j // slots + 1) * width)
         for t in range(query_count // tile):
             rows = slice(t * tile, (t + 1) * tile)
@@ -208,7 +210,7 @@
             pltpu.VMEM((head_count, 2, half, HD), jnp.float32),
             pltpu.VMEM(mass.shape, jnp.float32),
             pltpu.VMEM((query_count, HD), jnp.float32),
-            pltpu.SemaphoreType.DMA((3,)),
+            pltpu.SemaphoreType.DMA((2 + head_count // group_size,)),
             pltpu.SemaphoreType.DMA((head_count, 2)),
             pltpu.SemaphoreType.DMA((groups,)),
         ],
@@ -297,6 +299,35 @@
     )(keep, got, weights)
 
 
+def finish_kernel(count, *refs):
+    mass_ref, mass_got_ref, attended_ref, out_ref = refs[2 * count :]
+    at = 0
+    for total_ref, got_ref in zip(refs[:count], refs[count : 2 * count]):
+        columns = slice(at, at + total_ref.shape[1])
+        attended_ref[:, columns] = (total_ref[...] + got_ref[...]).astype(attended_ref.dtype)
+        at += total_ref.shape[1]
+    out_ref[...] = mass_ref[...] + mass_got_ref[...]
+
+
+def finish(totals, blocks, mass, mass_got):
+    rows = totals[0].shape[0]
+    columns = sum(total.shape[1] for total in totals)
+    vmem = pl.BlockSpec(memory_space=pltpu.VMEM)
+    return pl.pallas_call(
+        functools.partial(finish_kernel, len(totals)),
+        in_specs=[vmem] * (2 * len(totals) + 2),
+        out_specs=[vmem] * 2,
+        out_shape=[
+            jax.ShapeDtypeStruct((rows, columns), jnp.bfloat16),
+            jax.ShapeDtypeStruct(mass.shape, jnp.float32),
+        ],
+        compiler_params=pltpu.CompilerParams(vmem_limit_bytes=VMEM_LIMIT),
+        cost_estimate=pl.CostEstimate(
+            flops=rows * columns, bytes_accessed=10 * rows * columns, transcendentals=0
+        ),
+    )(*totals, *blocks, mass, mass_got)
+
+
 def in_log2(stats):
     return jnp.concatenate([stats[:STAT_ROWS] * LOG2_SCALE, stats[STAT_ROWS:]], axis=0)
 
@@ -331,13 +362,20 @@
     def exchange(array, axis, bit):
         return lax.ppermute(array, axis, [(i, i ^ bit) for i in range(lax.axis_size(axis))])
 
+    def fenced(name, array, axis, bit):
+        if (name,) not in FENCES:
+            return exchange(array, axis, bit)
+        return lax.cond(
+            stretch_lengths[0] > 0, lambda sent: exchange(sent, axis, bit), jnp.zeros_like, array
+        )
+
     def after(names, arrays):
         waits = [arrived(other) for name in names for other in TIES.get(name, ()) if known(other)]
         return lax.optimization_barrier((*arrays, *waits))[: len(arrays)] if waits else arrays
 
     def run(names, step, state):
         state = tuple(after(names, state))
-        if names not in FENCES:
+        if len(names) == 1:
             return step(names[0], *state)
 
         def steps(*state):
@@ -383,7 +421,7 @@
         return int(bit) in bits
 
     stat_steps = ["a.%d" % bit for bit in bits]
-    stat_runs, mass_runs = runs(stat_steps), runs(mass_steps)
+    stat_runs, mass_runs = runs(stat_steps), runs(mass_steps[:-1]) + [(mass_steps[-1],)]
     run_of = {name: i for names in (stat_runs, mass_runs) for i, run_ in enumerate(names) for name in run_}
 
     @once
@@ -404,7 +442,7 @@
         message = raw_stats if opening else joined
         if bit in firsts and not opening:
             message = jnp.concatenate([message, own[:STAT_ROWS]], axis=0)
-        got = exchange(message, "ctx", bit)
+        got = fenced(name, message, "ctx", bit)
         joined = join_stats(joined, in_log2(got) if opening else got[: 2 * STAT_ROWS])
         if bit in firsts:
             top = got[:STAT_ROWS] * LOG2_SCALE if opening else got[2 * STAT_ROWS :]
@@ -413,7 +451,7 @@
 
     def mass_step(name, total):
         kind, bit = name.split(".")
-        return (total + exchange(total, "head" if kind == "h" else "ctx", int(bit)),)
+        return (total + fenced(name, total, "head" if kind == "h" else "ctx", int(bit)),)
 
     @once
     def stats(step):
@@ -442,13 +480,16 @@
             kind = orders[order]
             return merge(first_head, kind, keeps[n], got, weighed()[1 + kind])
         total = halved(n, i - 1)[0] + got
-        if i == len(order):
-            return total
         rows = total.shape[0] // 2
         return total[:rows], total[rows:]
 
-    done = [halved(n, len(bits)).astype(jnp.bfloat16) for n in range(len(parts))]
-    return jnp.concatenate(done, axis=1), mass(len(mass_runs))[0]
+    last = len(bits) - 1
+    totals = [halved(n, last)[0] for n in range(len(parts))]
+    blocks = [arrived("c%d.%d" % (n, order[last])) for n, (order, _) in enumerate(parts)]
+    name = mass_steps[-1]
+    (before,) = mass(len(mass_runs) - 1)
+    got = exchange(after([name], (before,))[0], "head" if name[0] == "h" else "ctx", int(name[2:]))
+    return tuple(finish(totals, blocks, before, got))
 
 
 def solution(mesh):

time: 60.4 us -> 59.1 us (0.978)
  starting transfers between devices: 31.2 us -> 25.8 us
  waiting for transfers between devices: 15.9 us -> 19.6 us
  other arithmetic: 2.41 us -> 1.01 us
  Pallas kernels: 9.68 us -> 10.6 us
  local copies, waits for them, and re-layouts: 0.05 us -> 0.87 us
    ppermute x20 -> x17, starting transfers between devices: 31.2 us -> 25.8 us  [exchange(): lax.ppermute(array, axis, [(i, i ^ bit) for i in range(lax.axis_size(axis...]
    ppermute x20 -> x17, waiting for transfers between devices: 15.9 us -> 19.6 us  [exchange(): lax.ppermute(array, axis, [(i, i ^ bit) for i in range(lax.axis_size(axis...]
    slice x0 -> x1, local copies, waits for them, and re-layouts: none -> 0.8 us  [join_stats(): top = jnp.maximum(one[:STAT_ROWS], two[:STAT_ROWS])]
    pallas_call x0 -> x1, Pallas kernels: none -> 0.72 us  [finish(): pl.pallas_call(functools.partial(finish_kernel, len(totals)), in_specs=[v...]
    concatenate x1 -> x0, other arithmetic: 0.68 us -> none  [local(): return (jnp.concatenate(done, axis=1), mass(len(mass_runs))[0])]
    add x5 -> x4, other arithmetic: 0.68 us -> 0.04 us  [mass_step(): total + fenced(name, total, 'head' if kind == 'h' else 'ctx', int(bit))]
  transfers between devices with their start and end apart: 20 -> 17, of which waited for: 8 -> 10; matrix products, arithmetic and copies ran while one was open for 3% -> 3% of each run, Pallas kernels for 2% -> 2%
where the time goes in v3:
time: 59.1 us; the launch traced here: 58.8 us
  starting transfers between devices  25.8 us (44%)
  waiting for transfers between devices  19.6 us (33%)
  Pallas kernels  10.6 us (18%)
  other arithmetic  1.01 us (2%)
  between operations  0.89 us (2%)
  local copies, waits for them, and re-layouts  0.87 us (1%)
    ppermute x17, starting transfers between devices, exchange(): lax.ppermute(array, axis, [(i, i ^ bit) for i in range(lax.axis_size(axis...  25.8 us
    ppermute x17, waiting for transfers between devices, exchange(): lax.ppermute(array, axis, [(i, i ^ bit) for i in range(lax.axis_size(axis...  19.6 us
    pallas_call x1, Pallas kernels, flash(): pl.pallas_call(functools.partial(flash_kernel, parts, group_size, slots),...  8.6 us
  transfers between devices with their start and end apart: 17, of which 10 were waited for; matrix products, arithmetic and copies ran while one was open for 3% of the time, Pallas kernels for 2%

profile of v3, /device:TPU:0, one launch (start us, length us, event | category | flops | bytes accessed | tf_op | source)
XLA Modules:
  0.0 58.8 jit_solution(16040331647595114223)
XLA Ops:
  0.6 0.0 copy-start.5
  0.6 8.6 %shard_map.77 = (f32[256,512]{1,0:T(8,128)}, f32[256,512]{1,0:T(8,128)}, f32[256,256]{1,0:T(8,128)}, f32[256,512]{1,0:T(8,128)}, f32[256,512]{1,0:T(8,128)}, /*i...) custom-call(s32[32]{0:T(128)} %lens_ref.1, s32[4,128]{1,0:T(4,128)} %bitcast.3, ...), custom_call_target="tpu_custom_call" | custom-call | flops 1342177280 | bytes 2621440 | tf_op jit(solution)/shard_map/pallas_call | solution.py:197
  9.2 0.0 copy-start.4
  9.3 0.0 copy-start
  9.3 3.0 %collective-permute-start.2 = (f32[32,512]{1,0:T(8,128)}, f32[32,512]{1,0:T(8,128)S(1)}, u32[]{:S(2)}, u32[]{:S(2)}) collective-permute-start(f32[32,512]{1,0:T(8,128)} %get-tuple-element.32), channel_id=1, source_target_pairs={{0,4},{4,0},{8,12},{12,8},{16,20},{20,16},{24,28},{28,24},{1,5},{5... | collective-permute-start | bytes 196616 | tf_op jit(solution)/shard_map/ppermute | solution.py:363
  12.3 0.1 collective-permute-start.1
  12.3 0.8 %slice_multiply_fusion.4 = (f32[16,512]{1,0:T(8,128)S(1)}, f32[16,512]{1,0:T(8,128)S(1)}) fusion(f32[32,512]{1,0:T(8,128)} %get-tuple-element.32), kind=kLoop, calls=%fused_computation.11 | loop fusion | flops 8192 | bytes 131072 | tf_op jit(solution)/shard_map/mul | solution.py:332
  13.2 1.9 %collective-permute-done.2 = f32[32,512]{1,0:T(8,128)S(1)} collective-permute-done((f32[32,512]{1,0:T(8,128)}, f32[32,512]{1,0:T(8,128)S(1)}, u32[]{:S(2)}, u32[]{:S(2)}) %collective-permute-start.2) | collective-permute-done | bytes 65568 | tf_op jit(solution)/shard_map/ppermute | solution.py:363
  15.1 6.0 %conditional.1 = (f32[48,512]{1,0:T(8,128)}, f32[16,512]{1,0:T(8,128)S(1)}, f32[16,512]{1,0:T(8,128)S(1)}, f32[16,512]{1,0:T(8,128)S(1)}) conditional(s32[]{:T(128)} %bitcast.1, () %tuple.20, f32[48,512]{1,0:T(8,128)S(1)} %pad_maximum_fusion), branch_computations={%region_0.0_spmd, %region_1.0_spmd} | conditional | bytes 589896 | solution.py:368
  15.2 2.4 %collective-permute-start = (f32[48,512]{1,0:T(8,128)S(1)}, f32[48,512]{1,0:T(8,128)}, u32[]{:S(2)}, u32[]{:S(2)}) collective-permute-start(f32[48,512]{1,0:T(8,128)S(1)} %param.1), channel_id=1, source_target_pairs={{0,8},{4,12},{8,0},{12,4},{16,24},{20,28},{24,16},{28,20},{1,9},{5... | collective-permute-start | bytes 294920 | tf_op jit(solution)/shard_map/cond/branch_1_fun/ppermute | solution.py:363
  17.6 2.7 %collective-permute-done = f32[48,512]{1,0:T(8,128)} collective-permute-done((f32[48,512]{1,0:T(8,128)S(1)}, f32[48,512]{1,0:T(8,128)}, u32[]{:S(2)}, u32[]{:S(2)}) %collective-permute-start) | collective-permute-done | bytes 98336 | tf_op jit(solution)/shard_map/cond/branch_1_fun/ppermute | solution.py:363
  20.3 0.8 %fusion.2 = (f32[16,512]{1,0:T(8,128)S(1)}, f32[16,512]{1,0:T(8,128)S(1)}, f32[16,512]{1,0:T(8,128)S(1)}) fusion(f32[48,512]{1,0:T(8,128)} %collective-permute-done), kind=kLoop, calls=%fused_computation.14 | loop fusion | bytes 196608 | tf_op jit(solution)/shard_map/slice | solution.py:336
  21.1 3.1 %collective-permute-start.3 = (f32[32,512]{1,0:T(8,128)S(1)}, f32[32,512]{1,0:T(8,128)S(1)}, u32[]{:S(2)}, u32[]{:S(2)}) collective-permute-start(f32[32,512]{1,0:T(8,128)S(1)} %pad_maximum_fusion.2), channel_id=1, source_target_pairs={{0,16},{4,20},{8,24},{12,28},{16,0},{20,4},{24,8},{28,12},{1,17},{... | collective-permute-start | bytes 196616 | tf_op jit(solution)/shard_map/ppermute | solution.py:363
  24.2 1.6 %collective-permute-start.7 = (f32[256,256]{1,0:T(8,128)}, f32[256,256]{1,0:T(8,128)S(1)}, u32[]{:S(2)}, u32[]{:S(2)}) collective-permute-start(f32[256,256]{1,0:T(8,128)} %get-tuple-element.47), channel_id=1, source_target_pairs={{0,8},{4,12},{8,0},{12,4},{16,24},{20,28},{24,16},{28,20},{1,9},{5... | collective-permute-start | bytes 786440 | tf_op jit(solution)/shard_map/ppermute | solution.py:363
  25.8 1.6 %collective-permute-start.5 = (f32[256,512]{1,0:T(8,128)S(1)}, f32[256,512]{1,0:T(8,128)S(1)}, u32[]{:S(2)}, u32[]{:S(2)}) collective-permute-start(f32[256,512]{1,0:T(8,128)S(1)} %copy-done.4), channel_id=1, source_target_pairs={{0,4},{4,0},{8,12},{12,8},{16,20},{20,16},{24,28},{28,24},{1,5},{5... | collective-permute-start | bytes 1572872 | tf_op jit(solution)/shard_map/ppermute | solution.py:363
  27.4 0.0 collective-permute-done.3
  27.5 0.4 shard_map.78
  27.8 0.0 copy-start.1
  27.8 0.0 collective-permute-done.1.got_ref
  27.9 0.4 shard_map.79
  28.2 1.1 %collective-permute-start.4 = (f32[128,512]{1,0:T(8,128)S(1)}, f32[128,512]{1,0:T(8,128)S(1)}, u32[]{:S(2)}, u32[]{:S(2)}) collective-permute-start(f32[128,512]{1,0:T(8,128)S(1)} %get-tuple-element.39), channel_id=1, source_target_pairs={{0,8},{4,12},{8,0},{12,4},{16,24},{20,28},{24,16},{28,20},{1,9},{5... | collective-permute-start | bytes 786440 | tf_op jit(solution)/shard_map/ppermute | solution.py:363
  29.3 0.0 collective-permute-start.12
  29.3 3.7 %collective-permute-done.7.got_ref = f32[256,256]{1,0:T(8,128)S(1)} collective-permute-done((f32[256,256]{1,0:T(8,128)}, f32[256,256]{1,0:T(8,128)S(1)}, u32[]{:S(2)}, u32[]{:S(2)}) %collective-permute-start.7) | collective-permute-done | bytes 262176 | tf_op jit(solution)/shard_map/ppermute | solution.py:363
  33.1 0.0 copy-done.3
  33.1 0.2 shard_map.81
  33.3 0.1 collective-permute-start.8
  33.4 0.0 collective-permute-done.12
  33.4 1.4 %collective-permute-start.13 = (f32[32,512]{1,0:T(8,128)S(1)}, f32[32,512]{1,0:T(8,128)S(1)}, u32[]{:S(2)}, u32[]{:S(2)}) collective-permute-start(f32[32,512]{1,0:T(8,128)S(1)} %add.36), channel_id=1, source_target_pairs={{0,2},{1,3},{2,0},{3,1},{4,6},{5,7},{6,4},{7,5},{8,10},{9,11},{10,... | collective-permute-start | bytes 196616 | tf_op jit(solution)/shard_map/ppermute | solution.py:363
  34.8 2.9 %collective-permute-done.13 = f32[32,512]{1,0:T(8,128)S(1)} collective-permute-done((f32[32,512]{1,0:T(8,128)S(1)}, f32[32,512]{1,0:T(8,128)S(1)}, u32[]{:S(2)}, u32[]{:S(2)}) %collective-permute-start.13) | collective-permute-done | bytes 65568 | tf_op jit(solution)/shard_map/ppermute | solution.py:363
  37.7 2.2 %collective-permute-start.14 = (f32[32,512]{1,0:T(8,128)S(1)}, f32[32,512]{1,0:T(8,128)S(1)}, u32[]{:S(2)}, u32[]{:S(2)}) collective-permute-start(f32[32,512]{1,0:T(8,128)S(1)} %add.37), channel_id=1, source_target_pairs={{0,4},{4,0},{8,12},{12,8},{16,20},{20,16},{24,28},{28,24},{1,5},{5... | collective-permute-start | bytes 196616 | tf_op jit(solution)/shard_map/ppermute | solution.py:363
  39.9 0.0 collective-permute-done.5.got_ref
  39.9 0.4 shard_map.80
  40.3 1.6 %collective-permute-start.6 = (f32[128,512]{1,0:T(8,128)S(1)}, f32[128,512]{1,0:T(8,128)S(1)}, u32[]{:S(2)}, u32[]{:S(2)}) collective-permute-start(f32[128,512]{1,0:T(8,128)S(1)} %get-tuple-element.44), channel_id=1, source_target_pairs={{0,8},{4,12},{8,0},{12,4},{16,24},{20,28},{24,16},{28,20},{1,9},{5... | collective-permute-start | bytes 786440 | tf_op jit(solution)/shard_map/ppermute | solution.py:363
  41.9 0.0 collective-permute-done.8
  41.9 0.2 collective-permute-done.14
  42.2 3.0 %collective-permute-start.15 = (f32[32,512]{1,0:T(8,128)S(1)}, f32[32,512]{1,0:T(8,128)S(1)}, u32[]{:S(2)}, u32[]{:S(2)}) collective-permute-start(f32[32,512]{1,0:T(8,128)S(1)} %add.38), channel_id=1, source_target_pairs={{0,16},{4,20},{8,24},{12,28},{16,0},{20,4},{24,8},{28,12},{1,17},{... | collective-permute-start | bytes 196616 | tf_op jit(solution)/shard_map/ppermute | solution.py:363
  45.1 0.0 collective-permute-done.4
  45.2 0.1 collective-permute-start.9
  45.3 4.1 %collective-permute-done.6 = f32[128,512]{1,0:T(8,128)S(1)} collective-permute-done((f32[128,512]{1,0:T(8,128)S(1)}, f32[128,512]{1,0:T(8,128)S(1)}, u32[]{:S(2)}, u32[]{:S(2)}) %collective-permute-start.6) | collective-permute-done | bytes 262176 | tf_op jit(solution)/shard_map/ppermute | solution.py:363
  49.4 2.4 %collective-permute-start.10 = (f32[64,512]{1,0:T(8,128)S(1)}, f32[64,512]{1,0:T(8,128)S(1)}, u32[]{:S(2)}, u32[]{:S(2)}) collective-permute-start(f32[64,512]{1,0:T(8,128)S(1)} %get-tuple-element.60), channel_id=1, source_target_pairs={{0,16},{4,20},{8,24},{12,28},{16,0},{20,4},{24,8},{28,12},{1,17},{... | collective-permute-start | bytes 393224 | tf_op jit(solution)/shard_map/ppermute | solution.py:363
  51.9 0.2 collective-permute-start.11
  52.1 0.0 collective-permute-done.15
  52.1 1.9 %collective-permute-start.16 = (f32[32,512]{1,0:T(8,128)S(1)}, f32[32,512]{1,0:T(8,128)S(1)}, u32[]{:S(2)}, u32[]{:S(2)}) collective-permute-start(f32[32,512]{1,0:T(8,128)S(1)} %add.39.refs_6_), channel_id=1, source_target_pairs={{0,8},{4,12},{8,0},{12,4},{16,24},{20,28},{24,16},{28,20},{1,9},{5... | collective-permute-start | bytes 196616 | tf_op jit(solution)/shard_map/ppermute | solution.py:363
  54.0 2.2 %collective-permute-done.11.refs_5_ = f32[64,256]{1,0:T(8,128)S(1)} collective-permute-done((f32[64,256]{1,0:T(8,128)S(1)}, f32[64,256]{1,0:T(8,128)S(1)}, u32[]{:S(2)}, u32[]{:S(2)}) %collective-permute-start.11) | collective-permute-done | bytes 65568 | tf_op jit(solution)/shard_map/ppermute | solution.py:363
  56.2 0.2 collective-permute-done.16.refs_7_
  56.4 0.3 collective-permute-done.9.refs_3_
  56.7 1.4 %collective-permute-done.10.refs_4_ = f32[64,512]{1,0:T(8,128)S(1)} collective-permute-done((f32[64,512]{1,0:T(8,128)S(1)}, f32[64,512]{1,0:T(8,128)S(1)}, u32[]{:S(2)}, u32[]{:S(2)}) %collective-permute-start.10) | collective-permute-done | bytes 131104 | tf_op jit(solution)/shard_map/ppermute | solution.py:363
  58.1 0.7 %shard_map.82 = (bf16[64,1280]{1,0:T(8,128)(2,1)}, f32[32,512]{1,0:T(8,128)}) custom-call(f32[64,512]{1,0:T(8,128)S(1)} %get-tuple-element.63.refs_0_, f32[64,512]{1,0:T(8,128)S(1)} %get-tuple-element.61.refs_1_, f32[64,256]{1,0:T(8,128)S(1)} %get-tuple-element.65.refs_2_, f32[64,512]{1,0:T(8,128)S(1)} %collective-permute-done.9.refs_3_, ...), custom_call_target="tpu_custom_call" | custom-call | flops 81920 | bytes 819200 | tf_op jit(solution)/shard_map/pallas_call | solution.py:316
  (24 shorter events, 0.3 us)
Async XLA Ops:
  0.6 12.5 %copy-start.5 = (s32[32]{0:T(128)S(1)}, s32[32]{0:T(128)}, u32[]{:S(2)}) copy-start(s32[32]{0:T(128)} %lens_ref.1) | copy-start | bytes 388
  9.2 16.6 %copy-start.4 = (f32[256,512]{1,0:T(8,128)S(1)}, f32[256,512]{1,0:T(8,128)}, u32[]{:S(2)}) copy-start(f32[256,512]{1,0:T(8,128)} %get-tuple-element.42) | copy-start | bytes 1572868
  9.3 18.2 %copy-start = (f32[512,384]{1,0:T(8,128)S(1)}, f32[512,384]{1,0:T(8,128)}, u32[]{:S(2)}) copy-start(f32[512,384]{1,0:T(8,128)} %get-tuple-element.36.refs_2_) | copy-start | bytes 2359300
  9.3 5.8 %collective-permute-start.2 = (f32[32,512]{1,0:T(8,128)}, f32[32,512]{1,0:T(8,128)S(1)}, u32[]{:S(2)}, u32[]{:S(2)}) collective-permute-start(f32[32,512]{1,0:T(8,128)} %get-tuple-element.32), channel_id=1, source_target_pairs={{0,4},{4,0},{8,12},{12,8},{16,20},{20,16},{24,28},{28,24},{1,5},{5... | collective-permute-start | bytes 196616 | tf_op jit(solution)/shard_map/ppermute | solution.py:363
  12.3 15.6 %collective-permute-start.1 = (f32[256,512]{1,0:T(8,128)}, f32[256,512]{1,0:T(8,128)S(1)}, u32[]{:S(2)}, u32[]{:S(2)}) collective-permute-start(f32[256,512]{1,0:T(8,128)} %get-tuple-element.31), channel_id=1, source_target_pairs={{0,4},{4,0},{8,12},{12,8},{16,20},{20,16},{24,28},{28,24},{1,5},{5... | collective-permute-start | bytes 1572872 | tf_op jit(solution)/shard_map/ppermute | solution.py:363
  13.2 14.7 %copy-start.2 = (f32[256,512]{1,0:T(8,128)S(1)}, f32[256,512]{1,0:T(8,128)}, u32[]{:S(2)}) copy-start(f32[256,512]{1,0:T(8,128)} %get-tuple-element.30.keep_ref) | copy-start | bytes 1572868
  15.2 5.1 %collective-permute-start = (f32[48,512]{1,0:T(8,128)S(1)}, f32[48,512]{1,0:T(8,128)}, u32[]{:S(2)}, u32[]{:S(2)}) collective-permute-start(f32[48,512]{1,0:T(8,128)S(1)} %param.1), channel_id=1, source_target_pairs={{0,8},{4,12},{8,0},{12,4},{16,24},{20,28},{24,16},{28,20},{1,9},{5... | collective-permute-start | bytes 294920 | tf_op jit(solution)/shard_map/cond/branch_1_fun/ppermute | solution.py:363
  21.1 11.9 %copy-start.3 = (f32[256,256]{1,0:T(8,128)S(1)}, f32[256,256]{1,0:T(8,128)}, u32[]{:S(2)}) copy-start(f32[256,256]{1,0:T(8,128)} %get-tuple-element.45.keep_ref) | copy-start | bytes 786436
  21.1 6.3 %collective-permute-start.3 = (f32[32,512]{1,0:T(8,128)S(1)}, f32[32,512]{1,0:T(8,128)S(1)}, u32[]{:S(2)}, u32[]{:S(2)}) collective-permute-start(f32[32,512]{1,0:T(8,128)S(1)} %pad_maximum_fusion.2), channel_id=1, source_target_pairs={{0,16},{4,20},{8,24},{12,28},{16,0},{20,4},{24,8},{28,12},{1,17},{... | collective-permute-start | bytes 196616 | tf_op jit(solution)/shard_map/ppermute | solution.py:363
  24.2 8.8 %collective-permute-start.7 = (f32[256,256]{1,0:T(8,128)}, f32[256,256]{1,0:T(8,128)S(1)}, u32[]{:S(2)}, u32[]{:S(2)}) collective-permute-start(f32[256,256]{1,0:T(8,128)} %get-tuple-element.47), channel_id=1, source_target_pairs={{0,8},{4,12},{8,0},{12,4},{16,24},{20,28},{24,16},{28,20},{1,9},{5... | collective-permute-start | bytes 786440 | tf_op jit(solution)/shard_map/ppermute | solution.py:363
  25.8 14.1 %collective-permute-start.5 = (f32[256,512]{1,0:T(8,128)S(1)}, f32[256,512]{1,0:T(8,128)S(1)}, u32[]{:S(2)}, u32[]{:S(2)}) collective-permute-start(f32[256,512]{1,0:T(8,128)S(1)} %copy-done.4), channel_id=1, source_target_pairs={{0,4},{4,0},{8,12},{12,8},{16,20},{20,16},{24,28},{28,24},{1,5},{5... | collective-permute-start | bytes 1572872 | tf_op jit(solution)/shard_map/ppermute | solution.py:363
  27.8 12.1 %copy-start.1 = (f32[256,512]{1,0:T(8,128)S(1)}, f32[256,512]{1,0:T(8,128)}, u32[]{:S(2)}) copy-start(f32[256,512]{1,0:T(8,128)} %get-tuple-element.40.keep_ref) | copy-start | bytes 1572868
  28.2 16.9 %collective-permute-start.4 = (f32[128,512]{1,0:T(8,128)S(1)}, f32[128,512]{1,0:T(8,128)S(1)}, u32[]{:S(2)}, u32[]{:S(2)}) collective-permute-start(f32[128,512]{1,0:T(8,128)S(1)} %get-tuple-element.39), channel_id=1, source_target_pairs={{0,8},{4,12},{8,0},{12,4},{16,24},{20,28},{24,16},{28,20},{1,9},{5... | collective-permute-start | bytes 786440 | tf_op jit(solution)/shard_map/ppermute | solution.py:363
  29.3 4.0 %collective-permute-start.12 = (f32[32,512]{1,0:T(8,128)S(1)}, f32[32,512]{1,0:T(8,128)S(1)}, u32[]{:S(2)}, u32[]{:S(2)}) collective-permute-start(f32[32,512]{1,0:T(8,128)S(1)} %get-tuple-element.52), channel_id=1, source_target_pairs={{0,1},{1,0},{2,3},{3,2},{4,5},{5,4},{6,7},{7,6},{8,9},{9,8},{10,11... | collective-permute-start | bytes 196616 | tf_op jit(solution)/shard_map/ppermute | solution.py:363
  33.3 8.6 %collective-permute-start.8 = (f32[128,256]{1,0:T(8,128)S(1)}, f32[128,256]{1,0:T(8,128)S(1)}, u32[]{:S(2)}, u32[]{:S(2)}) collective-permute-start(f32[128,256]{1,0:T(8,128)S(1)} %get-tuple-element.50), channel_id=1, source_target_pairs={{0,16},{4,20},{8,24},{12,28},{16,0},{20,4},{24,8},{28,12},{1,17},{... | collective-permute-start | bytes 393224 | tf_op jit(solution)/shard_map/ppermute | solution.py:363
  33.4 4.3 %collective-permute-start.13 = (f32[32,512]{1,0:T(8,128)S(1)}, f32[32,512]{1,0:T(8,128)S(1)}, u32[]{:S(2)}, u32[]{:S(2)}) collective-permute-start(f32[32,512]{1,0:T(8,128)S(1)} %add.36), channel_id=1, source_target_pairs={{0,2},{1,3},{2,0},{3,1},{4,6},{5,7},{6,4},{7,5},{8,10},{9,11},{10,... | collective-permute-start | bytes 196616 | tf_op jit(solution)/shard_map/ppermute | solution.py:363
  37.7 4.4 %collective-permute-start.14 = (f32[32,512]{1,0:T(8,128)S(1)}, f32[32,512]{1,0:T(8,128)S(1)}, u32[]{:S(2)}, u32[]{:S(2)}) collective-permute-start(f32[32,512]{1,0:T(8,128)S(1)} %add.37), channel_id=1, source_target_pairs={{0,4},{4,0},{8,12},{12,8},{16,20},{20,16},{24,28},{28,24},{1,5},{5... | collective-permute-start | bytes 196616 | tf_op jit(solution)/shard_map/ppermute | solution.py:363
  40.3 9.1 %collective-permute-start.6 = (f32[128,512]{1,0:T(8,128)S(1)}, f32[128,512]{1,0:T(8,128)S(1)}, u32[]{:S(2)}, u32[]{:S(2)}) collective-permute-start(f32[128,512]{1,0:T(8,128)S(1)} %get-tuple-element.44), channel_id=1, source_target_pairs={{0,8},{4,12},{8,0},{12,4},{16,24},{20,28},{24,16},{28,20},{1,9},{5... | collective-permute-start | bytes 786440 | tf_op jit(solution)/shard_map/ppermute | solution.py:363
  42.2 9.9 %collective-permute-start.15 = (f32[32,512]{1,0:T(8,128)S(1)}, f32[32,512]{1,0:T(8,128)S(1)}, u32[]{:S(2)}, u32[]{:S(2)}) collective-permute-start(f32[32,512]{1,0:T(8,128)S(1)} %add.38), channel_id=1, source_target_pairs={{0,16},{4,20},{8,24},{12,28},{16,0},{20,4},{24,8},{28,12},{1,17},{... | collective-permute-start | bytes 196616 | tf_op jit(solution)/shard_map/ppermute | solution.py:363
  45.2 11.5 %collective-permute-start.9 = (f32[64,512]{1,0:T(8,128)S(1)}, f32[64,512]{1,0:T(8,128)S(1)}, u32[]{:S(2)}, u32[]{:S(2)}) collective-permute-start(f32[64,512]{1,0:T(8,128)S(1)} %get-tuple-element.62), channel_id=1, source_target_pairs={{0,16},{4,20},{8,24},{12,28},{16,0},{20,4},{24,8},{28,12},{1,17},{... | collective-permute-start | bytes 393224 | tf_op jit(solution)/shard_map/ppermute | solution.py:363
  49.4 8.7 %collective-permute-start.10 = (f32[64,512]{1,0:T(8,128)S(1)}, f32[64,512]{1,0:T(8,128)S(1)}, u32[]{:S(2)}, u32[]{:S(2)}) collective-permute-start(f32[64,512]{1,0:T(8,128)S(1)} %get-tuple-element.60), channel_id=1, source_target_pairs={{0,16},{4,20},{8,24},{12,28},{16,0},{20,4},{24,8},{28,12},{1,17},{... | collective-permute-start | bytes 393224 | tf_op jit(solution)/shard_map/ppermute | solution.py:363
  51.9 4.3 %collective-permute-start.11 = (f32[64,256]{1,0:T(8,128)S(1)}, f32[64,256]{1,0:T(8,128)S(1)}, u32[]{:S(2)}, u32[]{:S(2)}) collective-permute-start(f32[64,256]{1,0:T(8,128)S(1)} %get-tuple-element.64), channel_id=1, source_target_pairs={{0,4},{4,0},{8,12},{12,8},{16,20},{20,16},{24,28},{28,24},{1,5},{5... | collective-permute-start | bytes 196616 | tf_op jit(solution)/shard_map/ppermute | solution.py:363
  52.1 4.3 %collective-permute-start.16 = (f32[32,512]{1,0:T(8,128)S(1)}, f32[32,512]{1,0:T(8,128)S(1)}, u32[]{:S(2)}, u32[]{:S(2)}) collective-permute-start(f32[32,512]{1,0:T(8,128)S(1)} %add.39.refs_6_), channel_id=1, source_target_pairs={{0,8},{4,12},{8,0},{12,4},{16,24},{20,28},{24,16},{28,20},{1,9},{5... | collective-permute-start | bytes 196616 | tf_op jit(solution)/shard_map/ppermute | solution.py:363

commit v4 on v3

--- a/solution.py
+++ b/solution.py
@@ -117,13 +117,13 @@
         for slot in range(slots):
             values[g, slot, :, :HD] = v_ref[:, g * HD : (g + 1) * HD]
     k_copy.wait()
+    for copy in q_copies:
+        copy.wait()
 
     tile = min(TILE, query_count)
     half_copies, mass_copies = [], []
     for j in range(head_count):
         g = j // group_size
-        if j % group_size == 0:
-            q_copies[g].wait()
         lanes = slice(j // slots * width, (j // slots + 1) * width)
         for t in range(query_count // tile):
             rows = slice(t * tile, (t + 1) * tile)
@@ -168,12 +168,15 @@
                         )
                     )
                     half_copies[-1].start()
-    for group in range(-(-head_count // slots)):
-        lanes = pl.ds(group * width, width)
-        mass_copies.append(
-            pltpu.make_async_copy(mass_ref.at[:, lanes], mass_hbm.at[:, lanes], mass_sems.at[group])
-        )
-        mass_copies[-1].start()
+            whole_groups = (j + 1) // slots if j < head_count - 1 else -(-head_count // slots)
+            for group in range(len(mass_copies), whole_groups):
+                lanes = pl.ds(group * width, width)
+                mass_copies.append(
+                    pltpu.make_async_copy(
+                        mass_ref.at[:, lanes], mass_hbm.at[:, lanes], mass_sems.at[group]
+                    )
+                )
+                mass_copies[-1].start()
     stats_ref[...] = columns[...].T[: 2 * STAT_ROWS]
     for copy in half_copies + mass_copies:
         copy.wait()

time: 59.1 us -> 58.7 us (level)
  no operation moved by 1% of the time
where the time goes in v4:
time: 58.7 us; the launch traced here: 58.4 us
  starting transfers between devices  25.6 us (44%)
  waiting for transfers between devices  19.9 us (34%)
  Pallas kernels  10.2 us (17%)
  other arithmetic  1.01 us (2%)
  between operations  0.91 us (2%)
  local copies, waits for them, and re-layouts  0.87 us (1%)
    ppermute x17, starting transfers between devices, exchange(): lax.ppermute(array, axis, [(i, i ^ bit) for i in range(lax.axis_size(axis...  25.6 us
    ppermute x17, waiting for transfers between devices, exchange(): lax.ppermute(array, axis, [(i, i ^ bit) for i in range(lax.axis_size(axis...  19.9 us
    pallas_call x1, Pallas kernels, flash(): pl.pallas_call(functools.partial(flash_kernel, parts, group_size, slots),...  8.16 us
  transfers between devices with their start and end apart: 17, of which 10 were waited for; matrix products, arithmetic and copies ran while one was open for 3% of the time, Pallas kernels for 2%

profile of v4, /device:TPU:0, one launch (start us, length us, event | category | flops | bytes accessed | tf_op | source)
XLA Modules:
  0.0 58.4 jit_solution(12665657090351541998)
XLA Ops:
  0.6 0.0 copy-start.5
  0.6 8.2 %shard_map.77 = (f32[256,512]{1,0:T(8,128)}, f32[256,512]{1,0:T(8,128)}, f32[256,256]{1,0:T(8,128)}, f32[256,512]{1,0:T(8,128)}, f32[256,512]{1,0:T(8,128)}, /*i...) custom-call(s32[32]{0:T(128)} %lens_ref.1, s32[4,128]{1,0:T(4,128)} %bitcast.3, ...), custom_call_target="tpu_custom_call" | custom-call | flops 1342177280 | bytes 2621440 | tf_op jit(solution)/shard_map/pallas_call | solution.py:200
  8.8 0.0 copy-start.4
  8.8 0.0 copy-start
  8.8 3.0 %collective-permute-start.2 = (f32[32,512]{1,0:T(8,128)}, f32[32,512]{1,0:T(8,128)S(1)}, u32[]{:S(2)}, u32[]{:S(2)}) collective-permute-start(f32[32,512]{1,0:T(8,128)} %get-tuple-element.32), channel_id=1, source_target_pairs={{0,4},{4,0},{8,12},{12,8},{16,20},{20,16},{24,28},{28,24},{1,5},{5... | collective-permute-start | bytes 196616 | tf_op jit(solution)/shard_map/ppermute | solution.py:366
  11.8 0.1 collective-permute-start.1
  11.9 0.8 %slice_multiply_fusion.4 = (f32[16,512]{1,0:T(8,128)S(1)}, f32[16,512]{1,0:T(8,128)S(1)}) fusion(f32[32,512]{1,0:T(8,128)} %get-tuple-element.32), kind=kLoop, calls=%fused_computation.11 | loop fusion | flops 8192 | bytes 131072 | tf_op jit(solution)/shard_map/mul | solution.py:335
  12.7 0.0 copy-done.5
  12.8 1.9 %collective-permute-done.2 = f32[32,512]{1,0:T(8,128)S(1)} collective-permute-done((f32[32,512]{1,0:T(8,128)}, f32[32,512]{1,0:T(8,128)S(1)}, u32[]{:S(2)}, u32[]{:S(2)}) %collective-permute-start.2) | collective-permute-done | bytes 65568 | tf_op jit(solution)/shard_map/ppermute | solution.py:366
  14.7 6.0 %conditional.1 = (f32[48,512]{1,0:T(8,128)}, f32[16,512]{1,0:T(8,128)S(1)}, f32[16,512]{1,0:T(8,128)S(1)}, f32[16,512]{1,0:T(8,128)S(1)}) conditional(s32[]{:T(128)} %bitcast.1, () %tuple.20, f32[48,512]{1,0:T(8,128)S(1)} %pad_maximum_fusion), branch_computations={%region_0.0_spmd, %region_1.0_spmd} | conditional | bytes 589896 | solution.py:371
  14.7 2.4 %collective-permute-start = (f32[48,512]{1,0:T(8,128)S(1)}, f32[48,512]{1,0:T(8,128)}, u32[]{:S(2)}, u32[]{:S(2)}) collective-permute-start(f32[48,512]{1,0:T(8,128)S(1)} %param.1), channel_id=1, source_target_pairs={{0,8},{4,12},{8,0},{12,4},{16,24},{20,28},{24,16},{28,20},{1,9},{5... | collective-permute-start | bytes 294920 | tf_op jit(solution)/shard_map/cond/branch_1_fun/ppermute | solution.py:366
  17.2 2.7 %collective-permute-done = f32[48,512]{1,0:T(8,128)} collective-permute-done((f32[48,512]{1,0:T(8,128)S(1)}, f32[48,512]{1,0:T(8,128)}, u32[]{:S(2)}, u32[]{:S(2)}) %collective-permute-start) | collective-permute-done | bytes 98336 | tf_op jit(solution)/shard_map/cond/branch_1_fun/ppermute | solution.py:366
  19.9 0.8 %fusion.2 = (f32[16,512]{1,0:T(8,128)S(1)}, f32[16,512]{1,0:T(8,128)S(1)}, f32[16,512]{1,0:T(8,128)S(1)}) fusion(f32[48,512]{1,0:T(8,128)} %collective-permute-done), kind=kLoop, calls=%fused_computation.14 | loop fusion | bytes 196608 | tf_op jit(solution)/shard_map/slice | solution.py:339
  20.7 3.1 %collective-permute-start.3 = (f32[32,512]{1,0:T(8,128)S(1)}, f32[32,512]{1,0:T(8,128)S(1)}, u32[]{:S(2)}, u32[]{:S(2)}) collective-permute-start(f32[32,512]{1,0:T(8,128)S(1)} %pad_maximum_fusion.2), channel_id=1, source_target_pairs={{0,16},{4,20},{8,24},{12,28},{16,0},{20,4},{24,8},{28,12},{1,17},{... | collective-permute-start | bytes 196616 | tf_op jit(solution)/shard_map/ppermute | solution.py:366
  23.8 1.6 %collective-permute-start.7 = (f32[256,256]{1,0:T(8,128)}, f32[256,256]{1,0:T(8,128)S(1)}, u32[]{:S(2)}, u32[]{:S(2)}) collective-permute-start(f32[256,256]{1,0:T(8,128)} %get-tuple-element.47), channel_id=1, source_target_pairs={{0,8},{4,12},{8,0},{12,4},{16,24},{20,28},{24,16},{28,20},{1,9},{5... | collective-permute-start | bytes 786440 | tf_op jit(solution)/shard_map/ppermute | solution.py:366
  25.4 1.6 %collective-permute-start.5 = (f32[256,512]{1,0:T(8,128)S(1)}, f32[256,512]{1,0:T(8,128)S(1)}, u32[]{:S(2)}, u32[]{:S(2)}) collective-permute-start(f32[256,512]{1,0:T(8,128)S(1)} %copy-done.4), channel_id=1, source_target_pairs={{0,4},{4,0},{8,12},{12,8},{16,20},{20,16},{24,28},{28,24},{1,5},{5... | collective-permute-start | bytes 1572872 | tf_op jit(solution)/shard_map/ppermute | solution.py:366
  27.0 0.0 collective-permute-done.3
  27.0 0.4 shard_map.78
  27.4 0.0 collective-permute-done.1.got_ref
  27.4 0.4 shard_map.79
  27.8 1.1 %collective-permute-start.4 = (f32[128,512]{1,0:T(8,128)S(1)}, f32[128,512]{1,0:T(8,128)S(1)}, u32[]{:S(2)}, u32[]{:S(2)}) collective-permute-start(f32[128,512]{1,0:T(8,128)S(1)} %get-tuple-element.39), channel_id=1, source_target_pairs={{0,8},{4,12},{8,0},{12,4},{16,24},{20,28},{24,16},{28,20},{1,9},{5... | collective-permute-start | bytes 786440 | tf_op jit(solution)/shard_map/ppermute | solution.py:366
  28.9 0.0 collective-permute-start.12
  28.9 3.7 %collective-permute-done.7.got_ref = f32[256,256]{1,0:T(8,128)S(1)} collective-permute-done((f32[256,256]{1,0:T(8,128)}, f32[256,256]{1,0:T(8,128)S(1)}, u32[]{:S(2)}, u32[]{:S(2)}) %collective-permute-start.7) | collective-permute-done | bytes 262176 | tf_op jit(solution)/shard_map/ppermute | solution.py:366
  32.6 0.0 copy-done.3
  32.6 0.2 shard_map.81
  32.9 0.1 collective-permute-start.8
  32.9 0.0 collective-permute-done.12
  33.0 1.4 %collective-permute-start.13 = (f32[32,512]{1,0:T(8,128)S(1)}, f32[32,512]{1,0:T(8,128)S(1)}, u32[]{:S(2)}, u32[]{:S(2)}) collective-permute-start(f32[32,512]{1,0:T(8,128)S(1)} %add.36), channel_id=1, source_target_pairs={{0,2},{1,3},{2,0},{3,1},{4,6},{5,7},{6,4},{7,5},{8,10},{9,11},{10,... | collective-permute-start | bytes 196616 | tf_op jit(solution)/shard_map/ppermute | solution.py:366
  34.4 2.9 %collective-permute-done.13 = f32[32,512]{1,0:T(8,128)S(1)} collective-permute-done((f32[32,512]{1,0:T(8,128)S(1)}, f32[32,512]{1,0:T(8,128)S(1)}, u32[]{:S(2)}, u32[]{:S(2)}) %collective-permute-start.13) | collective-permute-done | bytes 65568 | tf_op jit(solution)/shard_map/ppermute | solution.py:366
  37.3 2.1 %collective-permute-start.14 = (f32[32,512]{1,0:T(8,128)S(1)}, f32[32,512]{1,0:T(8,128)S(1)}, u32[]{:S(2)}, u32[]{:S(2)}) collective-permute-start(f32[32,512]{1,0:T(8,128)S(1)} %add.37), channel_id=1, source_target_pairs={{0,4},{4,0},{8,12},{12,8},{16,20},{20,16},{24,28},{28,24},{1,5},{5... | collective-permute-start | bytes 196616 | tf_op jit(solution)/shard_map/ppermute | solution.py:366
  39.4 0.0 collective-permute-done.5.got_ref
  39.5 0.4 shard_map.80
  39.8 1.6 %collective-permute-start.6 = (f32[128,512]{1,0:T(8,128)S(1)}, f32[128,512]{1,0:T(8,128)S(1)}, u32[]{:S(2)}, u32[]{:S(2)}) collective-permute-start(f32[128,512]{1,0:T(8,128)S(1)} %get-tuple-element.44), channel_id=1, source_target_pairs={{0,8},{4,12},{8,0},{12,4},{16,24},{20,28},{24,16},{28,20},{1,9},{5... | collective-permute-start | bytes 786440 | tf_op jit(solution)/shard_map/ppermute | solution.py:366
  41.5 0.0 collective-permute-done.8
  41.5 0.2 collective-permute-done.14
  41.7 3.0 %collective-permute-start.15 = (f32[32,512]{1,0:T(8,128)S(1)}, f32[32,512]{1,0:T(8,128)S(1)}, u32[]{:S(2)}, u32[]{:S(2)}) collective-permute-start(f32[32,512]{1,0:T(8,128)S(1)} %add.38), channel_id=1, source_target_pairs={{0,16},{4,20},{8,24},{12,28},{16,0},{20,4},{24,8},{28,12},{1,17},{... | collective-permute-start | bytes 196616 | tf_op jit(solution)/shard_map/ppermute | solution.py:366
  44.7 0.0 collective-permute-done.4
  44.7 0.1 collective-permute-start.9
  44.8 4.1 %collective-permute-done.6 = f32[128,512]{1,0:T(8,128)S(1)} collective-permute-done((f32[128,512]{1,0:T(8,128)S(1)}, f32[128,512]{1,0:T(8,128)S(1)}, u32[]{:S(2)}, u32[]{:S(2)}) %collective-permute-start.6) | collective-permute-done | bytes 262176 | tf_op jit(solution)/shard_map/ppermute | solution.py:366
  49.0 2.5 %collective-permute-start.10 = (f32[64,512]{1,0:T(8,128)S(1)}, f32[64,512]{1,0:T(8,128)S(1)}, u32[]{:S(2)}, u32[]{:S(2)}) collective-permute-start(f32[64,512]{1,0:T(8,128)S(1)} %get-tuple-element.60), channel_id=1, source_target_pairs={{0,16},{4,20},{8,24},{12,28},{16,0},{20,4},{24,8},{28,12},{1,17},{... | collective-permute-start | bytes 393224 | tf_op jit(solution)/shard_map/ppermute | solution.py:366
  51.4 0.1 collective-permute-start.11
  51.5 0.0 collective-permute-done.15
  51.6 1.8 %collective-permute-start.16 = (f32[32,512]{1,0:T(8,128)S(1)}, f32[32,512]{1,0:T(8,128)S(1)}, u32[]{:S(2)}, u32[]{:S(2)}) collective-permute-start(f32[32,512]{1,0:T(8,128)S(1)} %add.39.refs_6_), channel_id=1, source_target_pairs={{0,8},{4,12},{8,0},{12,4},{16,24},{20,28},{24,16},{28,20},{1,9},{5... | collective-permute-start | bytes 196616 | tf_op jit(solution)/shard_map/ppermute | solution.py:366
  53.4 2.4 %collective-permute-done.11.refs_5_ = f32[64,256]{1,0:T(8,128)S(1)} collective-permute-done((f32[64,256]{1,0:T(8,128)S(1)}, f32[64,256]{1,0:T(8,128)S(1)}, u32[]{:S(2)}, u32[]{:S(2)}) %collective-permute-start.11) | collective-permute-done | bytes 65568 | tf_op jit(solution)/shard_map/ppermute | solution.py:366
  55.8 0.1 collective-permute-done.16.refs_7_
  55.9 0.4 collective-permute-done.9.refs_3_
  56.3 1.4 %collective-permute-done.10.refs_4_ = f32[64,512]{1,0:T(8,128)S(1)} collective-permute-done((f32[64,512]{1,0:T(8,128)S(1)}, f32[64,512]{1,0:T(8,128)S(1)}, u32[]{:S(2)}, u32[]{:S(2)}) %collective-permute-start.10) | collective-permute-done | bytes 131104 | tf_op jit(solution)/shard_map/ppermute | solution.py:366
  57.7 0.7 %shard_map.82 = (bf16[64,1280]{1,0:T(8,128)(2,1)}, f32[32,512]{1,0:T(8,128)}) custom-call(f32[64,512]{1,0:T(8,128)S(1)} %get-tuple-element.63.refs_0_, f32[64,512]{1,0:T(8,128)S(1)} %get-tuple-element.61.refs_1_, f32[64,256]{1,0:T(8,128)S(1)} %get-tuple-element.65.refs_2_, f32[64,512]{1,0:T(8,128)S(1)} %collective-permute-done.9.refs_3_, ...), custom_call_target="tpu_custom_call" | custom-call | flops 81920 | bytes 819200 | tf_op jit(solution)/shard_map/pallas_call | solution.py:319
  (24 shorter events, 0.3 us)
Async XLA Ops:
  0.6 12.1 %copy-start.5 = (s32[32]{0:T(128)S(1)}, s32[32]{0:T(128)}, u32[]{:S(2)}) copy-start(s32[32]{0:T(128)} %lens_ref.1) | copy-start | bytes 388
  8.8 16.6 %copy-start.4 = (f32[256,512]{1,0:T(8,128)S(1)}, f32[256,512]{1,0:T(8,128)}, u32[]{:S(2)}) copy-start(f32[256,512]{1,0:T(8,128)} %get-tuple-element.42) | copy-start | bytes 1572868
  8.8 18.2 %copy-start = (f32[512,384]{1,0:T(8,128)S(1)}, f32[512,384]{1,0:T(8,128)}, u32[]{:S(2)}) copy-start(f32[512,384]{1,0:T(8,128)} %get-tuple-element.36.refs_2_) | copy-start | bytes 2359300
  8.8 5.8 %collective-permute-start.2 = (f32[32,512]{1,0:T(8,128)}, f32[32,512]{1,0:T(8,128)S(1)}, u32[]{:S(2)}, u32[]{:S(2)}) collective-permute-start(f32[32,512]{1,0:T(8,128)} %get-tuple-element.32), channel_id=1, source_target_pairs={{0,4},{4,0},{8,12},{12,8},{16,20},{20,16},{24,28},{28,24},{1,5},{5... | collective-permute-start | bytes 196616 | tf_op jit(solution)/shard_map/ppermute | solution.py:366
  11.8 15.6 %collective-permute-start.1 = (f32[256,512]{1,0:T(8,128)}, f32[256,512]{1,0:T(8,128)S(1)}, u32[]{:S(2)}, u32[]{:S(2)}) collective-permute-start(f32[256,512]{1,0:T(8,128)} %get-tuple-element.31), channel_id=1, source_target_pairs={{0,4},{4,0},{8,12},{12,8},{16,20},{20,16},{24,28},{28,24},{1,5},{5... | collective-permute-start | bytes 1572872 | tf_op jit(solution)/shard_map/ppermute | solution.py:366
  12.7 14.7 %copy-start.2 = (f32[256,512]{1,0:T(8,128)S(1)}, f32[256,512]{1,0:T(8,128)}, u32[]{:S(2)}) copy-start(f32[256,512]{1,0:T(8,128)} %get-tuple-element.30.keep_ref) | copy-start | bytes 1572868
  14.7 5.1 %collective-permute-start = (f32[48,512]{1,0:T(8,128)S(1)}, f32[48,512]{1,0:T(8,128)}, u32[]{:S(2)}, u32[]{:S(2)}) collective-permute-start(f32[48,512]{1,0:T(8,128)S(1)} %param.1), channel_id=1, source_target_pairs={{0,8},{4,12},{8,0},{12,4},{16,24},{20,28},{24,16},{28,20},{1,9},{5... | collective-permute-start | bytes 294920 | tf_op jit(solution)/shard_map/cond/branch_1_fun/ppermute | solution.py:366
  20.7 12.0 %copy-start.3 = (f32[256,256]{1,0:T(8,128)S(1)}, f32[256,256]{1,0:T(8,128)}, u32[]{:S(2)}) copy-start(f32[256,256]{1,0:T(8,128)} %get-tuple-element.45.keep_ref) | copy-start | bytes 786436
  20.7 6.3 %collective-permute-start.3 = (f32[32,512]{1,0:T(8,128)S(1)}, f32[32,512]{1,0:T(8,128)S(1)}, u32[]{:S(2)}, u32[]{:S(2)}) collective-permute-start(f32[32,512]{1,0:T(8,128)S(1)} %pad_maximum_fusion.2), channel_id=1, source_target_pairs={{0,16},{4,20},{8,24},{12,28},{16,0},{20,4},{24,8},{28,12},{1,17},{... | collective-permute-start | bytes 196616 | tf_op jit(solution)/shard_map/ppermute | solution.py:366
  23.8 8.8 %collective-permute-start.7 = (f32[256,256]{1,0:T(8,128)}, f32[256,256]{1,0:T(8,128)S(1)}, u32[]{:S(2)}, u32[]{:S(2)}) collective-permute-start(f32[256,256]{1,0:T(8,128)} %get-tuple-element.47), channel_id=1, source_target_pairs={{0,8},{4,12},{8,0},{12,4},{16,24},{20,28},{24,16},{28,20},{1,9},{5... | collective-permute-start | bytes 786440 | tf_op jit(solution)/shard_map/ppermute | solution.py:366
  25.4 14.1 %collective-permute-start.5 = (f32[256,512]{1,0:T(8,128)S(1)}, f32[256,512]{1,0:T(8,128)S(1)}, u32[]{:S(2)}, u32[]{:S(2)}) collective-permute-start(f32[256,512]{1,0:T(8,128)S(1)} %copy-done.4), channel_id=1, source_target_pairs={{0,4},{4,0},{8,12},{12,8},{16,20},{20,16},{24,28},{28,24},{1,5},{5... | collective-permute-start | bytes 1572872 | tf_op jit(solution)/shard_map/ppermute | solution.py:366
  27.4 12.1 %copy-start.1 = (f32[256,512]{1,0:T(8,128)S(1)}, f32[256,512]{1,0:T(8,128)}, u32[]{:S(2)}) copy-start(f32[256,512]{1,0:T(8,128)} %get-tuple-element.40.keep_ref) | copy-start | bytes 1572868
  27.8 16.9 %collective-permute-start.4 = (f32[128,512]{1,0:T(8,128)S(1)}, f32[128,512]{1,0:T(8,128)S(1)}, u32[]{:S(2)}, u32[]{:S(2)}) collective-permute-start(f32[128,512]{1,0:T(8,128)S(1)} %get-tuple-element.39), channel_id=1, source_target_pairs={{0,8},{4,12},{8,0},{12,4},{16,24},{20,28},{24,16},{28,20},{1,9},{5... | collective-permute-start | bytes 786440 | tf_op jit(solution)/shard_map/ppermute | solution.py:366
  28.9 4.0 %collective-permute-start.12 = (f32[32,512]{1,0:T(8,128)S(1)}, f32[32,512]{1,0:T(8,128)S(1)}, u32[]{:S(2)}, u32[]{:S(2)}) collective-permute-start(f32[32,512]{1,0:T(8,128)S(1)} %get-tuple-element.52), channel_id=1, source_target_pairs={{0,1},{1,0},{2,3},{3,2},{4,5},{5,4},{6,7},{7,6},{8,9},{9,8},{10,11... | collective-permute-start | bytes 196616 | tf_op jit(solution)/shard_map/ppermute | solution.py:366
  32.9 8.6 %collective-permute-start.8 = (f32[128,256]{1,0:T(8,128)S(1)}, f32[128,256]{1,0:T(8,128)S(1)}, u32[]{:S(2)}, u32[]{:S(2)}) collective-permute-start(f32[128,256]{1,0:T(8,128)S(1)} %get-tuple-element.50), channel_id=1, source_target_pairs={{0,16},{4,20},{8,24},{12,28},{16,0},{20,4},{24,8},{28,12},{1,17},{... | collective-permute-start | bytes 393224 | tf_op jit(solution)/shard_map/ppermute | solution.py:366
  33.0 4.3 %collective-permute-start.13 = (f32[32,512]{1,0:T(8,128)S(1)}, f32[32,512]{1,0:T(8,128)S(1)}, u32[]{:S(2)}, u32[]{:S(2)}) collective-permute-start(f32[32,512]{1,0:T(8,128)S(1)} %add.36), channel_id=1, source_target_pairs={{0,2},{1,3},{2,0},{3,1},{4,6},{5,7},{6,4},{7,5},{8,10},{9,11},{10,... | collective-permute-start | bytes 196616 | tf_op jit(solution)/shard_map/ppermute | solution.py:366
  37.3 4.4 %collective-permute-start.14 = (f32[32,512]{1,0:T(8,128)S(1)}, f32[32,512]{1,0:T(8,128)S(1)}, u32[]{:S(2)}, u32[]{:S(2)}) collective-permute-start(f32[32,512]{1,0:T(8,128)S(1)} %add.37), channel_id=1, source_target_pairs={{0,4},{4,0},{8,12},{12,8},{16,20},{20,16},{24,28},{28,24},{1,5},{5... | collective-permute-start | bytes 196616 | tf_op jit(solution)/shard_map/ppermute | solution.py:366
  39.8 9.1 %collective-permute-start.6 = (f32[128,512]{1,0:T(8,128)S(1)}, f32[128,512]{1,0:T(8,128)S(1)}, u32[]{:S(2)}, u32[]{:S(2)}) collective-permute-start(f32[128,512]{1,0:T(8,128)S(1)} %get-tuple-element.44), channel_id=1, source_target_pairs={{0,8},{4,12},{8,0},{12,4},{16,24},{20,28},{24,16},{28,20},{1,9},{5... | collective-permute-start | bytes 786440 | tf_op jit(solution)/shard_map/ppermute | solution.py:366
  41.7 9.8 %collective-permute-start.15 = (f32[32,512]{1,0:T(8,128)S(1)}, f32[32,512]{1,0:T(8,128)S(1)}, u32[]{:S(2)}, u32[]{:S(2)}) collective-permute-start(f32[32,512]{1,0:T(8,128)S(1)} %add.38), channel_id=1, source_target_pairs={{0,16},{4,20},{8,24},{12,28},{16,0},{20,4},{24,8},{28,12},{1,17},{... | collective-permute-start | bytes 196616 | tf_op jit(solution)/shard_map/ppermute | solution.py:366
  44.7 11.5 %collective-permute-start.9 = (f32[64,512]{1,0:T(8,128)S(1)}, f32[64,512]{1,0:T(8,128)S(1)}, u32[]{:S(2)}, u32[]{:S(2)}) collective-permute-start(f32[64,512]{1,0:T(8,128)S(1)} %get-tuple-element.62), channel_id=1, source_target_pairs={{0,16},{4,20},{8,24},{12,28},{16,0},{20,4},{24,8},{28,12},{1,17},{... | collective-permute-start | bytes 393224 | tf_op jit(solution)/shard_map/ppermute | solution.py:366
  49.0 8.7 %collective-permute-start.10 = (f32[64,512]{1,0:T(8,128)S(1)}, f32[64,512]{1,0:T(8,128)S(1)}, u32[]{:S(2)}, u32[]{:S(2)}) collective-permute-start(f32[64,512]{1,0:T(8,128)S(1)} %get-tuple-element.60), channel_id=1, source_target_pairs={{0,16},{4,20},{8,24},{12,28},{16,0},{20,4},{24,8},{28,12},{1,17},{... | collective-permute-start | bytes 393224 | tf_op jit(solution)/shard_map/ppermute | solution.py:366
  51.4 4.3 %collective-permute-start.11 = (f32[64,256]{1,0:T(8,128)S(1)}, f32[64,256]{1,0:T(8,128)S(1)}, u32[]{:S(2)}, u32[]{:S(2)}) collective-permute-start(f32[64,256]{1,0:T(8,128)S(1)} %get-tuple-element.64), channel_id=1, source_target_pairs={{0,4},{4,0},{8,12},{12,8},{16,20},{20,16},{24,28},{28,24},{1,5},{5... | collective-permute-start | bytes 196616 | tf_op jit(solution)/shard_map/ppermute | solution.py:366
  51.6 4.3 %collective-permute-start.16 = (f32[32,512]{1,0:T(8,128)S(1)}, f32[32,512]{1,0:T(8,128)S(1)}, u32[]{:S(2)}, u32[]{:S(2)}) collective-permute-start(f32[32,512]{1,0:T(8,128)S(1)} %add.39.refs_6_), channel_id=1, source_target_pairs={{0,8},{4,12},{8,0},{12,4},{16,24},{20,28},{24,16},{28,20},{1,9},{5... | collective-permute-start | bytes 196616 | tf_op jit(solution)/shard_map/ppermute | solution.py:366

commit v5 on v4

--- a/solution.py
+++ b/solution.py
@@ -19,7 +19,7 @@
 HALF_PI = (1.5706787109375, 1.1761486530303955e-4, 9.920935796805404e-10)
 
 CHUNKS = ((4, 0), (4, 0), (2, 1))
-TIES = {"c1.1": ("a.2",), "c2.2": ("a.2",), "h.1": ("c0.1",)}
+TIES = {"h.1": ("c0.1",)}
 FENCES = (("a.2",),)
 MASS_ORDER = ("h.1", "h.2", "m.1", "m.4", "m.2")
 

time: 58.7 us -> 58.7 us (level)
  no operation moved by 1% of the time
where the time goes in v5:
time: 58.7 us; the launch traced here: 58.4 us
  starting transfers between devices  25.6 us (44%)
  waiting for transfers between devices  19.9 us (34%)
  Pallas kernels  10.2 us (17%)
  other arithmetic  1.01 us (2%)
  between operations  0.91 us (2%)
  local copies, waits for them, and re-layouts  0.87 us (1%)
    ppermute x17, starting transfers between devices, exchange(): lax.ppermute(array, axis, [(i, i ^ bit) for i in range(lax.axis_size(axis...  25.6 us
    ppermute x17, waiting for transfers between devices, exchange(): lax.ppermute(array, axis, [(i, i ^ bit) for i in range(lax.axis_size(axis...  19.9 us
    pallas_call x1, Pallas kernels, flash(): pl.pallas_call(functools.partial(flash_kernel, parts, group_size, slots),...  8.16 us
  transfers between devices with their start and end apart: 17, of which 10 were waited for; matrix products, arithmetic and copies ran while one was open for 3% of the time, Pallas kernels for 2%

profile of v5, /device:TPU:0, one launch (start us, length us, event | category | flops | bytes accessed | tf_op | source)
XLA Modules:
  0.0 58.4 jit_solution(12665657090351541998)
XLA Ops:
  0.6 0.0 copy-start.5
  0.6 8.2 %shard_map.77 = (f32[256,512]{1,0:T(8,128)}, f32[256,512]{1,0:T(8,128)}, f32[256,256]{1,0:T(8,128)}, f32[256,512]{1,0:T(8,128)}, f32[256,512]{1,0:T(8,128)}, /*i...) custom-call(s32[32]{0:T(128)} %lens_ref.1, s32[4,128]{1,0:T(4,128)} %bitcast.3, ...), custom_call_target="tpu_custom_call" | custom-call | flops 1342177280 | bytes 2621440 | tf_op jit(solution)/shard_map/pallas_call | solution.py:200
  8.8 0.0 copy-start.4
  8.8 0.0 copy-start
  8.8 3.0 %collective-permute-start.2 = (f32[32,512]{1,0:T(8,128)}, f32[32,512]{1,0:T(8,128)S(1)}, u32[]{:S(2)}, u32[]{:S(2)}) collective-permute-start(f32[32,512]{1,0:T(8,128)} %get-tuple-element.30), channel_id=1, source_target_pairs={{0,4},{4,0},{8,12},{12,8},{16,20},{20,16},{24,28},{28,24},{1,5},{5... | collective-permute-start | bytes 196616 | tf_op jit(solution)/shard_map/ppermute | solution.py:366
  11.8 0.1 collective-permute-start.1
  11.9 0.8 %slice_multiply_fusion.4 = (f32[16,512]{1,0:T(8,128)S(1)}, f32[16,512]{1,0:T(8,128)S(1)}) fusion(f32[32,512]{1,0:T(8,128)} %get-tuple-element.30), kind=kLoop, calls=%fused_computation.11 | loop fusion | flops 8192 | bytes 131072 | tf_op jit(solution)/shard_map/mul | solution.py:335
  12.7 0.0 copy-done.5
  12.8 1.9 %collective-permute-done.2 = f32[32,512]{1,0:T(8,128)S(1)} collective-permute-done((f32[32,512]{1,0:T(8,128)}, f32[32,512]{1,0:T(8,128)S(1)}, u32[]{:S(2)}, u32[]{:S(2)}) %collective-permute-start.2) | collective-permute-done | bytes 65568 | tf_op jit(solution)/shard_map/ppermute | solution.py:366
  14.7 6.0 %conditional.1 = (f32[48,512]{1,0:T(8,128)}, f32[16,512]{1,0:T(8,128)S(1)}, f32[16,512]{1,0:T(8,128)S(1)}, f32[16,512]{1,0:T(8,128)S(1)}) conditional(s32[]{:T(128)} %bitcast.1, () %tuple.18, f32[48,512]{1,0:T(8,128)S(1)} %pad_maximum_fusion), branch_computations={%region_0.0_spmd, %region_1.0_spmd} | conditional | bytes 589896 | solution.py:371
  14.7 2.4 %collective-permute-start = (f32[48,512]{1,0:T(8,128)S(1)}, f32[48,512]{1,0:T(8,128)}, u32[]{:S(2)}, u32[]{:S(2)}) collective-permute-start(f32[48,512]{1,0:T(8,128)S(1)} %param.1), channel_id=1, source_target_pairs={{0,8},{4,12},{8,0},{12,4},{16,24},{20,28},{24,16},{28,20},{1,9},{5... | collective-permute-start | bytes 294920 | tf_op jit(solution)/shard_map/cond/branch_1_fun/ppermute | solution.py:366
  17.2 2.7 %collective-permute-done = f32[48,512]{1,0:T(8,128)} collective-permute-done((f32[48,512]{1,0:T(8,128)S(1)}, f32[48,512]{1,0:T(8,128)}, u32[]{:S(2)}, u32[]{:S(2)}) %collective-permute-start) | collective-permute-done | bytes 98336 | tf_op jit(solution)/shard_map/cond/branch_1_fun/ppermute | solution.py:366
  19.9 0.8 %fusion.2 = (f32[16,512]{1,0:T(8,128)S(1)}, f32[16,512]{1,0:T(8,128)S(1)}, f32[16,512]{1,0:T(8,128)S(1)}) fusion(f32[48,512]{1,0:T(8,128)} %collective-permute-done), kind=kLoop, calls=%fused_computation.14 | loop fusion | bytes 196608 | tf_op jit(solution)/shard_map/slice | solution.py:339
  20.7 3.1 %collective-permute-start.3 = (f32[32,512]{1,0:T(8,128)S(1)}, f32[32,512]{1,0:T(8,128)S(1)}, u32[]{:S(2)}, u32[]{:S(2)}) collective-permute-start(f32[32,512]{1,0:T(8,128)S(1)} %pad_maximum_fusion.2), channel_id=1, source_target_pairs={{0,16},{4,20},{8,24},{12,28},{16,0},{20,4},{24,8},{28,12},{1,17},{... | collective-permute-start | bytes 196616 | tf_op jit(solution)/shard_map/ppermute | solution.py:366
  23.8 1.6 %collective-permute-start.7 = (f32[256,256]{1,0:T(8,128)}, f32[256,256]{1,0:T(8,128)S(1)}, u32[]{:S(2)}, u32[]{:S(2)}) collective-permute-start(f32[256,256]{1,0:T(8,128)} %get-tuple-element.43), channel_id=1, source_target_pairs={{0,8},{4,12},{8,0},{12,4},{16,24},{20,28},{24,16},{28,20},{1,9},{5... | collective-permute-start | bytes 786440 | tf_op jit(solution)/shard_map/ppermute | solution.py:366
  25.4 1.6 %collective-permute-start.5 = (f32[256,512]{1,0:T(8,128)S(1)}, f32[256,512]{1,0:T(8,128)S(1)}, u32[]{:S(2)}, u32[]{:S(2)}) collective-permute-start(f32[256,512]{1,0:T(8,128)S(1)} %copy-done.4), channel_id=1, source_target_pairs={{0,4},{4,0},{8,12},{12,8},{16,20},{20,16},{24,28},{28,24},{1,5},{5... | collective-permute-start | bytes 1572872 | tf_op jit(solution)/shard_map/ppermute | solution.py:366
  27.0 0.0 collective-permute-done.3
  27.0 0.4 shard_map.78
  27.4 0.0 collective-permute-done.1.got_ref
  27.4 0.4 shard_map.79
  27.8 1.1 %collective-permute-start.4 = (f32[128,512]{1,0:T(8,128)S(1)}, f32[128,512]{1,0:T(8,128)S(1)}, u32[]{:S(2)}, u32[]{:S(2)}) collective-permute-start(f32[128,512]{1,0:T(8,128)S(1)} %get-tuple-element.37), channel_id=1, source_target_pairs={{0,8},{4,12},{8,0},{12,4},{16,24},{20,28},{24,16},{28,20},{1,9},{5... | collective-permute-start | bytes 786440 | tf_op jit(solution)/shard_map/ppermute | solution.py:366
  28.9 0.0 collective-permute-start.12
  28.9 3.7 %collective-permute-done.7.got_ref = f32[256,256]{1,0:T(8,128)S(1)} collective-permute-done((f32[256,256]{1,0:T(8,128)}, f32[256,256]{1,0:T(8,128)S(1)}, u32[]{:S(2)}, u32[]{:S(2)}) %collective-permute-start.7) | collective-permute-done | bytes 262176 | tf_op jit(solution)/shard_map/ppermute | solution.py:366
  32.6 0.0 copy-done.3
  32.6 0.2 shard_map.81
  32.9 0.1 collective-permute-start.8
  32.9 0.0 collective-permute-done.12
  33.0 1.4 %collective-permute-start.13 = (f32[32,512]{1,0:T(8,128)S(1)}, f32[32,512]{1,0:T(8,128)S(1)}, u32[]{:S(2)}, u32[]{:S(2)}) collective-permute-start(f32[32,512]{1,0:T(8,128)S(1)} %add.36), channel_id=1, source_target_pairs={{0,2},{1,3},{2,0},{3,1},{4,6},{5,7},{6,4},{7,5},{8,10},{9,11},{10,... | collective-permute-start | bytes 196616 | tf_op jit(solution)/shard_map/ppermute | solution.py:366
  34.4 2.9 %collective-permute-done.13 = f32[32,512]{1,0:T(8,128)S(1)} collective-permute-done((f32[32,512]{1,0:T(8,128)S(1)}, f32[32,512]{1,0:T(8,128)S(1)}, u32[]{:S(2)}, u32[]{:S(2)}) %collective-permute-start.13) | collective-permute-done | bytes 65568 | tf_op jit(solution)/shard_map/ppermute | solution.py:366
  37.3 2.1 %collective-permute-start.14 = (f32[32,512]{1,0:T(8,128)S(1)}, f32[32,512]{1,0:T(8,128)S(1)}, u32[]{:S(2)}, u32[]{:S(2)}) collective-permute-start(f32[32,512]{1,0:T(8,128)S(1)} %add.37), channel_id=1, source_target_pairs={{0,4},{4,0},{8,12},{12,8},{16,20},{20,16},{24,28},{28,24},{1,5},{5... | collective-permute-start | bytes 196616 | tf_op jit(solution)/shard_map/ppermute | solution.py:366
  39.4 0.0 collective-permute-done.5.got_ref
  39.5 0.4 shard_map.80
  39.8 1.6 %collective-permute-start.6 = (f32[128,512]{1,0:T(8,128)S(1)}, f32[128,512]{1,0:T(8,128)S(1)}, u32[]{:S(2)}, u32[]{:S(2)}) collective-permute-start(f32[128,512]{1,0:T(8,128)S(1)} %get-tuple-element.41), channel_id=1, source_target_pairs={{0,8},{4,12},{8,0},{12,4},{16,24},{20,28},{24,16},{28,20},{1,9},{5... | collective-permute-start | bytes 786440 | tf_op jit(solution)/shard_map/ppermute | solution.py:366
  41.5 0.0 collective-permute-done.8
  41.5 0.2 collective-permute-done.14
  41.7 3.0 %collective-permute-start.15 = (f32[32,512]{1,0:T(8,128)S(1)}, f32[32,512]{1,0:T(8,128)S(1)}, u32[]{:S(2)}, u32[]{:S(2)}) collective-permute-start(f32[32,512]{1,0:T(8,128)S(1)} %add.38), channel_id=1, source_target_pairs={{0,16},{4,20},{8,24},{12,28},{16,0},{20,4},{24,8},{28,12},{1,17},{... | collective-permute-start | bytes 196616 | tf_op jit(solution)/shard_map/ppermute | solution.py:366
  44.7 0.0 collective-permute-done.4
  44.7 0.1 collective-permute-start.9
  44.8 4.1 %collective-permute-done.6 = f32[128,512]{1,0:T(8,128)S(1)} collective-permute-done((f32[128,512]{1,0:T(8,128)S(1)}, f32[128,512]{1,0:T(8,128)S(1)}, u32[]{:S(2)}, u32[]{:S(2)}) %collective-permute-start.6) | collective-permute-done | bytes 262176 | tf_op jit(solution)/shard_map/ppermute | solution.py:366
  49.0 2.5 %collective-permute-start.10 = (f32[64,512]{1,0:T(8,128)S(1)}, f32[64,512]{1,0:T(8,128)S(1)}, u32[]{:S(2)}, u32[]{:S(2)}) collective-permute-start(f32[64,512]{1,0:T(8,128)S(1)} %get-tuple-element.56), channel_id=1, source_target_pairs={{0,16},{4,20},{8,24},{12,28},{16,0},{20,4},{24,8},{28,12},{1,17},{... | collective-permute-start | bytes 393224 | tf_op jit(solution)/shard_map/ppermute | solution.py:366
  51.4 0.1 collective-permute-start.11
  51.5 0.0 collective-permute-done.15
  51.6 1.8 %collective-permute-start.16 = (f32[32,512]{1,0:T(8,128)S(1)}, f32[32,512]{1,0:T(8,128)S(1)}, u32[]{:S(2)}, u32[]{:S(2)}) collective-permute-start(f32[32,512]{1,0:T(8,128)S(1)} %add.39.refs_6_), channel_id=1, source_target_pairs={{0,8},{4,12},{8,0},{12,4},{16,24},{20,28},{24,16},{28,20},{1,9},{5... | collective-permute-start | bytes 196616 | tf_op jit(solution)/shard_map/ppermute | solution.py:366
  53.4 2.4 %collective-permute-done.11.refs_5_ = f32[64,256]{1,0:T(8,128)S(1)} collective-permute-done((f32[64,256]{1,0:T(8,128)S(1)}, f32[64,256]{1,0:T(8,128)S(1)}, u32[]{:S(2)}, u32[]{:S(2)}) %collective-permute-start.11) | collective-permute-done | bytes 65568 | tf_op jit(solution)/shard_map/ppermute | solution.py:366
  55.8 0.1 collective-permute-done.16.refs_7_
  55.9 0.4 collective-permute-done.9.refs_3_
  56.3 1.4 %collective-permute-done.10.refs_4_ = f32[64,512]{1,0:T(8,128)S(1)} collective-permute-done((f32[64,512]{1,0:T(8,128)S(1)}, f32[64,512]{1,0:T(8,128)S(1)}, u32[]{:S(2)}, u32[]{:S(2)}) %collective-permute-start.10) | collective-permute-done | bytes 131104 | tf_op jit(solution)/shard_map/ppermute | solution.py:366
  57.7 0.7 %shard_map.82 = (bf16[64,1280]{1,0:T(8,128)(2,1)}, f32[32,512]{1,0:T(8,128)}) custom-call(f32[64,512]{1,0:T(8,128)S(1)} %get-tuple-element.59.refs_0_, f32[64,512]{1,0:T(8,128)S(1)} %get-tuple-element.57.refs_1_, f32[64,256]{1,0:T(8,128)S(1)} %get-tuple-element.61.refs_2_, f32[64,512]{1,0:T(8,128)S(1)} %collective-permute-done.9.refs_3_, ...), custom_call_target="tpu_custom_call" | custom-call | flops 81920 | bytes 819200 | tf_op jit(solution)/shard_map/pallas_call | solution.py:319
  (24 shorter events, 0.3 us)
Async XLA Ops:
  0.6 12.1 %copy-start.5 = (s32[32]{0:T(128)S(1)}, s32[32]{0:T(128)}, u32[]{:S(2)}) copy-start(s32[32]{0:T(128)} %lens_ref.1) | copy-start | bytes 388
  8.8 16.6 %copy-start.4 = (f32[256,512]{1,0:T(8,128)S(1)}, f32[256,512]{1,0:T(8,128)}, u32[]{:S(2)}) copy-start(f32[256,512]{1,0:T(8,128)} %get-tuple-element.39) | copy-start | bytes 1572868
  8.8 18.2 %copy-start = (f32[512,384]{1,0:T(8,128)S(1)}, f32[512,384]{1,0:T(8,128)}, u32[]{:S(2)}) copy-start(f32[512,384]{1,0:T(8,128)} %get-tuple-element.34.refs_2_) | copy-start | bytes 2359300
  8.8 5.8 %collective-permute-start.2 = (f32[32,512]{1,0:T(8,128)}, f32[32,512]{1,0:T(8,128)S(1)}, u32[]{:S(2)}, u32[]{:S(2)}) collective-permute-start(f32[32,512]{1,0:T(8,128)} %get-tuple-element.30), channel_id=1, source_target_pairs={{0,4},{4,0},{8,12},{12,8},{16,20},{20,16},{24,28},{28,24},{1,5},{5... | collective-permute-start | bytes 196616 | tf_op jit(solution)/shard_map/ppermute | solution.py:366
  11.8 15.6 %collective-permute-start.1 = (f32[256,512]{1,0:T(8,128)}, f32[256,512]{1,0:T(8,128)S(1)}, u32[]{:S(2)}, u32[]{:S(2)}) collective-permute-start(f32[256,512]{1,0:T(8,128)} %get-tuple-element.29), channel_id=1, source_target_pairs={{0,4},{4,0},{8,12},{12,8},{16,20},{20,16},{24,28},{28,24},{1,5},{5... | collective-permute-start | bytes 1572872 | tf_op jit(solution)/shard_map/ppermute | solution.py:366
  12.7 14.7 %copy-start.2 = (f32[256,512]{1,0:T(8,128)S(1)}, f32[256,512]{1,0:T(8,128)}, u32[]{:S(2)}) copy-start(f32[256,512]{1,0:T(8,128)} %get-tuple-element.28.keep_ref) | copy-start | bytes 1572868
  14.7 5.1 %collective-permute-start = (f32[48,512]{1,0:T(8,128)S(1)}, f32[48,512]{1,0:T(8,128)}, u32[]{:S(2)}, u32[]{:S(2)}) collective-permute-start(f32[48,512]{1,0:T(8,128)S(1)} %param.1), channel_id=1, source_target_pairs={{0,8},{4,12},{8,0},{12,4},{16,24},{20,28},{24,16},{28,20},{1,9},{5... | collective-permute-start | bytes 294920 | tf_op jit(solution)/shard_map/cond/branch_1_fun/ppermute | solution.py:366
  20.7 12.0 %copy-start.3 = (f32[256,256]{1,0:T(8,128)S(1)}, f32[256,256]{1,0:T(8,128)}, u32[]{:S(2)}) copy-start(f32[256,256]{1,0:T(8,128)} %get-tuple-element.42.keep_ref) | copy-start | bytes 786436
  20.7 6.3 %collective-permute-start.3 = (f32[32,512]{1,0:T(8,128)S(1)}, f32[32,512]{1,0:T(8,128)S(1)}, u32[]{:S(2)}, u32[]{:S(2)}) collective-permute-start(f32[32,512]{1,0:T(8,128)S(1)} %pad_maximum_fusion.2), channel_id=1, source_target_pairs={{0,16},{4,20},{8,24},{12,28},{16,0},{20,4},{24,8},{28,12},{1,17},{... | collective-permute-start | bytes 196616 | tf_op jit(solution)/shard_map/ppermute | solution.py:366
  23.8 8.8 %collective-permute-start.7 = (f32[256,256]{1,0:T(8,128)}, f32[256,256]{1,0:T(8,128)S(1)}, u32[]{:S(2)}, u32[]{:S(2)}) collective-permute-start(f32[256,256]{1,0:T(8,128)} %get-tuple-element.43), channel_id=1, source_target_pairs={{0,8},{4,12},{8,0},{12,4},{16,24},{20,28},{24,16},{28,20},{1,9},{5... | collective-permute-start | bytes 786440 | tf_op jit(solution)/shard_map/ppermute | solution.py:366
  25.4 14.1 %collective-permute-start.5 = (f32[256,512]{1,0:T(8,128)S(1)}, f32[256,512]{1,0:T(8,128)S(1)}, u32[]{:S(2)}, u32[]{:S(2)}) collective-permute-start(f32[256,512]{1,0:T(8,128)S(1)} %copy-done.4), channel_id=1, source_target_pairs={{0,4},{4,0},{8,12},{12,8},{16,20},{20,16},{24,28},{28,24},{1,5},{5... | collective-permute-start | bytes 1572872 | tf_op jit(solution)/shard_map/ppermute | solution.py:366
  27.4 12.1 %copy-start.1 = (f32[256,512]{1,0:T(8,128)S(1)}, f32[256,512]{1,0:T(8,128)}, u32[]{:S(2)}) copy-start(f32[256,512]{1,0:T(8,128)} %get-tuple-element.38.keep_ref) | copy-start | bytes 1572868
  27.8 16.9 %collective-permute-start.4 = (f32[128,512]{1,0:T(8,128)S(1)}, f32[128,512]{1,0:T(8,128)S(1)}, u32[]{:S(2)}, u32[]{:S(2)}) collective-permute-start(f32[128,512]{1,0:T(8,128)S(1)} %get-tuple-element.37), channel_id=1, source_target_pairs={{0,8},{4,12},{8,0},{12,4},{16,24},{20,28},{24,16},{28,20},{1,9},{5... | collective-permute-start | bytes 786440 | tf_op jit(solution)/shard_map/ppermute | solution.py:366
  28.9 4.0 %collective-permute-start.12 = (f32[32,512]{1,0:T(8,128)S(1)}, f32[32,512]{1,0:T(8,128)S(1)}, u32[]{:S(2)}, u32[]{:S(2)}) collective-permute-start(f32[32,512]{1,0:T(8,128)S(1)} %get-tuple-element.48), channel_id=1, source_target_pairs={{0,1},{1,0},{2,3},{3,2},{4,5},{5,4},{6,7},{7,6},{8,9},{9,8},{10,11... | collective-permute-start | bytes 196616 | tf_op jit(solution)/shard_map/ppermute | solution.py:366
  32.9 8.6 %collective-permute-start.8 = (f32[128,256]{1,0:T(8,128)S(1)}, f32[128,256]{1,0:T(8,128)S(1)}, u32[]{:S(2)}, u32[]{:S(2)}) collective-permute-start(f32[128,256]{1,0:T(8,128)S(1)} %get-tuple-element.46), channel_id=1, source_target_pairs={{0,16},{4,20},{8,24},{12,28},{16,0},{20,4},{24,8},{28,12},{1,17},{... | collective-permute-start | bytes 393224 | tf_op jit(solution)/shard_map/ppermute | solution.py:366
  33.0 4.3 %collective-permute-start.13 = (f32[32,512]{1,0:T(8,128)S(1)}, f32[32,512]{1,0:T(8,128)S(1)}, u32[]{:S(2)}, u32[]{:S(2)}) collective-permute-start(f32[32,512]{1,0:T(8,128)S(1)} %add.36), channel_id=1, source_target_pairs={{0,2},{1,3},{2,0},{3,1},{4,6},{5,7},{6,4},{7,5},{8,10},{9,11},{10,... | collective-permute-start | bytes 196616 | tf_op jit(solution)/shard_map/ppermute | solution.py:366
  37.3 4.4 %collective-permute-start.14 = (f32[32,512]{1,0:T(8,128)S(1)}, f32[32,512]{1,0:T(8,128)S(1)}, u32[]{:S(2)}, u32[]{:S(2)}) collective-permute-start(f32[32,512]{1,0:T(8,128)S(1)} %add.37), channel_id=1, source_target_pairs={{0,4},{4,0},{8,12},{12,8},{16,20},{20,16},{24,28},{28,24},{1,5},{5... | collective-permute-start | bytes 196616 | tf_op jit(solution)/shard_map/ppermute | solution.py:366
  39.8 9.1 %collective-permute-start.6 = (f32[128,512]{1,0:T(8,128)S(1)}, f32[128,512]{1,0:T(8,128)S(1)}, u32[]{:S(2)}, u32[]{:S(2)}) collective-permute-start(f32[128,512]{1,0:T(8,128)S(1)} %get-tuple-element.41), channel_id=1, source_target_pairs={{0,8},{4,12},{8,0},{12,4},{16,24},{20,28},{24,16},{28,20},{1,9},{5... | collective-permute-start | bytes 786440 | tf_op jit(solution)/shard_map/ppermute | solution.py:366
  41.7 9.8 %collective-permute-start.15 = (f32[32,512]{1,0:T(8,128)S(1)}, f32[32,512]{1,0:T(8,128)S(1)}, u32[]{:S(2)}, u32[]{:S(2)}) collective-permute-start(f32[32,512]{1,0:T(8,128)S(1)} %add.38), channel_id=1, source_target_pairs={{0,16},{4,20},{8,24},{12,28},{16,0},{20,4},{24,8},{28,12},{1,17},{... | collective-permute-start | bytes 196616 | tf_op jit(solution)/shard_map/ppermute | solution.py:366
  44.7 11.5 %collective-permute-start.9 = (f32[64,512]{1,0:T(8,128)S(1)}, f32[64,512]{1,0:T(8,128)S(1)}, u32[]{:S(2)}, u32[]{:S(2)}) collective-permute-start(f32[64,512]{1,0:T(8,128)S(1)} %get-tuple-element.58), channel_id=1, source_target_pairs={{0,16},{4,20},{8,24},{12,28},{16,0},{20,4},{24,8},{28,12},{1,17},{... | collective-permute-start | bytes 393224 | tf_op jit(solution)/shard_map/ppermute | solution.py:366
  49.0 8.7 %collective-permute-start.10 = (f32[64,512]{1,0:T(8,128)S(1)}, f32[64,512]{1,0:T(8,128)S(1)}, u32[]{:S(2)}, u32[]{:S(2)}) collective-permute-start(f32[64,512]{1,0:T(8,128)S(1)} %get-tuple-element.56), channel_id=1, source_target_pairs={{0,16},{4,20},{8,24},{12,28},{16,0},{20,4},{24,8},{28,12},{1,17},{... | collective-permute-start | bytes 393224 | tf_op jit(solution)/shard_map/ppermute | solution.py:366
  51.4 4.3 %collective-permute-start.11 = (f32[64,256]{1,0:T(8,128)S(1)}, f32[64,256]{1,0:T(8,128)S(1)}, u32[]{:S(2)}, u32[]{:S(2)}) collective-permute-start(f32[64,256]{1,0:T(8,128)S(1)} %get-tuple-element.60), channel_id=1, source_target_pairs={{0,4},{4,0},{8,12},{12,8},{16,20},{20,16},{24,28},{28,24},{1,5},{5... | collective-permute-start | bytes 196616 | tf_op jit(solution)/shard_map/ppermute | solution.py:366
  51.6 4.3 %collective-permute-start.16 = (f32[32,512]{1,0:T(8,128)S(1)}, f32[32,512]{1,0:T(8,128)S(1)}, u32[]{:S(2)}, u32[]{:S(2)}) collective-permute-start(f32[32,512]{1,0:T(8,128)S(1)} %add.39.refs_6_), channel_id=1, source_target_pairs={{0,8},{4,12},{8,0},{12,4},{16,24},{20,28},{24,16},{28,20},{1,9},{5... | collective-permute-start | bytes 196616 | tf_op jit(solution)/shard_map/ppermute | solution.py:366
